TPU v7x, 256 devices: a whole 4x4x8 slice. The times are simulated.
256 devices in a mesh: section: 4 (over y), dp: 64 (over x, z, core).
Axes of the slice: x: 4, y: 4, z: 8, core: 2. Of those that a mesh axis runs over, the one named last changes fastest.
Arguments:
- hidden: bfloat16 [4, 8192, 8192], P('section', 'dp'), may hold values from -6 to 6
- cotangent: bfloat16 [8192, 8192], P('dp'), may hold values from -6 to 6
- w_value: bfloat16 [4, 8192, 512], P('section', 'dp'), may hold values from -0.0625 to 0.0625
- w_out_t: bfloat16 [4, 8192, 512], P('section', 'dp'), may hold values from -0.0625 to 0.0625
- p_in: bfloat16 [4, 8192, 64], P('section'), may hold values from -0.015625 to 0.015625
- p_value_out: bfloat16 [4, 512, 64], P('section'), may hold values from -0.0625 to 0.0625
- p_value_in: bfloat16 [4, 512, 64], P('section'), may hold values from -0.0625 to 0.0625
- p_out: bfloat16 [4, 8192, 64], P('section'), may hold values from -0.015625 to 0.015625
- segments: int32 [8192], P('dp'), may hold values from 0 to 63, never falling along the last dimension, each value on 1 to 1024 neighbouring positions
- owner_slot: int32 [64], replicated, may hold values from 0 to 63, each once
Outputs:
- doc_grads: float32 [4, 2, 64, 4096], P('section', None, 'dp')
Inputs may be any that keep to these rules, and one draw needn't show every extreme that they name: `segments`: document numbers never fall along the row; each document has 1 to 1024 tokens and one has exactly 1024. `owner_slot`: each slot is taken by exactly one document.
All inputs are finite; a program needn't handle non-finite values.
Results may differ from a plain program's by a relative error of at most 0.008.
Values may be sent and summed in bfloat16 or wider, within the bound.
No kernel may reach another device: no remote copies, remote signals or barrier semaphores. Data moves between devices by JAX's collectives and lax.ppermute only.
A program may use at most 128 MiB of HBM per device.

v0:
```python
import jax
import jax.numpy as jnp
from jax import lax
from jax.sharding import PartitionSpec as P


def from_behind(value, axis, steps):
    count = lax.axis_size(axis)
    leading, last = (max(0, -steps), min(count, count - steps))
    return lax.ppermute(value, axis, [(source, source + steps) for source in range(leading, last)])


def layer_backward(grad, acts, full_value, full_out, proj_in, proj_vout, proj_vin, proj_out):
    upd = jnp.dot(grad, full_out, preferred_element_type=jnp.float32).astype(jnp.bfloat16)
    value = jnp.dot(acts, full_value, preferred_element_type=jnp.float32).astype(jnp.bfloat16)
    first_in = jnp.dot(acts, proj_in, preferred_element_type=jnp.float32).astype(jnp.bfloat16)
    first_out = jnp.dot(upd, proj_vout, preferred_element_type=jnp.float32).astype(jnp.bfloat16)
    second_in = jnp.dot(value, proj_vin, preferred_element_type=jnp.float32).astype(jnp.bfloat16)
    second_out = jnp.dot(grad, proj_out, preferred_element_type=jnp.float32).astype(jnp.bfloat16)
    packed = jnp.concatenate([first_in, first_out, second_in, second_out], axis=1)
    back = lax.dot_general(
        upd, full_value, (((1,), (1,)), ((), ())), preferred_element_type=jnp.float32
    )
    return ((grad.astype(jnp.float32) + back).astype(jnp.bfloat16), packed)


def doc_terms(packed, slots, count):
    rank = packed.shape[1] // 4
    total_rows = packed.shape[0]
    onehot = (slots[:, None] == jnp.arange(count, dtype=jnp.int32)[None, :]).astype(jnp.bfloat16)
    tables = []
    for layer in range(2):
        left = packed[:, 2 * layer * rank : (2 * layer + 1) * rank]
        right = packed[:, (2 * layer + 1) * rank : (2 * layer + 2) * rank]
        spread = (onehot[:, :, None] * left[:, None, :]).reshape(total_rows, count * rank)
        table = lax.dot_general(
            spread, right, (((0,), (0,)), ((), ())), preferred_element_type=jnp.float32
        )
        tables.append(table.reshape(count, rank * rank))
    return jnp.concatenate(tables, axis=1)


def body(
    hidden, cotangent, w_value, w_out_t, p_in, p_value_out, p_value_in, p_out, segments, owner_slot
):
    sections = lax.axis_size("section")
    section_id = lax.axis_index("section")
    full_value, full_out = (
        lax.all_gather(w_value[0], "dp", axis=0, tiled=True),
        lax.all_gather(w_out_t[0], "dp", axis=0, tiled=True),
    )
    acts = hidden[0]
    total_rows = acts.shape[0]
    rank = p_in.shape[2]
    blocks = 4
    block_rows = total_rows // blocks
    packed_all = jnp.zeros((total_rows, 4 * rank), jnp.bfloat16)
    received = jnp.zeros((block_rows, acts.shape[1]), jnp.bfloat16)
    ticks = blocks + sections - 1
    for tick in range(ticks):
        position = tick - (sections - 1 - section_id)
        clipped = jnp.clip(position, 0, blocks - 1)
        valid = jnp.logical_and(position >= 0, position < blocks)
        start = clipped * block_rows
        from_loss = lax.dynamic_slice_in_dim(cotangent, start, block_rows, 0)
        incoming = jnp.where(section_id == sections - 1, from_loss, received)
        local = lax.dynamic_slice_in_dim(acts, start, block_rows, 0)
        back, packed = layer_backward(
            incoming, local, full_value, full_out, p_in[0], p_value_out[0], p_value_in[0], p_out[0]
        )
        updated = lax.dynamic_update_slice_in_dim(packed_all, packed, start, 0)
        packed_all = jnp.where(valid, updated, packed_all)
        if tick < ticks - 1:
            received = from_behind(back, "section", -1)
    documents = owner_slot.shape[0]
    doc_dev = documents // lax.axis_size("dp")
    match = segments[:, None] == jnp.arange(documents, dtype=jnp.int32)[None, :]
    slot_tok = jnp.sum(jnp.where(match, owner_slot[None, :], 0), axis=1)
    result = lax.psum_scatter(
        doc_terms(packed_all, slot_tok, doc_dev * lax.axis_size("dp")),
        "dp",
        scatter_dimension=0,
        tiled=True,
    )
    return result.reshape(doc_dev, 2, rank * rank).transpose(1, 0, 2)[None]


def solution(mesh):
    placed = (
        P("section", "dp", None),
        P("dp", None),
        P("section", "dp", None),
        P("section", "dp", None),
        P("section", None, None),
        P("section", None, None),
        P("section", None, None),
        P("section", None, None),
        P("dp"),
        P(),
    )
    return jax.shard_map(
        body, mesh=mesh, in_specs=placed, out_specs=P("section", None, "dp", None), check_vma=False
    )
```

profile of v0, /device:TPU:32, one launch (start us, length us, event | category | flops | bytes accessed | tf_op | source)
XLA Modules:
  0.0 530.4 jit_solution(9555900662162650012)
XLA Ops:
  8.1 0.8 select_reduce_fusion
  9.0 1.6 convolution_convert_fusion.13
  10.6 1.6 convolution_convert_fusion.11
  12.2 1.6 convolution_convert_fusion.9
  13.9 1.6 convolution_convert_fusion.7
  15.5 1.6 convolution_convert_fusion.5
  18.0 1.4 convolution_convert_fusion.12
  19.4 76.5 %all-gather.5.cloned.1.call-done = bf16[1,8192,512]{2,1,0:T(8,128)(2,1)} async-done(((bf16[1,128,512]{2,1,0:T(8,128)(2,1)}), bf16[1,8192,512]{2,1,0:T(8,128)(2,1)}) %all-gather.5.cloned.1.call-update) | async-done | bytes 8388624 | tf_op jit(solution)/shard_map/all_gather | solution.py:50
  96.0 5.1 fusion.40
  101.2 77.8 %all-gather.7.cloned.1.call-done = bf16[1,8192,512]{2,1,0:T(8,128)(2,1)} async-done(((bf16[1,128,512]{2,1,0:T(8,128)(2,1)}), bf16[1,8192,512]{2,1,0:T(8,128)(2,1)}) %all-gather.7.cloned.1.call-update) | async-done | bytes 8388624 | tf_op jit(solution)/shard_map/all_gather | solution.py:49
  179.0 6.0 %fusion = bf16[32,8192]{1,0:T(8,128)(2,1)S(1)} fusion(bf16[32,512]{1,0:T(8,128)(2,1)S(1)} %fusion.40, bf16[1,8192,512]{2,1,0:T(8,128)(2,1)} %all-gather.7.cloned.1.call-done, bf16[128,8192]{1,0:T(8,128)(2,1)} %param.11, s32[]{:T(128)S(6)} %select_n.143, pred[]{:T(512)S(6)} %eq.45), kind=kOutput, calls=%fused_computation.1 | convolution fusion | flops 269484032 | bytes 9469957 | tf_op jit(solution)/shard_map/dot_general | solution.py:21
  185.0 1.5 collective-permute-start
  186.5 5.0 fusion.109
  191.6 5.0 fusion.112
  196.6 5.0 fusion.115
  201.7 5.0 fusion.118
  206.7 5.0 fusion.121
  211.7 5.0 fusion.124
  216.8 5.0 fusion.127
  221.9 1.5 dynamic-slice_select_fusion.5
  223.4 5.6 %fusion.43 = bf16[32,512]{1,0:T(8,128)(2,1)S(1)} fusion(bf16[32,8192]{1,0:T(8,128)(2,1)S(1)} %dynamic-slice_select_fusion.5, bf16[1,8192,512]{2,1,0:T(8,128)(2,1)} %all-gather.5.cloned.1.call-done), kind=kOutput, calls=%fused_computation.43 | convolution fusion | flops 268451840 | bytes 8945664 | tf_op jit(solution)/shard_map/dot_general | solution.py:14
  229.4 2.5 add_convert_fusion.4
  232.0 1.3 collective-permute-start.1
  233.9 14.7 %collective-permute-done.1 = bf16[32,8192]{1,0:T(8,128)(2,1)S(1)} collective-permute-done((bf16[32,8192]{1,0:T(8,128)(2,1)S(1)}, bf16[32,8192]{1,0:T(8,128)(2,1)S(1)}, u32[]{:S(2)}, u32[]{:S(2)}) %collective-permute-start.1) | collective-permute-done | bytes 524320 | tf_op jit(solution)/shard_map/ppermute | solution.py:10
  248.8 1.5 fusion.46
  250.3 2.6 add_convert_fusion.3
  252.8 1.5 collective-permute-start.2
  255.0 13.0 %collective-permute-done.2 = bf16[32,8192]{1,0:T(8,128)(2,1)S(1)} collective-permute-done((bf16[32,8192]{1,0:T(8,128)(2,1)S(1)}, bf16[32,8192]{1,0:T(8,128)(2,1)S(1)}, u32[]{:S(2)}, u32[]{:S(2)}) %collective-permute-start.2) | collective-permute-done | bytes 524320 | tf_op jit(solution)/shard_map/ppermute | solution.py:10
  268.1 1.5 fusion.49
  269.6 2.6 add_convert_fusion.2
  272.2 1.3 collective-permute-start.3
  274.1 12.3 %collective-permute-done.3 = bf16[32,8192]{1,0:T(8,128)(2,1)S(1)} collective-permute-done((bf16[32,8192]{1,0:T(8,128)(2,1)S(1)}, bf16[32,8192]{1,0:T(8,128)(2,1)S(1)}, u32[]{:S(2)}, u32[]{:S(2)}) %collective-permute-start.3) | collective-permute-done | bytes 524320 | tf_op jit(solution)/shard_map/ppermute | solution.py:10
  286.6 1.5 fusion.52
  288.1 2.6 add_convert_fusion.1
  290.7 1.3 collective-permute-start.4
  292.6 11.4 %collective-permute-done.4 = bf16[32,8192]{1,0:T(8,128)(2,1)S(1)} collective-permute-done((bf16[32,8192]{1,0:T(8,128)(2,1)S(1)}, bf16[32,8192]{1,0:T(8,128)(2,1)S(1)}, u32[]{:S(2)}, u32[]{:S(2)}) %collective-permute-start.4) | collective-permute-done | bytes 524320 | tf_op jit(solution)/shard_map/ppermute | solution.py:10
  304.1 1.5 fusion.55
  305.6 2.6 add_convert_fusion
  308.2 1.3 collective-permute-start.5
  310.1 10.4 %collective-permute-done.5 = bf16[32,8192]{1,0:T(8,128)(2,1)S(1)} collective-permute-done((bf16[32,8192]{1,0:T(8,128)(2,1)S(1)}, bf16[32,8192]{1,0:T(8,128)(2,1)S(1)}, u32[]{:S(2)}, u32[]{:S(2)}) %collective-permute-start.5) | collective-permute-done | bytes 524320 | tf_op jit(solution)/shard_map/ppermute | solution.py:10
  321.0 5.1 fusion.106
  326.5 1.8 fusion.202
  328.3 2.9 reshape.48
  331.3 1.8 fusion.204
  333.1 2.1 reshape.47
  335.2 2.7 pad_maximum_fusion
  338.6 183.0 %all-reduce.3.cloned.1.call-done = f32[64,8192]{1,0:T(8,128)} async-done(((f32[64,8192]{1,0:T(8,128)}), f32[64,8192]{1,0:T(8,128)}) %all-reduce.3.cloned.1.call-update) | async-done | bytes 2097168
  521.6 2.2 constant_dynamic-slice_fusion
  (65 shorter events, 8.3 us)
Async XLA Ops:
  6.5 2.4 copy-start
  6.5 10.6 %copy-start.1 = (bf16[1,8192,64]{1,2,0:T(8,128)(2,1)S(1)}, bf16[1,8192,64]{1,2,0:T(8,128)(2,1)}, u32[]{:S(2)}) copy-start(bf16[1,8192,64]{1,2,0:T(8,128)(2,1)} %param.14) | copy-start | bytes 3145732
  6.5 89.4 %all-gather.5.cloned.1.call-start = ((), (), s32[]{:S(2)}) async-start(), calls=%async_computation | async-start | bytes 8519680 | tf_op jit(solution)/shard_map/all_gather | solution.py:50
  7.3 171.8 %all-gather.7.cloned.1.call-start = ((), (), s32[]{:S(2)}) async-start(), calls=%async_computation.1 | async-start | bytes 8519680 | tf_op jit(solution)/shard_map/all_gather | solution.py:49
  8.0 513.6 %all-reduce.3.cloned.1.call-start = ((), (), s32[]{:S(2)}) async-start(), calls=%async_computation.2 | async-start | bytes 4194304
  8.1 9.9 %copy-start.2 = (bf16[1,8192,64]{1,2,0:T(8,128)(2,1)S(1)}, bf16[1,8192,64]{1,2,0:T(8,128)(2,1)}, u32[]{:S(2)}) copy-start(bf16[1,8192,64]{1,2,0:T(8,128)(2,1)} %param.17) | copy-start | bytes 3145732
  19.4 81.6 %copy-start.6 = (bf16[1,512,64]{1,2,0:T(8,128)(2,1)S(1)}, bf16[1,512,64]{1,2,0:T(8,128)(2,1)}, u32[]{:S(2)}) copy-start(bf16[1,512,64]{1,2,0:T(8,128)(2,1)} %param.15) | copy-start | bytes 196612
  101.1 85.4 %copy-start.5 = (bf16[1,512,64]{1,2,0:T(8,128)(2,1)S(1)}, bf16[1,512,64]{1,2,0:T(8,128)(2,1)}, u32[]{:S(2)}) copy-start(bf16[1,512,64]{1,2,0:T(8,128)(2,1)} %param.16) | copy-start | bytes 196612
  185.0 36.8 %collective-permute-start = (bf16[32,8192]{1,0:T(8,128)(2,1)S(1)}, bf16[32,8192]{1,0:T(8,128)(2,1)}, u32[]{:S(2)}, u32[]{:S(2)}) collective-permute-start(bf16[32,8192]{1,0:T(8,128)(2,1)S(1)} %fusion), channel_id=1, source_target_pairs={{64,0},{128,64},{192,128},{65,1},{129,65},{193,129},{66,2},{130,66... | collective-permute-start | bytes 1572872 | tf_op jit(solution)/shard_map/ppermute | solution.py:10
  221.8 7.1 %slice-start = ((s8[8388608]{0:T(1024)(128)(4,1)}), s8[4194304]{0:T(1024)(128)(4,1)S(1)}, s32[]{:S(2)}) async-start(s8[8388608]{0:T(1024)(128)(4,1)} %bitcast.242), calls=%async_computation.3 | async-start | bytes 8388608
  221.9 26.9 %slice-start.2 = ((s8[8388608]{0:T(1024)(128)(4,1)}), s8[4194304]{0:T(1024)(128)(4,1)S(1)}, s32[]{:S(2)}) async-start(s8[8388608]{0:T(1024)(128)(4,1)} %bitcast.244), calls=%async_computation.5 | async-start | bytes 8388608
  223.4 6.1 %slice-start.1 = ((s8[8388608]{0:T(1024)(128)(4,1)}), s8[4194304]{0:T(1024)(128)(4,1)S(1)}, s32[]{:S(2)}) async-start(s8[8388608]{0:T(1024)(128)(4,1)} %bitcast.242), calls=%async_computation.4 | async-start | bytes 8388608
  223.4 25.4 %slice-start.3 = ((s8[8388608]{0:T(1024)(128)(4,1)}), s8[4194304]{0:T(1024)(128)(4,1)S(1)}, s32[]{:S(2)}) async-start(s8[8388608]{0:T(1024)(128)(4,1)} %bitcast.244), calls=%async_computation.6 | async-start | bytes 8388608
  229.4 4.0 copy-start.3
  229.4 19.2 %copy-start.4 = (bf16[128,8192]{1,0:T(8,128)(2,1)S(1)}, bf16[128,8192]{1,0:T(8,128)(2,1)}, u32[]{:S(2)}) copy-start(bf16[128,8192]{1,0:T(8,128)(2,1)} %param.11) | copy-start | bytes 6291460
  232.0 16.6 %collective-permute-start.1 = (bf16[32,8192]{1,0:T(8,128)(2,1)S(1)}, bf16[32,8192]{1,0:T(8,128)(2,1)S(1)}, u32[]{:S(2)}, u32[]{:S(2)}) collective-permute-start(bf16[32,8192]{1,0:T(8,128)(2,1)S(1)} %add_convert_fusion.4), channel_id=1, source_target_pairs={{64,0},{128,64},{192,128},{65,1},{129,65},{193,129},{66,2},{130,66... | collective-permute-start | bytes 1572872 | tf_op jit(solution)/shard_map/ppermute | solution.py:10
  252.8 15.2 %collective-permute-start.2 = (bf16[32,8192]{1,0:T(8,128)(2,1)S(1)}, bf16[32,8192]{1,0:T(8,128)(2,1)S(1)}, u32[]{:S(2)}, u32[]{:S(2)}) collective-permute-start(bf16[32,8192]{1,0:T(8,128)(2,1)S(1)} %add_convert_fusion.3), channel_id=1, source_target_pairs={{64,0},{128,64},{192,128},{65,1},{129,65},{193,129},{66,2},{130,66... | collective-permute-start | bytes 1572872 | tf_op jit(solution)/shard_map/ppermute | solution.py:10
  272.2 14.2 %collective-permute-start.3 = (bf16[32,8192]{1,0:T(8,128)(2,1)S(1)}, bf16[32,8192]{1,0:T(8,128)(2,1)S(1)}, u32[]{:S(2)}, u32[]{:S(2)}) collective-permute-start(bf16[32,8192]{1,0:T(8,128)(2,1)S(1)} %add_convert_fusion.2), channel_id=1, source_target_pairs={{64,0},{128,64},{192,128},{65,1},{129,65},{193,129},{66,2},{130,66... | collective-permute-start | bytes 1572872 | tf_op jit(solution)/shard_map/ppermute | solution.py:10
  290.7 13.3 %collective-permute-start.4 = (bf16[32,8192]{1,0:T(8,128)(2,1)S(1)}, bf16[32,8192]{1,0:T(8,128)(2,1)S(1)}, u32[]{:S(2)}, u32[]{:S(2)}) collective-permute-start(bf16[32,8192]{1,0:T(8,128)(2,1)S(1)} %add_convert_fusion.1), channel_id=1, source_target_pairs={{64,0},{128,64},{192,128},{65,1},{129,65},{193,129},{66,2},{130,66... | collective-permute-start | bytes 1572872 | tf_op jit(solution)/shard_map/ppermute | solution.py:10
  308.2 12.4 %collective-permute-start.5 = (bf16[32,8192]{1,0:T(8,128)(2,1)S(1)}, bf16[32,8192]{1,0:T(8,128)(2,1)S(1)}, u32[]{:S(2)}, u32[]{:S(2)}) collective-permute-start(bf16[32,8192]{1,0:T(8,128)(2,1)S(1)} %add_convert_fusion), channel_id=1, source_target_pairs={{64,0},{128,64},{192,128},{65,1},{129,65},{193,129},{66,2},{130,66... | collective-permute-start | bytes 1572872 | tf_op jit(solution)/shard_map/ppermute | solution.py:10
  328.3 9.6 %copy-start.7 = (u32[256]{0:T(256)S(1)}, u32[256]{0:T(256)}, u32[]{:S(2)}) copy-start(u32[256]{0:T(256)} %constant.43) | copy-start | bytes 3076
Sparse Core Ops, SparseCore 0:
  10.1 85.7 all-gather.4
  98.7 80.2 all-gather.6
  338.1 183.4 all-reduce.2
where the time goes:
time: 534 us; the launch traced here: 530 us
  waiting for transfers between devices  401 us (75%)
  matrix products  93 us (17%)
  between operations  13.5 us (3%)
  local copies, waits for them, and re-layouts  8.68 us (2%)
  starting transfers between devices  8.23 us (2%)
  other arithmetic  6.38 us (1%)
    unnamed x4, waiting for transfers between devices  184 us
    all_gather x1, waiting for transfers between devices, body(): lax.all_gather(w_value[0], 'dp', axis=0, tiled=True)  77.8 us
    all_gather x1, waiting for transfers between devices, body(): lax.all_gather(w_out_t[0], 'dp', axis=0, tiled=True)  76.5 us
    ppermute x6, waiting for transfers between devices, from_behind(): lax.ppermute(value, axis, [(source, source + steps) for source in range(l...  61.8 us
    dot_general x7, matrix products, layer_backward(): jnp.dot(value, proj_vin, preferred_element_type=jnp.float32)  35.2 us
    dot_general x6, matrix products, layer_backward(): lax.dot_general(upd, full_value, (((1,), (1,)), ((), ())), preferred_elem...  18.7 us
    dot_general x6, matrix products, layer_backward(): jnp.dot(grad, full_out, preferred_element_type=jnp.float32)  16.8 us
  transfers between devices with their start and end apart: 9, of which 8 were waited for; matrix products, arithmetic and copies ran while one was open for 10% of the time, Pallas kernels for 0%

commit v1 on v0

v1 whole, which is shorter than its diff:
```python
import jax
import jax.numpy as jnp
from jax import lax
from jax.sharding import Mesh, PartitionSpec as P

XZ = ("x", "z")
DP = ("x", "z", "c")
SWAP = [(0, 1), (1, 0)]
BF16 = jnp.bfloat16
F32 = jnp.float32


def dot(left, right, left_dim=1):
    return lax.dot_general(
        left, right, (((left_dim,), (0,)), ((), ())), preferred_element_type=F32
    )


def from_above(value, steps):
    count = lax.axis_size("y")
    return lax.ppermute(value, "y", [(i, i - steps) for i in range(steps, count)])


def halves(mine, core, axis):
    got = lax.ppermute(mine, "c", SWAP)
    first = jnp.where(core == 0, mine, got)
    second = jnp.where(core == 0, got, mine)
    return jnp.concatenate([first, second], axis=axis)


def grams(wv, right, core):
    width = wv.shape[1] // 2
    mine = lax.dynamic_slice_in_dim(wv, core * width, width, 1)
    other = lax.dynamic_slice_in_dim(wv, (1 - core) * width, width, 1)
    left = jnp.concatenate([mine, lax.ppermute(other, "c", SWAP)], axis=0)
    rows = jnp.concatenate([right, lax.ppermute(right, "c", SWAP)], axis=0)
    parts = [dot(from_above(left, k), rows, 0).astype(BF16) for k in (1, 2, 3)]
    ranks = lax.axis_size(XZ)
    own = jnp.concatenate(parts, axis=0).reshape(ranks, -1, right.shape[1])
    slices = lax.all_to_all(own, XZ, 0, 0)
    total = jnp.sum(slices.astype(F32), axis=0).astype(BF16)
    every = lax.all_to_all(jnp.broadcast_to(total[None], own.shape), XZ, 0, 0)
    return every.reshape(3, width, right.shape[1])


def solve(half, pv_out, core, kv):
    above_one = from_above(half[:2, :, :kv], 1)
    above_two = from_above(half[:1, :, :kv], 2)
    own = halves(half, core, 1)
    g_one = halves(above_one, core, 1)
    g_two = halves(above_two, core, 1)
    first = [
        jnp.concatenate([dot(own[k, :, :kv], pv_out), own[k, :, kv:].astype(F32)], axis=1)
        for k in range(3)
    ]
    e_one = first[0].astype(BF16)
    e_two = (first[1] + dot(g_one[0], e_one)).astype(BF16)
    e_three = (first[2] + dot(g_one[1], e_one) + dot(g_two[0], e_two)).astype(BF16)
    return jnp.concatenate([e_one, e_two, e_three], axis=0)


def doc_sums(left, right, slots, core, rank):
    owners = lax.axis_size(XZ)
    named = 2 * jnp.arange(owners, dtype=jnp.int32) + core
    onehot = (slots[:, None] == named[None, :]).astype(BF16)
    spread = (onehot[:, :, None] * left[:, None, :]).reshape(left.shape[0], owners * 2 * rank)
    table = dot(spread, right, 0).reshape(owners, 2 * rank, 2 * rank)
    lane = lax.broadcasted_iota(jnp.int32, (1, rank, 2 * rank), 2)
    return jnp.where(lane < rank, table[:, :rank], table[:, rank:]).astype(BF16)


def body(
    hidden, cotangent, w_value, w_out_t, p_in, p_value_out, p_value_in, p_out, segments, owner_slot
):
    core = lax.axis_index("c")
    device = lax.axis_index(DP)
    wv, wo, acts = w_value[0], w_out_t[0], hidden[0]
    rows, kv = wv.shape
    rank = p_in.shape[2]
    documents = owner_slot.shape[0]

    mixed = jnp.concatenate([wo, dot(wv, p_value_in[0]).astype(BF16)], axis=1)
    full = lax.all_gather(mixed, DP, axis=0, tiled=True)

    out_rows = lax.dynamic_slice_in_dim(p_out[0], device * rows, rows, 0)
    half = grams(wv, jnp.concatenate([wo, out_rows], axis=1), core)
    spread_e = solve(half, p_value_out[0], core, kv)

    match = segments[:, None] == jnp.arange(documents, dtype=jnp.int32)[None, :]
    slots = jnp.sum(jnp.where(match, owner_slot[None, :], 0), axis=1)
    slots = jnp.concatenate([slots, lax.ppermute(slots, "c", SWAP)])
    first_in = dot(acts, p_in[0])
    direct_out = dot(cotangent, p_out[0])
    tokens = cotangent.shape[0]
    both = jnp.concatenate([cotangent, acts], axis=0)

    product = dot(both, full).astype(BF16)
    upd = product[:tokens, :kv]
    above = jnp.concatenate([from_above(upd, k) for k in (1, 2, 3)], axis=1)
    direct = jnp.concatenate([dot(upd, p_value_out[0]), direct_out], axis=1)
    right = (direct + dot(above, spread_e)).astype(BF16)
    left = jnp.concatenate([first_in.astype(BF16), product[tokens:, kv:]], axis=1)
    packed = jnp.concatenate([left, right], axis=1)
    packed = jnp.concatenate([packed, lax.ppermute(packed, "c", SWAP)], axis=0)
    sums = doc_sums(packed[:, : 2 * rank], packed[:, 2 * rank :], slots, core, rank)
    parts = lax.all_to_all(sums, XZ, 0, 0)
    total = jnp.sum(parts.astype(F32), axis=0)
    tables = total.reshape(rank, 2, rank).transpose(1, 0, 2)
    return tables.reshape(1, 2, 1, rank * rank)


def solution(mesh):
    grid = Mesh(mesh.devices.reshape(4, 4, 8, 2), ("y", "x", "z", "c"))
    placed = (
        P("y", DP, None),
        P(DP, None),
        P("y", DP, None),
        P("y", DP, None),
        P("y", None, None),
        P("y", None, None),
        P("y", None, None),
        P("y", None, None),
        P(DP),
        P(),
    )
    return jax.shard_map(
        body, mesh=grid, in_specs=placed, out_specs=P("y", None, DP, None), check_vma=False
    )
```

time: 534 us -> 196 us (0.37)
  waiting for transfers between devices: 401 us -> 71.8 us
  matrix products: 93 us -> 20.1 us
  blocking collectives: 0 us -> 63.3 us
  starting transfers between devices: 8.23 us -> 16.9 us
    unnamed x4 -> x1, waiting for transfers between devices: 184 us -> 0.02 us
    all_gather x2 -> x1, waiting for transfers between devices: 154 us -> 0.01 us  [body(): full = lax.all_gather(mixed, DP, axis=0, tiled=True)]
    dot_general x42 -> x16, matrix products: 93 us -> 20.1 us  [dot(): lax.dot_general(left, right, (((left_dim,), (0,)), ((), ())), preferred_e...]
    all_to_all x0 -> x2, blocking collectives: none -> 63.3 us  [the longest x1 39.8 us: grams(): slices = lax.all_to_all(own, XZ, 0, 0)]
    all_to_all x0 -> x1, waiting for transfers between devices: none -> 34.6 us  [grams(): every = lax.all_to_all(jnp.broadcast_to(total[None], own.shape), XZ, 0, 0)]
    ppermute x6 -> x15, waiting for transfers between devices: 61.8 us -> 37.2 us  [the longest x8 34 us: from_above(): lax.ppermute(value, 'y', [(i, i - steps) for i in range(steps, count)])]
    all_to_all x0 -> x1, starting transfers between devices: none -> 5.67 us  [grams(): every = lax.all_to_all(jnp.broadcast_to(total[None], own.shape), XZ, 0, 0)]
    ppermute x6 -> x15, starting transfers between devices: 8.15 us -> 11.2 us  [the longest x8 10.3 us: from_above(): lax.ppermute(value, 'y', [(i, i - steps) for i in range(steps, count)])]
  transfers between devices with their start and end apart: 9 -> 17, of which waited for: 8 -> 11; matrix products, arithmetic and copies ran while one was open for 10% -> 8% of each run, Pallas kernels for 0% -> 0%
where the time goes in v1:
time: 196 us
  waiting for transfers between devices  71.8 us (37%)
  blocking collectives  63.3 us (32%)
  matrix products  20.1 us (10%)
  starting transfers between devices  16.9 us (9%)
  between operations  13.8 us (7%)
  local copies, waits for them, and re-layouts  6.38 us (3%)
  other arithmetic  3.48 us (2%)
    all_to_all x1, blocking collectives, grams(): slices = lax.all_to_all(own, XZ, 0, 0)  39.8 us
    all_to_all x1, waiting for transfers between devices, grams(): every = lax.all_to_all(jnp.broadcast_to(total[None], own.shape), XZ, 0, 0)  34.6 us
    ppermute x8, waiting for transfers between devices, from_above(): lax.ppermute(value, 'y', [(i, i - steps) for i in range(steps, count)])  34 us
    all_to_all x1, blocking collectives, body(): parts = lax.all_to_all(sums, XZ, 0, 0)  23.5 us
    dot_general x16, matrix products, dot(): lax.dot_general(left, right, (((left_dim,), (0,)), ((), ())), preferred_e...  20.1 us
    ppermute x8, starting transfers between devices, from_above(): lax.ppermute(value, 'y', [(i, i - steps) for i in range(steps, count)])  10.3 us
    all_to_all x1, starting transfers between devices, grams(): every = lax.all_to_all(jnp.broadcast_to(total[None], own.shape), XZ, 0, 0)  5.67 us
  transfers between devices with their start and end apart: 17, of which 11 were waited for; matrix products, arithmetic and copies ran while one was open for 8% of the time, Pallas kernels for 0%

profile of v1, /device:TPU:32, one launch (start us, length us, event | category | flops | bytes accessed | tf_op | source)
XLA Modules:
  0.0 195.8 jit_solution(2493847151487835631)
XLA Ops:
  6.5 1.2 copy-done
  7.9 1.1 convolution_convert_fusion.4
  9.1 1.6 pad_maximum_fusion.3
  10.7 0.9 dynamic-slice_bitcast_fusion.1
  11.7 0.5 collective-permute-start.6
  12.2 0.7 collective-permute-done.4
  13.0 1.3 collective-permute-start.7
  14.3 1.3 collective-permute-start.5
  15.6 1.3 collective-permute-start.8
  16.9 5.0 %collective-permute-done.7 = bf16[256,256]{1,0:T(8,128)(2,1)S(1)} collective-permute-done((bf16[256,256]{1,0:T(8,128)(2,1)S(1)}, bf16[256,256]{1,0:T(8,128)(2,1)S(1)}, u32[]{:S(2)}, u32[]{:S(2)}) %collective-permute-start.7) | collective-permute-done | bytes 131104 | tf_op jit(solution)/shard_map/ppermute | solution.py:21
  21.9 1.2 convolution_convert_fusion.1
  23.2 0.3 convolution_convert_fusion.2
  23.5 2.0 %collective-permute-done.8 = bf16[256,256]{1,0:T(8,128)(2,1)S(1)} collective-permute-done((bf16[256,256]{1,0:T(8,128)(2,1)S(1)}, bf16[256,256]{1,0:T(8,128)(2,1)S(1)}, u32[]{:S(2)}, u32[]{:S(2)}) %collective-permute-start.8) | collective-permute-done | bytes 131104 | tf_op jit(solution)/shard_map/ppermute | solution.py:21
  25.4 0.3 convolution_convert_fusion
  25.8 0.6 copy.34
  26.4 39.8 %all_to_all.15 = bf16[32,24,576]{2,1,0:T(8,128)(2,1)S(1)} all-to-all(bf16[32,24,576]{2,1,0:T(8,128)(2,1)S(1)} %bitcast.81), channel_id=1, replica_groups=mesh['y'=4,'x'=4,'z'=8,'c'=2] {'x','z'}, dimensions={0} | all-to-all | bytes 1769472 | tf_op jit(solution)/shard_map/all_to_all | solution.py:40
  66.3 0.2 reduce_sum.31
  66.5 1.0 broadcast_in_dim.36
  67.5 5.7 %all-to-all-start.1 = ((bf16[32,24,576]{2,1,0:T(8,128)(2,1)}), bf16[32,24,576]{2,1,0:T(8,128)(2,1)S(1)}, u32[]{:S(2)}, u32[]{:S(2)}) async-start(bf16[32,24,576]{2,1,0:T(8,128)(2,1)} %broadcast_in_dim.36), calls=%async_computation.1 | async-start | bytes 1966080 | tf_op jit(solution)/shard_map/all_to_all | solution.py:42
  73.4 2.4 %fusion.14 = f32[128,64]{0,1:T(8,128)S(1)} fusion(bf16[128,8192]{1,0:T(8,128)(2,1)} %param.11, bf16[1,8192,64]{1,2,0:T(8,128)(2,1)S(1)} %copy-done), kind=kOutput, calls=%fused_computation.35 | convolution fusion | flops 134217728 | bytes 3178496 | tf_op jit(solution)/shard_map/dot_general | solution.py:14
  75.8 34.6 %all-to-all-done.1 = bf16[32,24,576]{2,1,0:T(8,128)(2,1)S(1)} async-done(((bf16[32,24,576]{2,1,0:T(8,128)(2,1)}), bf16[32,24,576]{2,1,0:T(8,128)(2,1)S(1)}, u32[]{:S(2)}, u32[]{:S(2)}) %all-to-all-start.1) | async-done | bytes 884768 | tf_op jit(solution)/shard_map/all_to_all | solution.py:42
  110.4 0.6 copy.36
  111.1 0.8 slice.74
  112.1 1.3 collective-permute-start.10
  113.4 1.3 collective-permute-start.12
  114.7 2.8 %convolution_convert_fusion.5 = bf16[128,64]{0,1:T(8,128)(2,1)S(1)} fusion(bf16[1,8192,64]{1,2,0:T(8,128)(2,1)} %param.14, bf16[1,128,8192]{2,1,0:T(8,128)(2,1)} %param.10), kind=kOutput, calls=%fused_computation.30 | convolution fusion | flops 134225920 | bytes 3162112 | tf_op jit(solution)/shard_map/dot_general | solution.py:14
  117.4 9.1 %collective-permute-done.12 = bf16[1,256,512]{2,1,0:T(8,128)(2,1)S(1)} collective-permute-done((bf16[1,256,512]{2,1,0:T(8,128)(2,1)S(1)}, bf16[1,256,512]{2,1,0:T(8,128)(2,1)S(1)}, u32[]{:S(2)}, u32[]{:S(2)}) %collective-permute-start.12) | collective-permute-done | bytes 262176 | tf_op jit(solution)/shard_map/ppermute | solution.py:21
  126.6 2.8 %collective-permute-done.10 = bf16[2,256,512]{2,1,0:T(8,128)(2,1)} collective-permute-done((bf16[2,256,512]{2,1,0:T(8,128)(2,1)}, bf16[2,256,512]{2,1,0:T(8,128)(2,1)}, u32[]{:S(2)}, u32[]{:S(2)}) %collective-permute-start.10) | collective-permute-done | bytes 524320 | tf_op jit(solution)/shard_map/ppermute | solution.py:21
  129.6 0.2 convolution_convert_fusion.3
  129.8 0.2 fusion.34
  130.0 0.2 fusion.36
  130.2 1.3 collective-permute-done.11
  131.5 1.1 broadcast_select_fusion.3
  132.6 0.3 fusion.10
  132.9 0.3 convolution_add_fusion.1
  133.3 1.0 fusion.11
  134.2 8.7 %fusion.7 = bf16[256,576]{0,1:T(8,128)(2,1)S(1)} fusion(bf16[8192,576]{1,0:T(8,128)(2,1)} %all-gather.2.cloned.1.call-done, bf16[128,8192]{1,0:T(8,128)(2,1)S(1)} %bitcast.82, bf16[128,8192]{1,0:T(8,128)(2,1)} %param.11), kind=kOutput, calls=%fused_computation.17 | convolution fusion | flops 2424455168 | bytes 13926400 | tf_op jit(solution)/shard_map/dot_general | solution.py:14
  143.0 1.3 collective-permute-start.1
  144.3 1.3 collective-permute-start.2
  145.6 1.3 collective-permute-start.3
  147.1 9.2 %collective-permute-done.1 = bf16[128,512]{0,1:T(8,128)(2,1)S(1)} collective-permute-done((bf16[128,512]{0,1:T(8,128)(2,1)S(1)}, bf16[128,512]{0,1:T(8,128)(2,1)S(1)}, u32[]{:S(2)}, u32[]{:S(2)}) %collective-permute-start.1) | collective-permute-done | bytes 131104 | tf_op jit(solution)/shard_map/ppermute | solution.py:21
  156.3 3.1 %collective-permute-done.2 = bf16[128,512]{0,1:T(8,128)(2,1)S(1)} collective-permute-done((bf16[128,512]{0,1:T(8,128)(2,1)S(1)}, bf16[128,512]{0,1:T(8,128)(2,1)S(1)}, u32[]{:S(2)}, u32[]{:S(2)}) %collective-permute-start.2) | collective-permute-done | bytes 131104 | tf_op jit(solution)/shard_map/ppermute | solution.py:21
  159.4 2.8 %collective-permute-done.3 = bf16[128,512]{0,1:T(8,128)(2,1)S(1)} collective-permute-done((bf16[128,512]{0,1:T(8,128)(2,1)S(1)}, bf16[128,512]{0,1:T(8,128)(2,1)S(1)}, u32[]{:S(2)}, u32[]{:S(2)}) %collective-permute-start.3) | collective-permute-done | bytes 131104 | tf_op jit(solution)/shard_map/ppermute | solution.py:21
  162.2 0.3 fusion.12
  162.6 1.2 collective-permute-done.14
  163.8 0.7 fusion.4
  164.6 23.5 %all_to_all.16 = bf16[32,64,128]{2,1,0:T(8,128)(2,1)S(1)} all-to-all(bf16[32,64,128]{2,1,0:T(8,128)(2,1)S(1)} %fusion.13), channel_id=1, replica_groups=mesh['y'=4,'x'=4,'z'=8,'c'=2] {'x','z'}, dimensions={0} | all-to-all | bytes 1048576 | tf_op jit(solution)/shard_map/all_to_all | solution.py:106
  188.2 0.7 reshape.72
  (51 shorter events, 1.6 us)
Async XLA Ops:
  6.5 1.2 copy-start
  6.5 16.6 %copy-start.3 = (bf16[1,128,512]{2,1,0:T(8,128)(2,1)S(1)}, bf16[1,128,512]{2,1,0:T(8,128)(2,1)}, u32[]{:S(2)}) copy-start(bf16[1,128,512]{2,1,0:T(8,128)(2,1)} %param.13) | copy-start | bytes 393220
  6.5 127.7 %all-gather.2.cloned.1.call-start = ((), (), s32[]{:S(2)}) async-start(), calls=%async_computation.3 | async-start | bytes 10649600 | tf_op jit(solution)/shard_map/all_gather | solution.py:83
  11.6 1.3 collective-permute-start.4
  11.7 5.2 %collective-permute-start.6 = (bf16[128,576]{1,0:T(8,128)(2,1)S(1)}, bf16[128,576]{1,0:T(8,128)(2,1)S(1)}, u32[]{:S(2)}, u32[]{:S(2)}) collective-permute-start(bf16[128,576]{1,0:T(8,128)(2,1)S(1)} %get-tuple-element.15), channel_id=1, source_target_pairs={{0,1},{1,0},{2,3},{3,2},{4,5},{5,4},{6,7},{7,6},{8,9},{9,8},{10,11... | collective-permute-start | bytes 442376 | tf_op jit(solution)/shard_map/ppermute | solution.py:36
  13.0 9.0 %collective-permute-start.7 = (bf16[256,256]{1,0:T(8,128)(2,1)S(1)}, bf16[256,256]{1,0:T(8,128)(2,1)S(1)}, u32[]{:S(2)}, u32[]{:S(2)}) collective-permute-start(bf16[256,256]{1,0:T(8,128)(2,1)S(1)} %pad_maximum_fusion.5), channel_id=1, source_target_pairs={{128,0},{192,64},{129,1},{193,65},{130,2},{194,66},{131,3},{195,67... | collective-permute-start | bytes 393224 | tf_op jit(solution)/shard_map/ppermute | solution.py:21
  14.3 8.9 %collective-permute-start.5 = (bf16[256,256]{1,0:T(8,128)(2,1)S(1)}, bf16[256,256]{1,0:T(8,128)(2,1)S(1)}, u32[]{:S(2)}, u32[]{:S(2)}) collective-permute-start(bf16[256,256]{1,0:T(8,128)(2,1)S(1)} %pad_maximum_fusion.5), channel_id=1, source_target_pairs={{64,0},{128,64},{192,128},{65,1},{129,65},{193,129},{66,2},{130,66... | collective-permute-start | bytes 393224 | tf_op jit(solution)/shard_map/ppermute | solution.py:21
  15.6 9.9 %collective-permute-start.8 = (bf16[256,256]{1,0:T(8,128)(2,1)S(1)}, bf16[256,256]{1,0:T(8,128)(2,1)S(1)}, u32[]{:S(2)}, u32[]{:S(2)}) collective-permute-start(bf16[256,256]{1,0:T(8,128)(2,1)S(1)} %pad_maximum_fusion.5), channel_id=1, source_target_pairs={{192,0},{193,1},{194,2},{195,3},{196,4},{197,5},{198,6},{199,7},{2... | collective-permute-start | bytes 393224 | tf_op jit(solution)/shard_map/ppermute | solution.py:21
  66.3 6.9 %copy-start.4 = (s32[64]{0:T(128)S(1)}, s32[64]{0:T(128)}, u32[]{:S(2)}) copy-start(s32[64]{0:T(128)} %param.19) | copy-start | bytes 772
  66.3 6.9 %copy-start.5 = (s32[128]{0:T(128)S(1)}, s32[128]{0:T(128)}, u32[]{:S(2)}) copy-start(s32[128]{0:T(128)} %param.18) | copy-start | bytes 1540
  67.5 43.0 %all-to-all-start.1 = ((bf16[32,24,576]{2,1,0:T(8,128)(2,1)}), bf16[32,24,576]{2,1,0:T(8,128)(2,1)S(1)}, u32[]{:S(2)}, u32[]{:S(2)}) async-start(bf16[32,24,576]{2,1,0:T(8,128)(2,1)} %broadcast_in_dim.36), calls=%async_computation.1 | async-start | bytes 1966080 | tf_op jit(solution)/shard_map/all_to_all | solution.py:42
  73.3 53.3 %collective-permute-start = (s32[128]{0:T(128)S(1)}, s32[128]{0:T(128)S(1)}, u32[]{:S(2)}, u32[]{:S(2)}) collective-permute-start(s32[128]{0:T(128)S(1)} %select_reduce_fusion), channel_id=1, source_target_pairs={{0,1},{1,0},{2,3},{3,2},{4,5},{5,4},{6,7},{7,6},{8,9},{9,8},{10,11... | collective-permute-start | bytes 1544 | tf_op jit(solution)/shard_map/ppermute | solution.py:91
  112.0 17.5 %collective-permute-start.9 = (bf16[3,256,576]{1,2,0:T(8,128)(2,1)S(1)}, bf16[3,256,576]{1,2,0:T(8,128)(2,1)S(1)}, u32[]{:S(2)}, u32[]{:S(2)}) collective-permute-start(bf16[3,256,576]{1,2,0:T(8,128)(2,1)S(1)} %copy.36), channel_id=1, source_target_pairs={{0,1},{1,0},{2,3},{3,2},{4,5},{5,4},{6,7},{7,6},{8,9},{9,8},{10,11... | collective-permute-start | bytes 2654216 | tf_op jit(solution)/shard_map/ppermute | solution.py:25
  112.1 17.3 %collective-permute-start.10 = (bf16[2,256,512]{2,1,0:T(8,128)(2,1)}, bf16[2,256,512]{2,1,0:T(8,128)(2,1)}, u32[]{:S(2)}, u32[]{:S(2)}) collective-permute-start(bf16[2,256,512]{2,1,0:T(8,128)(2,1)} %slice.74), channel_id=1, source_target_pairs={{64,0},{128,64},{192,128},{65,1},{129,65},{193,129},{66,2},{130,66... | collective-permute-start | bytes 1572872 | tf_op jit(solution)/shard_map/ppermute | solution.py:21
  113.4 13.2 %collective-permute-start.12 = (bf16[1,256,512]{2,1,0:T(8,128)(2,1)S(1)}, bf16[1,256,512]{2,1,0:T(8,128)(2,1)S(1)}, u32[]{:S(2)}, u32[]{:S(2)}) collective-permute-start(bf16[1,256,512]{2,1,0:T(8,128)(2,1)S(1)} %slice.79), channel_id=1, source_target_pairs={{128,0},{192,64},{129,1},{193,65},{130,2},{194,66},{131,3},{195,67... | collective-permute-start | bytes 786440 | tf_op jit(solution)/shard_map/ppermute | solution.py:21
  126.5 2.9 %collective-permute-start.13 = (bf16[1,256,512]{2,1,0:T(8,128)(2,1)S(1)}, bf16[1,256,512]{2,1,0:T(8,128)(2,1)S(1)}, u32[]{:S(2)}, u32[]{:S(2)}) collective-permute-start(bf16[1,256,512]{2,1,0:T(8,128)(2,1)S(1)} %collective-permute-done.12), channel_id=1, source_target_pairs={{0,1},{1,0},{2,3},{3,2},{4,5},{5,4},{6,7},{7,6},{8,9},{9,8},{10,11... | collective-permute-start | bytes 786440 | tf_op jit(solution)/shard_map/ppermute | solution.py:25
  126.6 3.0 %copy-start.2 = (bf16[1,512,64]{1,2,0:T(8,128)(2,1)S(1)}, bf16[1,512,64]{1,2,0:T(8,128)(2,1)}, u32[]{:S(2)}) copy-start(bf16[1,512,64]{1,2,0:T(8,128)(2,1)} %param.15) | copy-start | bytes 196612
  129.4 2.1 %collective-permute-start.11 = (bf16[2,256,512]{2,1,0:T(8,128)(2,1)}, bf16[2,256,512]{2,1,0:T(8,128)(2,1)S(1)}, u32[]{:S(2)}, u32[]{:S(2)}) collective-permute-start(bf16[2,256,512]{2,1,0:T(8,128)(2,1)} %collective-permute-done.10), channel_id=1, source_target_pairs={{0,1},{1,0},{2,3},{3,2},{4,5},{5,4},{6,7},{7,6},{8,9},{9,8},{10,11... | collective-permute-start | bytes 1572872 | tf_op jit(solution)/shard_map/ppermute | solution.py:25
  132.6 1.6 copy-start.1
  134.2 27.9 %copy-start.6 = (bf16[512,128]{0,1:T(8,128)(2,1)S(1)}, bf16[512,128]{0,1:T(8,128)(2,1)}, u32[]{:S(2)}) copy-start(bf16[512,128]{0,1:T(8,128)(2,1)} %fusion.11) | copy-start | bytes 393220
  143.0 13.3 %collective-permute-start.1 = (bf16[128,512]{0,1:T(8,128)(2,1)S(1)}, bf16[128,512]{0,1:T(8,128)(2,1)S(1)}, u32[]{:S(2)}, u32[]{:S(2)}) collective-permute-start(bf16[128,512]{0,1:T(8,128)(2,1)S(1)} %slice.65), channel_id=1, source_target_pairs={{64,0},{128,64},{192,128},{65,1},{129,65},{193,129},{66,2},{130,66... | collective-permute-start | bytes 393224 | tf_op jit(solution)/shard_map/ppermute | solution.py:21
  144.3 15.1 %collective-permute-start.2 = (bf16[128,512]{0,1:T(8,128)(2,1)S(1)}, bf16[128,512]{0,1:T(8,128)(2,1)S(1)}, u32[]{:S(2)}, u32[]{:S(2)}) collective-permute-start(bf16[128,512]{0,1:T(8,128)(2,1)S(1)} %slice.65), channel_id=1, source_target_pairs={{128,0},{192,64},{129,1},{193,65},{130,2},{194,66},{131,3},{195,67... | collective-permute-start | bytes 393224 | tf_op jit(solution)/shard_map/ppermute | solution.py:21
  145.6 16.6 %collective-permute-start.3 = (bf16[128,512]{0,1:T(8,128)(2,1)S(1)}, bf16[128,512]{0,1:T(8,128)(2,1)S(1)}, u32[]{:S(2)}, u32[]{:S(2)}) collective-permute-start(bf16[128,512]{0,1:T(8,128)(2,1)S(1)} %slice.65), channel_id=1, source_target_pairs={{192,0},{193,1},{194,2},{195,3},{196,4},{197,5},{198,6},{199,7},{2... | collective-permute-start | bytes 393224 | tf_op jit(solution)/shard_map/ppermute | solution.py:21
  162.4 1.3 collective-permute-start.14
Sparse Core Ops, SparseCore 0:
  10.8 109.5 all-gather.1

commit v2 on v1

--- a/solution.py
+++ b/solution.py
@@ -16,47 +16,62 @@
     )
 
 
-def from_above(value, steps):
-    count = lax.axis_size("y")
-    return lax.ppermute(value, "y", [(i, i - steps) for i in range(steps, count)])
+def send(value, pairs):
+    return lax.ppermute(value, "y", pairs)
 
 
-def halves(mine, core, axis):
-    got = lax.ppermute(mine, "c", SWAP)
-    first = jnp.where(core == 0, mine, got)
-    second = jnp.where(core == 0, got, mine)
-    return jnp.concatenate([first, second], axis=axis)
-
-
-def grams(wv, right, core):
+def grams(wv, right, plane, core):
     width = wv.shape[1] // 2
     mine = lax.dynamic_slice_in_dim(wv, core * width, width, 1)
     other = lax.dynamic_slice_in_dim(wv, (1 - core) * width, width, 1)
     left = jnp.concatenate([mine, lax.ppermute(other, "c", SWAP)], axis=0)
     rows = jnp.concatenate([right, lax.ppermute(right, "c", SWAP)], axis=0)
-    parts = [dot(from_above(left, k), rows, 0).astype(BF16) for k in (1, 2, 3)]
+    near = send(left, [(1, 0), (2, 1), (3, 2)])
+    far = send(rows, [(1, 3)])
+    two, three = send(left, [(2, 0)]), send(left, [(3, 0)])
+    kv, columns = wv.shape[1], right.shape[1]
+    main = dot(jnp.where(plane == 3, left, near), jnp.where(plane == 3, far, rows), 0)
+    own = [dot(item, rows[:, kv:], 0) for item in (near, two, three)]
+    own = jnp.concatenate(own + [jnp.zeros((width, columns - 3 * (columns - kv)), F32)], axis=1)
+    parts = jnp.where(plane == 0, own, main).astype(BF16)
     ranks = lax.axis_size(XZ)
-    own = jnp.concatenate(parts, axis=0).reshape(ranks, -1, right.shape[1])
-    slices = lax.all_to_all(own, XZ, 0, 0)
+    shape = (ranks, width // ranks, columns)
+    slices = lax.all_to_all(parts.reshape(shape), XZ, 0, 0)
     total = jnp.sum(slices.astype(F32), axis=0).astype(BF16)
-    every = lax.all_to_all(jnp.broadcast_to(total[None], own.shape), XZ, 0, 0)
-    return every.reshape(3, width, right.shape[1])
+    every = lax.all_to_all(jnp.broadcast_to(total[None], shape), XZ, 0, 0)
+    return every.reshape(width, columns)
 
 
-def solve(half, pv_out, core, kv):
-    above_one = from_above(half[:2, :, :kv], 1)
-    above_two = from_above(half[:1, :, :kv], 2)
-    own = halves(half, core, 1)
-    g_one = halves(above_one, core, 1)
-    g_two = halves(above_two, core, 1)
-    first = [
-        jnp.concatenate([dot(own[k, :, :kv], pv_out), own[k, :, kv:].astype(F32)], axis=1)
-        for k in range(3)
+def solve(half, plane, core, kv):
+    count = lax.axis_size("y")
+    around = [half] + [
+        send(half, [(i, (i - k) % count) for i in range(count)]) for k in range(1, count)
     ]
-    e_one = first[0].astype(BF16)
-    e_two = (first[1] + dot(g_one[0], e_one)).astype(BF16)
-    e_three = (first[2] + dot(g_one[1], e_one) + dot(g_two[0], e_two)).astype(BF16)
-    return jnp.concatenate([e_one, e_two, e_three], axis=0)
+    planes = []
+    for p in range(count):
+        steps = (p - plane) % count
+        item = around[0]
+        for k in range(1, count):
+            item = jnp.where(steps == k, around[k], item)
+        planes.append(item)
+    mine = jnp.stack(planes)
+    got = lax.ppermute(mine, "c", SWAP)
+    first, second = jnp.where(core == 0, mine, got), jnp.where(core == 0, got, mine)
+    table = jnp.concatenate([first, second], axis=1)
+    block = half.shape[1] - kv
+    f01, f02, f03 = (table[0, :, k * block : (k + 1) * block] for k in range(3))
+    g21, g32, g31 = (table[k, :, :kv] for k in (1, 2, 3))
+    f12, f23, f13 = (table[k, :, kv:] for k in (1, 2, 3))
+    e02 = (f02.astype(F32) + dot(g21, f01)).astype(BF16)
+    e13 = (f13.astype(F32) + dot(g32, f12)).astype(BF16)
+    e03 = (f03.astype(F32) + dot(g31, f01) + dot(g32, e02)).astype(BF16)
+    zero = jnp.zeros_like(f01)
+    columns = (
+        jnp.where(plane == 1, f01, jnp.where(plane == 2, e02, e03)),
+        jnp.where(plane == 2, f12, jnp.where(plane == 3, e13, zero)),
+        jnp.where(plane == 3, f23, zero),
+    )
+    return jnp.concatenate(columns, axis=1)
 
 
 def doc_sums(left, right, slots, core, rank):
@@ -72,7 +87,7 @@
 def body(
     hidden, cotangent, w_value, w_out_t, p_in, p_value_out, p_value_in, p_out, segments, owner_slot
 ):
-    core = lax.axis_index("c")
+    plane, core = lax.axis_index("y"), lax.axis_index("c")
     device = lax.axis_index(DP)
     wv, wo, acts = w_value[0], w_out_t[0], hidden[0]
     rows, kv = wv.shape
@@ -83,8 +98,9 @@
     full = lax.all_gather(mixed, DP, axis=0, tiled=True)
 
     out_rows = lax.dynamic_slice_in_dim(p_out[0], device * rows, rows, 0)
-    half = grams(wv, jnp.concatenate([wo, out_rows], axis=1), core)
-    spread_e = solve(half, p_value_out[0], core, kv)
+    projected = dot(wo, p_value_out[0]).astype(BF16)
+    right_rows = jnp.concatenate([wo, projected, out_rows], axis=1)
+    spread_e = solve(grams(wv, right_rows, plane, core), plane, core, kv)
 
     match = segments[:, None] == jnp.arange(documents, dtype=jnp.int32)[None, :]
     slots = jnp.sum(jnp.where(match, owner_slot[None, :], 0), axis=1)
@@ -96,9 +112,14 @@
 
     product = dot(both, full).astype(BF16)
     upd = product[:tokens, :kv]
-    above = jnp.concatenate([from_above(upd, k) for k in (1, 2, 3)], axis=1)
-    direct = jnp.concatenate([dot(upd, p_value_out[0]), direct_out], axis=1)
-    right = (direct + dot(above, spread_e)).astype(BF16)
+    right = jnp.concatenate([dot(upd, p_value_out[0]), direct_out], axis=1)
+    below = dot(upd, spread_e).astype(BF16)
+    count = lax.axis_size("y")
+    for k in range(1, count):
+        start = jnp.maximum(plane - k, 0) * 2 * rank
+        item = lax.dynamic_slice_in_dim(below, start, 2 * rank, 1)
+        right = right + send(item, [(i, i - k) for i in range(k, count)]).astype(F32)
+    right = right.astype(BF16)
     left = jnp.concatenate([first_in.astype(BF16), product[tokens:, kv:]], axis=1)
     packed = jnp.concatenate([left, right], axis=1)
     packed = jnp.concatenate([packed, lax.ppermute(packed, "c", SWAP)], axis=0)

time: 196 us -> 156 us (0.80)
  waiting for transfers between devices: 71.8 us -> 22.5 us
  starting transfers between devices: 16.9 us -> 22.4 us
  other arithmetic: 3.48 us -> 7.72 us
  blocking collectives: 63.3 us -> 66.7 us
  local copies, waits for them, and re-layouts: 6.38 us -> 3.64 us
  matrix products: 20.1 us -> 17.8 us
    all_to_all x1 -> x0, waiting for transfers between devices: 34.6 us -> none  [grams(): every = lax.all_to_all(jnp.broadcast_to(total[None], own.shape), XZ, 0, 0)]
    ppermute x11, waiting for transfers between devices: 35.3 us -> 21.3 us  [the longest x10 21.3 us: send(): return lax.ppermute(value, 'y', pairs)]
    ppermute x11, starting transfers between devices: 10.4 us -> 20.9 us  [the longest x10 20.9 us: send(): return lax.ppermute(value, 'y', pairs)]
    all_to_all x1 -> x0, starting transfers between devices: 5.67 us -> none  [grams(): every = lax.all_to_all(jnp.broadcast_to(total[None], own.shape), XZ, 0, 0)]
    all_to_all x1 -> x2, blocking collectives: 39.8 us -> 43.4 us  [the longest x1 25.8 us: grams(): slices = lax.all_to_all(parts.reshape(shape), XZ, 0, 0)]
    another operation x0 -> x2, other arithmetic: none -> 2.38 us  [solve(): mine = jnp.stack(planes)]
    dot_general x16, matrix products: 20.1 us -> 17.8 us  [dot(): lax.dot_general(left, right, (((left_dim,), (0,)), ((), ())), preferred_e...]
  transfers between devices with their start and end apart: 17 -> 16, of which waited for: 11 -> 6; matrix products, arithmetic and copies ran while one was open for 8% -> 9% of each run, Pallas kernels for 0% -> 0%
where the time goes in v2:
time: 156 us; the launch traced here: 155 us
  blocking collectives  66.7 us (43%)
  waiting for transfers between devices  22.5 us (14%)
  starting transfers between devices  22.4 us (14%)
  matrix products  17.8 us (11%)
  between operations  13.9 us (9%)
  other arithmetic  7.72 us (5%)
  local copies, waits for them, and re-layouts  3.64 us (2%)
    all_to_all x1, blocking collectives, grams(): slices = lax.all_to_all(parts.reshape(shape), XZ, 0, 0)  25.8 us
    all_to_all x1, blocking collectives, body(): parts = lax.all_to_all(sums, XZ, 0, 0)  23.3 us
    ppermute x10, waiting for transfers between devices, send(): return lax.ppermute(value, 'y', pairs)  21.3 us
    ppermute x10, starting transfers between devices, send(): return lax.ppermute(value, 'y', pairs)  20.9 us
    dot_general x16, matrix products, dot(): lax.dot_general(left, right, (((left_dim,), (0,)), ((), ())), preferred_e...  17.8 us
    all_to_all x1, blocking collectives, grams(): every = lax.all_to_all(jnp.broadcast_to(total[None], shape), XZ, 0, 0)  17.6 us
  transfers between devices with their start and end apart: 16, of which 6 were waited for; matrix products, arithmetic and copies ran while one was open for 9% of the time, Pallas kernels for 0%

profile of v2, /device:TPU:32, one launch (start us, length us, event | category | flops | bytes accessed | tf_op | source)
XLA Modules:
  0.0 154.6 jit_solution(5521022488754018583)
XLA Ops:
  6.5 1.2 convolution_convert_fusion.2
  7.7 0.1 copy.48
  7.8 1.6 %pad_maximum_fusion.2 = bf16[128,576]{1,0:T(8,128)(2,1)} fusion(bf16[128,64]{1,0:T(8,128)(2,1)S(1)} %copy.48, bf16[128,512]{1,0:T(8,128)(2,1)} %bitcast.96), kind=kLoop, calls=%fused_computation.68 | loop fusion | flops 294912 | bytes 294912 | tf_op jit(solution)/shard_map/concatenate | solution.py:97
  9.4 0.9 dynamic-slice_bitcast_fusion.1
  10.6 1.1 convolution_convert_fusion.1
  11.7 0.1 copy.49
  11.8 1.0 pad_maximum_fusion.3
  12.8 0.6 collective-permute-start.3
  13.4 1.3 collective-permute-start.5
  14.7 1.3 collective-permute-start.4
  16.0 1.3 collective-permute-start.2
  17.4 0.7 collective-permute-start.6
  18.1 6.6 %collective-permute-done.5 = bf16[256,256]{1,0:T(8,128)(2,1)S(1)} collective-permute-done((bf16[256,256]{1,0:T(8,128)(2,1)S(1)}, bf16[256,256]{1,0:T(8,128)(2,1)S(1)}, u32[]{:S(2)}, u32[]{:S(2)}) %collective-permute-start.5) | collective-permute-done | bytes 131104 | tf_op jit(solution)/shard_map/ppermute | solution.py:20
  24.7 0.2 fusion.70
  25.0 0.2 fusion.72
  25.2 0.2 fusion.74
  25.5 0.3 fusion.35
  25.8 25.8 %all_to_all.15 = bf16[32,8,640]{2,1,0:T(8,128)(2,1)S(1)} all-to-all(bf16[32,8,640]{2,1,0:T(8,128)(2,1)S(1)} %fusion.35), channel_id=1, replica_groups=mesh['y'=4,'x'=4,'z'=8,'c'=2] {'x','z'}, dimensions={0} | all-to-all | bytes 655360 | tf_op jit(solution)/shard_map/all_to_all | solution.py:39
  51.6 17.6 %all_to_all.16 = bf16[32,8,640]{2,1,0:T(8,128)(2,1)S(1)} all-to-all(bf16[32,8,640]{2,1,0:T(8,128)(2,1)S(1)} %broadcast_in_dim.45), channel_id=1, replica_groups=mesh['y'=4,'x'=4,'z'=8,'c'=2] {'x','z'}, dimensions={0} | all-to-all | bytes 655360 | tf_op jit(solution)/shard_map/all_to_all | solution.py:41
  69.3 0.2 copy.54
  69.4 6.5 %collective-permute-start.7 = (bf16[256,640]{0,1:T(8,128)(2,1)S(1)}, bf16[256,640]{0,1:T(8,128)(2,1)S(1)}, u32[]{:S(2)}, u32[]{:S(2)}) collective-permute-start(bf16[256,640]{0,1:T(8,128)(2,1)S(1)} %copy.54), channel_id=1, source_target_pairs={{0,64},{64,128},{128,192},{192,0},{1,65},{65,129},{129,193},{193,1... | collective-permute-start | bytes 983048 | tf_op jit(solution)/shard_map/ppermute | solution.py:20
  76.0 5.9 %collective-permute-start.8 = (bf16[256,640]{0,1:T(8,128)(2,1)S(1)}, bf16[256,640]{0,1:T(8,128)(2,1)S(1)}, u32[]{:S(2)}, u32[]{:S(2)}) collective-permute-start(bf16[256,640]{0,1:T(8,128)(2,1)S(1)} %copy.54), channel_id=1, source_target_pairs={{0,128},{64,192},{128,0},{192,64},{1,129},{65,193},{129,1},{193,65... | collective-permute-start | bytes 983048 | tf_op jit(solution)/shard_map/ppermute | solution.py:20
  81.9 6.6 %collective-permute-done.7 = bf16[256,640]{0,1:T(8,128)(2,1)S(1)} collective-permute-done((bf16[256,640]{0,1:T(8,128)(2,1)S(1)}, bf16[256,640]{0,1:T(8,128)(2,1)S(1)}, u32[]{:S(2)}, u32[]{:S(2)}) %collective-permute-start.7) | collective-permute-done | bytes 327712 | tf_op jit(solution)/shard_map/ppermute | solution.py:20
  88.5 3.5 %collective-permute-done.8 = bf16[256,640]{0,1:T(8,128)(2,1)S(1)} collective-permute-done((bf16[256,640]{0,1:T(8,128)(2,1)S(1)}, bf16[256,640]{0,1:T(8,128)(2,1)S(1)}, u32[]{:S(2)}, u32[]{:S(2)}) %collective-permute-start.8) | collective-permute-done | bytes 327712 | tf_op jit(solution)/shard_map/ppermute | solution.py:20
  92.0 1.2 select_bitcast_fusion.3
  93.2 1.2 pad_maximum_fusion
  94.5 0.8 collective-permute-start
  95.3 2.9 %convolution_convert_fusion.3 = bf16[128,64]{0,1:T(8,128)(2,1)S(1)} fusion(bf16[1,8192,64]{1,2,0:T(8,128)(2,1)} %param.14, bf16[1,128,8192]{2,1,0:T(8,128)(2,1)} %param.10), kind=kOutput, calls=%fused_computation.30 | convolution fusion | flops 134225920 | bytes 3162112 | tf_op jit(solution)/shard_map/dot_general | solution.py:14
  98.2 0.8 fusion.14
  99.1 1.6 %broadcast_select_fusion.1 = (bf16[4,256,640]{1,2,0:T(8,128)(2,1)S(1)}, bf16[4,256,640]{1,2,0:T(8,128)(2,1)S(1)}) fusion(bf16[4,256,640]{1,2,0:T(8,128)(2,1)} %collective-permute-done.10, pred[]{:T(512)S(6)} %eq.98, bf16[1,256,640]{1,2,0:T(8,128)(2,1)S(1)} %get-tuple-element.8, bf16[1,256,640]{1,2,0:T(8,128)(2,1)S(1)} %get-tuple-element.9, ...), kind=kLoop, calls=%fused_computation.21 | loop fusion | flops 3276800 | bytes 5242881 | tf_op jit(solution)/shard_map/jit(_where)/select_n | solution.py:59
  100.7 0.7 fusion.50
  101.3 0.2 fusion.48
  101.6 0.2 fusion.26
  101.8 0.2 fusion.28
  102.1 0.3 fusion.12
  102.3 1.3 copy-done.2
  103.6 8.7 %fusion.7 = bf16[256,576]{0,1:T(8,128)(2,1)S(1)} fusion(bf16[8192,576]{1,0:T(8,128)(2,1)} %all-gather.2.cloned.1.call-done, bf16[128,8192]{1,0:T(8,128)(2,1)} %bitcast.95, bf16[128,8192]{1,0:T(8,128)(2,1)S(1)} %copy-done.2), kind=kOutput, calls=%fused_computation.22 | convolution fusion | flops 2424455168 | bytes 13926400 | tf_op jit(solution)/shard_map/dot_general | solution.py:14
  112.4 0.3 convolution_convert_fusion
  112.7 1.3 collective-permute-start.13
  114.0 1.3 collective-permute-start.12
  115.3 1.3 collective-permute-start.11
  116.6 0.2 fusion.61
  116.8 2.9 %collective-permute-done.13 = bf16[128,128]{0,1:T(8,128)(2,1)S(1)} collective-permute-done((bf16[128,128]{0,1:T(8,128)(2,1)S(1)}, bf16[128,128]{0,1:T(8,128)(2,1)S(1)}, u32[]{:S(2)}, u32[]{:S(2)}) %collective-permute-start.13) | collective-permute-done | bytes 32800 | tf_op jit(solution)/shard_map/ppermute | solution.py:20
  119.7 1.6 %collective-permute-done.12 = bf16[128,128]{0,1:T(8,128)(2,1)S(1)} collective-permute-done((bf16[128,128]{0,1:T(8,128)(2,1)S(1)}, bf16[128,128]{0,1:T(8,128)(2,1)S(1)}, u32[]{:S(2)}, u32[]{:S(2)}) %collective-permute-start.12) | collective-permute-done | bytes 32800 | tf_op jit(solution)/shard_map/ppermute | solution.py:20
  121.5 1.2 collective-permute-done.14
  122.7 0.7 fusion.4
  123.5 23.3 %all_to_all.17 = bf16[32,64,128]{2,1,0:T(8,128)(2,1)S(1)} all-to-all(bf16[32,64,128]{2,1,0:T(8,128)(2,1)S(1)} %fusion.13), channel_id=1, replica_groups=mesh['y'=4,'x'=4,'z'=8,'c'=2] {'x','z'}, dimensions={0} | all-to-all | bytes 1048576 | tf_op jit(solution)/shard_map/all_to_all | solution.py:127
  147.0 0.7 reshape.76
  (54 shorter events, 1.1 us)
Async XLA Ops:
  6.5 3.9 %copy-start = (bf16[1,8192,64]{1,2,0:T(8,128)(2,1)S(1)}, bf16[1,8192,64]{1,2,0:T(8,128)(2,1)}, u32[]{:S(2)}) copy-start(bf16[1,8192,64]{1,2,0:T(8,128)(2,1)} %param.17) | copy-start | bytes 3145732
  6.5 10.8 %copy-start.3 = (bf16[1,128,512]{2,1,0:T(8,128)(2,1)S(1)}, bf16[1,128,512]{2,1,0:T(8,128)(2,1)}, u32[]{:S(2)}) copy-start(bf16[1,128,512]{2,1,0:T(8,128)(2,1)} %param.13) | copy-start | bytes 393220
  6.5 95.8 %all-gather.2.cloned.1.call-start = ((), (), s32[]{:S(2)}) async-start(), calls=%async_computation.3 | async-start | bytes 10649600 | tf_op jit(solution)/shard_map/all_gather | solution.py:98
  10.3 3.0 %collective-permute-start.1 = (bf16[128,256]{1,0:T(8,128)(2,1)S(1)}, bf16[128,256]{1,0:T(8,128)(2,1)S(1)}, u32[]{:S(2)}, u32[]{:S(2)}) collective-permute-start(bf16[128,256]{1,0:T(8,128)(2,1)S(1)} %get-tuple-element.12), channel_id=1, source_target_pairs={{0,1},{1,0},{2,3},{3,2},{4,5},{5,4},{6,7},{7,6},{8,9},{9,8},{10,11... | collective-permute-start | bytes 196616 | tf_op jit(solution)/shard_map/ppermute | solution.py:27
  12.8 4.5 %collective-permute-start.3 = (bf16[128,640]{1,0:T(8,128)(2,1)S(1)}, bf16[128,640]{1,0:T(8,128)(2,1)S(1)}, u32[]{:S(2)}, u32[]{:S(2)}) collective-permute-start(bf16[128,640]{1,0:T(8,128)(2,1)S(1)} %pad_maximum_fusion.3), channel_id=1, source_target_pairs={{0,1},{1,0},{2,3},{3,2},{4,5},{5,4},{6,7},{7,6},{8,9},{9,8},{10,11... | collective-permute-start | bytes 491528 | tf_op jit(solution)/shard_map/ppermute | solution.py:28
  13.4 11.4 %collective-permute-start.5 = (bf16[256,256]{1,0:T(8,128)(2,1)S(1)}, bf16[256,256]{1,0:T(8,128)(2,1)S(1)}, u32[]{:S(2)}, u32[]{:S(2)}) collective-permute-start(bf16[256,256]{1,0:T(8,128)(2,1)S(1)} %pad_maximum_fusion.5), channel_id=1, source_target_pairs={{192,0},{193,1},{194,2},{195,3},{196,4},{197,5},{198,6},{199,7},{2... | collective-permute-start | bytes 393224 | tf_op jit(solution)/shard_map/ppermute | solution.py:20
  14.7 10.3 %collective-permute-start.4 = (bf16[256,256]{1,0:T(8,128)(2,1)S(1)}, bf16[256,256]{1,0:T(8,128)(2,1)S(1)}, u32[]{:S(2)}, u32[]{:S(2)}) collective-permute-start(bf16[256,256]{1,0:T(8,128)(2,1)S(1)} %pad_maximum_fusion.5), channel_id=1, source_target_pairs={{128,0},{129,1},{130,2},{131,3},{132,4},{133,5},{134,6},{135,7},{1... | collective-permute-start | bytes 393224 | tf_op jit(solution)/shard_map/ppermute | solution.py:20
  16.0 9.2 %collective-permute-start.2 = (bf16[256,256]{1,0:T(8,128)(2,1)S(1)}, bf16[256,256]{1,0:T(8,128)(2,1)S(1)}, u32[]{:S(2)}, u32[]{:S(2)}) collective-permute-start(bf16[256,256]{1,0:T(8,128)(2,1)S(1)} %pad_maximum_fusion.5), channel_id=1, source_target_pairs={{64,0},{128,64},{192,128},{65,1},{129,65},{193,129},{66,2},{130,66... | collective-permute-start | bytes 393224 | tf_op jit(solution)/shard_map/ppermute | solution.py:20
  17.4 8.0 %collective-permute-start.6 = (bf16[256,640]{1,0:T(8,128)(2,1)S(1)}, bf16[256,640]{1,0:T(8,128)(2,1)S(1)}, u32[]{:S(2)}, u32[]{:S(2)}) collective-permute-start(bf16[256,640]{1,0:T(8,128)(2,1)S(1)} %pad_maximum_fusion.1), channel_id=1, source_target_pairs={{64,192},{65,193},{66,194},{67,195},{68,196},{69,197},{70,198},{71... | collective-permute-start | bytes 983048 | tf_op jit(solution)/shard_map/ppermute | solution.py:20
  69.4 19.1 %collective-permute-start.7 = (bf16[256,640]{0,1:T(8,128)(2,1)S(1)}, bf16[256,640]{0,1:T(8,128)(2,1)S(1)}, u32[]{:S(2)}, u32[]{:S(2)}) collective-permute-start(bf16[256,640]{0,1:T(8,128)(2,1)S(1)} %copy.54), channel_id=1, source_target_pairs={{0,64},{64,128},{128,192},{192,0},{1,65},{65,129},{129,193},{193,1... | collective-permute-start | bytes 983048 | tf_op jit(solution)/shard_map/ppermute | solution.py:20
  76.0 16.0 %collective-permute-start.8 = (bf16[256,640]{0,1:T(8,128)(2,1)S(1)}, bf16[256,640]{0,1:T(8,128)(2,1)S(1)}, u32[]{:S(2)}, u32[]{:S(2)}) collective-permute-start(bf16[256,640]{0,1:T(8,128)(2,1)S(1)} %copy.54), channel_id=1, source_target_pairs={{0,128},{64,192},{128,0},{192,64},{1,129},{65,193},{129,1},{193,65... | collective-permute-start | bytes 983048 | tf_op jit(solution)/shard_map/ppermute | solution.py:20
  81.8 10.2 %collective-permute-start.9 = (bf16[256,640]{0,1:T(8,128)(2,1)S(1)}, bf16[256,640]{0,1:T(8,128)(2,1)}, u32[]{:S(2)}, u32[]{:S(2)}) collective-permute-start(bf16[256,640]{0,1:T(8,128)(2,1)S(1)} %copy.54), channel_id=1, source_target_pairs={{0,192},{64,0},{128,64},{192,128},{1,193},{65,1},{129,65},{193,129... | collective-permute-start | bytes 983048 | tf_op jit(solution)/shard_map/ppermute | solution.py:20
  81.9 12.5 %copy-start.6 = (s32[64]{0:T(128)S(1)}, s32[64]{0:T(128)}, u32[]{:S(2)}) copy-start(s32[64]{0:T(128)} %param.19) | copy-start | bytes 772
  81.9 12.5 %copy-start.7 = (s32[128]{0:T(128)S(1)}, s32[128]{0:T(128)}, u32[]{:S(2)}) copy-start(s32[128]{0:T(128)} %param.18) | copy-start | bytes 1540
  94.4 4.7 %collective-permute-start.10 = (bf16[4,256,640]{1,2,0:T(8,128)(2,1)}, bf16[4,256,640]{1,2,0:T(8,128)(2,1)}, u32[]{:S(2)}, u32[]{:S(2)}) collective-permute-start(bf16[4,256,640]{1,2,0:T(8,128)(2,1)} %pad_maximum_fusion), channel_id=1, source_target_pairs={{0,1},{1,0},{2,3},{3,2},{4,5},{5,4},{6,7},{7,6},{8,9},{9,8},{10,11... | collective-permute-start | bytes 3932168 | tf_op jit(solution)/shard_map/ppermute | solution.py:58
  94.5 4.6 %collective-permute-start = (s32[128]{0:T(128)S(1)}, s32[128]{0:T(128)S(1)}, u32[]{:S(2)}, u32[]{:S(2)}) collective-permute-start(s32[128]{0:T(128)S(1)} %select_reduce_fusion), channel_id=1, source_target_pairs={{0,1},{1,0},{2,3},{3,2},{4,5},{5,4},{6,7},{7,6},{8,9},{9,8},{10,11... | collective-permute-start | bytes 1544 | tf_op jit(solution)/shard_map/ppermute | solution.py:107
  95.3 2.9 %copy-start.1 = (bf16[128,8192]{1,0:T(8,128)(2,1)S(1)}, bf16[128,8192]{1,0:T(8,128)(2,1)}, u32[]{:S(2)}) copy-start(bf16[128,8192]{1,0:T(8,128)(2,1)} %param.11) | copy-start | bytes 6291460
  102.0 1.6 %copy-start.2 = (bf16[128,8192]{1,0:T(8,128)(2,1)S(1)}, bf16[128,8192]{1,0:T(8,128)(2,1)}, u32[]{:S(2)}) copy-start(bf16[128,8192]{1,0:T(8,128)(2,1)} %param.11) | copy-start | bytes 6291460
  103.6 8.7 %copy-start.5 = (bf16[512,128]{0,1:T(8,128)(2,1)S(1)}, bf16[512,128]{0,1:T(8,128)(2,1)}, u32[]{:S(2)}) copy-start(bf16[512,128]{0,1:T(8,128)(2,1)} %fusion.50) | copy-start | bytes 393220
  103.6 12.9 %copy-start.4 = (bf16[1,512,64]{1,2,0:T(8,128)(2,1)S(1)}, bf16[1,512,64]{1,2,0:T(8,128)(2,1)}, u32[]{:S(2)}) copy-start(bf16[1,512,64]{1,2,0:T(8,128)(2,1)} %param.15) | copy-start | bytes 196612
  112.7 7.0 %collective-permute-start.13 = (bf16[128,128]{0,1:T(8,128)(2,1)S(1)}, bf16[128,128]{0,1:T(8,128)(2,1)S(1)}, u32[]{:S(2)}, u32[]{:S(2)}) collective-permute-start(bf16[128,128]{0,1:T(8,128)(2,1)S(1)} %get-tuple-element.14), channel_id=1, source_target_pairs={{192,0},{193,1},{194,2},{195,3},{196,4},{197,5},{198,6},{199,7},{2... | collective-permute-start | bytes 98312 | tf_op jit(solution)/shard_map/ppermute | solution.py:20
  114.0 7.3 %collective-permute-start.12 = (bf16[128,128]{0,1:T(8,128)(2,1)S(1)}, bf16[128,128]{0,1:T(8,128)(2,1)S(1)}, u32[]{:S(2)}, u32[]{:S(2)}) collective-permute-start(bf16[128,128]{0,1:T(8,128)(2,1)S(1)} %get-tuple-element.15), channel_id=1, source_target_pairs={{128,0},{192,64},{129,1},{193,65},{130,2},{194,66},{131,3},{195,67... | collective-permute-start | bytes 98312 | tf_op jit(solution)/shard_map/ppermute | solution.py:20
  115.3 6.0 %collective-permute-start.11 = (bf16[128,128]{0,1:T(8,128)(2,1)S(1)}, bf16[128,128]{0,1:T(8,128)(2,1)S(1)}, u32[]{:S(2)}, u32[]{:S(2)}) collective-permute-start(bf16[128,128]{0,1:T(8,128)(2,1)S(1)} %get-tuple-element.13), channel_id=1, source_target_pairs={{64,0},{128,64},{192,128},{65,1},{129,65},{193,129},{66,2},{130,66... | collective-permute-start | bytes 98312 | tf_op jit(solution)/shard_map/ppermute | solution.py:20
  121.3 1.3 collective-permute-start.14
Sparse Core Ops, SparseCore 0:
  10.1 89.5 all-gather.1

commit v3 on v2

v3 whole, which is shorter than its diff:
```python
import jax
import jax.numpy as jnp
from jax import lax
from jax.experimental import pallas as pl
from jax.experimental.pallas import tpu as pltpu
from jax.sharding import Mesh, PartitionSpec as P

XZ = ("x", "z")
DP = ("x", "z", "c")
SWAP = [(0, 1), (1, 0)]
BF16 = jnp.bfloat16
F32 = jnp.float32


def dot(left, right, left_dim=1):
    return lax.dot_general(
        left, right, (((left_dim,), (0,)), ((), ())), preferred_element_type=F32
    )


def send(value, pairs):
    return lax.ppermute(value, "y", pairs)


def swap(value):
    return lax.ppermute(value, "c", SWAP)


def half_of(value, core, axis=1):
    width = value.shape[axis] // 2
    return lax.dynamic_slice_in_dim(value, core * width, width, axis)


def ordered(mine, core):
    got = swap(mine)
    return jnp.concatenate([jnp.where(core == 0, mine, got), jnp.where(core == 0, got, mine)])


def gather(wo, projected, core):
    mine = jnp.concatenate([half_of(wo, core), projected], axis=1)
    other = jnp.concatenate([half_of(wo, 1 - core), projected], axis=1)
    got = swap(other)
    chip = jnp.concatenate([jnp.where(core == 0, mine, got), jnp.where(core == 0, got, mine)])
    width = wo.shape[1] // 2
    shard = jnp.concatenate([chip[:, :width], chip[:, width:].T], axis=0)
    count, place = lax.axis_size("x"), lax.axis_index("x")
    around = [shard] + [
        lax.ppermute(shard, "x", [(i, (i - k) % count) for i in range(count)])
        for k in range(1, count)
    ]
    column = []
    for p in range(count):
        steps = (p - place) % count
        item = around[0]
        for k in range(1, count):
            item = jnp.where(steps == k, around[k], item)
        column.append(item)
    return lax.all_gather(jnp.stack(column), "z", axis=0, tiled=True)


def product_kernel(across, cot_mine, cot_got, act_mine, act_got, block, upd, value, upd_sum, value_sum):
    step, last = pl.program_id(0), pl.num_programs(0) - 1
    width = block.shape[2]

    @pl.when(step == 0)
    def _():
        upd_sum[...] = jnp.zeros_like(upd_sum)
        value_sum[...] = jnp.zeros_like(value_sum)

    for k in range(across):
        start = pl.multiple_of((k * (last + 1) + step) * width, width)
        cols = pl.ds(start, width)
        cot = jnp.concatenate([cot_mine[:, cols], cot_got[:, cols]], axis=0)
        act = jnp.concatenate([act_mine[:, cols], act_got[:, cols]], axis=0)
        upd_sum[...] += jnp.dot(cot, block[k, :width, :], preferred_element_type=F32)
        value_sum[...] += lax.dot_general(
            act, block[k, width:, :], (((1,), (1,)), ((), ())), preferred_element_type=F32
        )

    @pl.when(step == last)
    def _():
        upd[...] = upd_sum[...].astype(BF16)
        value[...] = value_sum[...].astype(BF16)


def products(cot_mine, cot_got, act_mine, act_got, full, across):
    tokens, depth = cot_mine.shape
    count, rows, width = full.shape
    rank = rows - width
    whole = pl.BlockSpec(memory_space=pltpu.VMEM)
    return pl.pallas_call(
        lambda *refs: product_kernel(across, *refs),
        grid=(count // across,),
        in_specs=[whole] * 4 + [pl.BlockSpec((across, rows, width), lambda i: (i, 0, 0))],
        out_specs=[whole, whole],
        out_shape=[
            jax.ShapeDtypeStruct((2 * tokens, width), BF16),
            jax.ShapeDtypeStruct((2 * tokens, rank), BF16),
        ],
        scratch_shapes=[
            pltpu.VMEM((2 * tokens, width), F32),
            pltpu.VMEM((2 * tokens, rank), F32),
        ],
        compiler_params=pltpu.CompilerParams(
            dimension_semantics=("arbitrary",), vmem_limit_bytes=40 * 1024 * 1024
        ),
        cost_estimate=pl.CostEstimate(
            flops=4 * tokens * depth * rows, bytes_accessed=2 * full.size, transcendentals=0
        ),
    )(cot_mine, cot_got, act_mine, act_got, full)


def grams(wv, right, plane, core, later):
    kv, columns = wv.shape[1], right.shape[1]
    width = kv // 2
    near, far = send(wv, [(3, 0), (2, 1)]), send(wv, [(3, 1)])
    above, below = send(right, [(0, 1), (1, 2), (2, 3)]), send(right, [(1, 0)])
    right = jnp.where(plane == 0, below, above)
    lefts = [jnp.where(plane == 0, near, wv), near, far]
    got = swap(jnp.concatenate([half_of(item, 1 - core) for item in lefts], axis=1))
    mine = jnp.concatenate([half_of(item, core) for item in lefts], axis=1)
    left = jnp.concatenate([mine, got], axis=0)
    rows = jnp.concatenate([right, swap(right)], axis=0)
    main = dot(left[:, :width], rows, 0)
    own = [dot(left[:, k * width : (k + 1) * width], rows[:, kv:], 0) for k in range(3)]
    own = jnp.concatenate(own + [jnp.zeros((width, columns - 3 * (columns - kv)), F32)], axis=1)
    parts = jnp.where(plane == 1, own, main).astype(BF16)
    parts, *later = lax.optimization_barrier((parts, *later))
    ranks = lax.axis_size(XZ)
    shape = (ranks, width // ranks, columns)
    slices = lax.all_to_all(parts.reshape(shape), XZ, 0, 0)
    total = jnp.sum(slices.astype(F32), axis=0).astype(BF16)
    every = lax.all_to_all(jnp.broadcast_to(total[None], shape), XZ, 0, 0)
    return every.reshape(width, columns), [swap(item) for item in later]


def solve(half, plane, core, kv):
    block = half.shape[1] - kv
    above = send(half, [(1, 2), (2, 3)])
    wrap = send(half, [(0, 3)])
    twice = send(half[:, : 3 * block], [(1, 3)])
    first = jnp.where(plane == 1, half[:, : 3 * block], above[:, : 3 * block])
    first = jnp.where(plane == 3, twice, first)
    second = jnp.where(plane == 2, half, above)
    f01, f02, f03 = (first[:, k * block : (k + 1) * block] for k in range(3))
    g21, g31, g32 = second[:, :kv], wrap[:, :kv], half[:, :kv]
    f12, f13, f23 = second[:, kv:], wrap[:, kv:], half[:, kv:]
    known = ordered(jnp.concatenate([f01, f12], axis=1), core)
    f01_all, f12_all = known[:, :block], known[:, block:]
    e02 = (f02.astype(F32) + dot(g21, f01_all)).astype(BF16)
    e02_all = ordered(e02, core)
    e13 = (f13.astype(F32) + dot(g32, f12_all)).astype(BF16)
    e03 = (f03.astype(F32) + dot(g31, f01_all) + dot(g32, e02_all)).astype(BF16)
    zero = jnp.zeros_like(f01)
    columns = (
        jnp.where(plane == 1, f01, jnp.where(plane == 2, e02, e03)),
        jnp.where(plane == 2, f12, jnp.where(plane == 3, e13, zero)),
        jnp.where(plane == 3, f23, zero),
    )
    return jnp.concatenate(columns, axis=1)


def doc_sums(left, right, slots, core, rank):
    owners = lax.axis_size(XZ)
    named = 2 * jnp.arange(owners, dtype=jnp.int32) + core
    onehot = (slots[:, None] == named[None, :]).astype(BF16)
    spread = (onehot[:, :, None] * left[:, None, :]).reshape(left.shape[0], owners * 2 * rank)
    table = dot(spread, right, 0).reshape(owners, 2 * rank, 2 * rank)
    lane = lax.broadcasted_iota(jnp.int32, (1, rank, 2 * rank), 2)
    return jnp.where(lane < rank, table[:, :rank], table[:, rank:]).astype(BF16)


def body(
    hidden, cotangent, w_value, w_out_t, p_in, p_value_out, p_value_in, p_out, segments, owner_slot
):
    plane, core = lax.axis_index("y"), lax.axis_index("c")
    device = lax.axis_index(DP)
    wv, wo, acts = w_value[0], w_out_t[0], hidden[0]
    rows, kv = wv.shape
    rank = p_in.shape[2]
    documents = owner_slot.shape[0]
    tokens = cotangent.shape[0]

    full = gather(wo, dot(wv, p_value_in[0]).astype(BF16), core)

    out_rows = lax.dynamic_slice_in_dim(p_out[0], device * rows, rows, 0)
    right_rows = jnp.concatenate([wo, dot(wo, p_value_out[0]).astype(BF16), out_rows], axis=1)
    half, (cot_got, act_got) = grams(wv, right_rows, plane, core, (cotangent, acts))
    spread_e = solve(half, plane, core, kv)

    match = segments[:, None] == jnp.arange(documents, dtype=jnp.int32)[None, :]
    slots = jnp.sum(jnp.where(match, owner_slot[None, :], 0), axis=1)
    slots = jnp.concatenate([slots, swap(slots)])
    first_in = dot(acts, p_in[0]).astype(BF16)
    first_in = jnp.concatenate([first_in, swap(first_in)], axis=0)
    direct_out = dot(cotangent, p_out[0])
    direct_out = jnp.concatenate([direct_out, jnp.zeros_like(direct_out)], axis=0)

    upd, second_in = products(
        cotangent, cot_got, acts, act_got, full.reshape(-1, *full.shape[-2:]), lax.axis_size("x")
    )
    right = jnp.concatenate([dot(upd, half_of(p_value_out[0], core, 0)), direct_out], axis=1)
    below = dot(upd, spread_e).astype(BF16)
    count = lax.axis_size("y")
    for k in range(1, count):
        start = jnp.maximum(plane - k, 0) * 2 * rank
        item = lax.dynamic_slice_in_dim(below, start, 2 * rank, 1)
        right = right + send(item, [(i, i - k) for i in range(k, count)]).astype(F32)
    right = (right + swap(jnp.concatenate([right[tokens:], right[:tokens]], axis=0))).astype(BF16)
    left = jnp.concatenate([first_in, second_in], axis=1)
    parts = lax.all_to_all(doc_sums(left, right, slots, core, rank), XZ, 0, 0)
    total = jnp.sum(parts.astype(F32), axis=0)
    tables = total.reshape(rank, 2, rank).transpose(1, 0, 2)
    return tables.reshape(1, 2, 1, rank * rank)


def solution(mesh):
    grid = Mesh(mesh.devices.reshape(4, 4, 8, 2), ("y", "x", "z", "c"))
    placed = (
        P("y", DP, None),
        P(DP, None),
        P("y", DP, None),
        P("y", DP, None),
        P("y", None, None),
        P("y", None, None),
        P("y", None, None),
        P("y", None, None),
        P(DP),
        P(),
    )
    return jax.shard_map(
        body, mesh=grid, in_specs=placed, out_specs=P("y", None, DP, None), check_vma=False
    )
```

time: 156 us -> 173 us (1.11)
  waiting for transfers between devices: 22.5 us -> 45 us
  blocking collectives: 66.7 us -> 49.6 us
  local copies, waits for them, and re-layouts: 3.64 us -> 13.4 us
  matrix products: 17.8 us -> 11 us
  starting transfers between devices: 22.4 us -> 28.8 us
  Pallas kernels: 0 us -> 3.59 us
    all_to_all x2 -> x1, blocking collectives: 40.9 us -> 23.4 us  [body(): parts = lax.all_to_all(doc_sums(left, right, slots, core, rank), XZ, 0, 0)]
    all_to_all x0 -> x1, waiting for transfers between devices: none -> 12.9 us  [grams(): every = lax.all_to_all(jnp.broadcast_to(total[None], shape), XZ, 0, 0)]
    ppermute x5 -> x13, waiting for transfers between devices: 1.18 us -> 12.4 us  [the longest x3 9.31 us: gather(): lax.ppermute(shard, 'x', [(i, (i - k) % count) for i in range(count)])]
    unnamed x16 -> x28, local copies, waits for them, and re-layouts: 1.33 us -> 10 us
    dot_general x16 -> x15, matrix products: 17.8 us -> 11 us  [dot(): lax.dot_general(left, right, (((left_dim,), (0,)), ((), ())), preferred_e...]
    ppermute x5 -> x13, starting transfers between devices: 1.51 us -> 7.04 us  [the longest x3 4.52 us: gather(): lax.ppermute(shard, 'x', [(i, (i - k) % count) for i in range(count)])]
    all_to_all x0 -> x1, starting transfers between devices: none -> 5.26 us  [grams(): every = lax.all_to_all(jnp.broadcast_to(total[None], shape), XZ, 0, 0)]
    ppermute x10, starting transfers between devices: 20.9 us -> 16.5 us  [send(): return lax.ppermute(value, 'y', pairs)]
  transfers between devices with their start and end apart: 16 -> 25, of which waited for: 6 -> 14; matrix products, arithmetic and copies ran while one was open for 9% -> 9% of each run, Pallas kernels for 0% -> 2%
where the time goes in v3:
time: 173 us; the launch traced here: 172 us
  blocking collectives  49.6 us (29%)
  waiting for transfers between devices  45 us (26%)
  starting transfers between devices  28.8 us (17%)
  between operations  14 us (8%)
  local copies, waits for them, and re-layouts  13.4 us (8%)
  matrix products  11 us (6%)
  other arithmetic  6.86 us (4%)
  Pallas kernels  3.59 us (2%)
    all_to_all x1, blocking collectives, grams(): slices = lax.all_to_all(parts.reshape(shape), XZ, 0, 0)  26.2 us
    all_to_all x1, blocking collectives, body(): parts = lax.all_to_all(doc_sums(left, right, slots, core, rank), XZ, 0, 0)  23.4 us
    ppermute x10, waiting for transfers between devices, send(): return lax.ppermute(value, 'y', pairs)  19.7 us
    ppermute x10, starting transfers between devices, send(): return lax.ppermute(value, 'y', pairs)  16.5 us
    all_to_all x1, waiting for transfers between devices, grams(): every = lax.all_to_all(jnp.broadcast_to(total[None], shape), XZ, 0, 0)  12.9 us
    dot_general x15, matrix products, dot(): lax.dot_general(left, right, (((left_dim,), (0,)), ((), ())), preferred_e...  11 us
    unnamed x28, local copies, waits for them, and re-layouts  10 us
    ppermute x3, waiting for transfers between devices, gather(): lax.ppermute(shard, 'x', [(i, (i - k) % count) for i in range(count)])  9.31 us
  transfers between devices with their start and end apart: 25, of which 14 were waited for; matrix products, arithmetic and copies ran while one was open for 9% of the time, Pallas kernels for 2%

profile of v3, /device:TPU:32, one launch (start us, length us, event | category | flops | bytes accessed | tf_op | source)
XLA Modules:
  0.0 172.2 jit_solution(12754763881244911408)
XLA Ops:
  6.5 1.0 constant_dynamic-slice_fusion.4
  7.6 1.1 convolution_convert_fusion.2
  8.9 1.1 collective-permute-done.10
  10.3 2.8 %collective-permute-start.13 = (bf16[320,256]{1,0:T(8,128)(2,1)S(1)}, bf16[320,256]{1,0:T(8,128)(2,1)S(1)}, u32[]{:S(2)}, u32[]{:S(2)}) collective-permute-start(bf16[320,256]{1,0:T(8,128)(2,1)S(1)} %pad_maximum_fusion.4), channel_id=1, source_target_pairs={{0,48},{16,0},{32,16},{48,32},{1,49},{17,1},{33,17},{49,33},{2,50}... | collective-permute-start | bytes 491528 | tf_op jit(solution)/shard_map/ppermute | solution.py:48
  13.2 0.8 collective-permute-start.12
  14.0 0.9 collective-permute-start.11
  14.9 5.6 %collective-permute-done.13 = bf16[320,256]{1,0:T(8,128)(2,1)S(1)} collective-permute-done((bf16[320,256]{1,0:T(8,128)(2,1)S(1)}, bf16[320,256]{1,0:T(8,128)(2,1)S(1)}, u32[]{:S(2)}, u32[]{:S(2)}) %collective-permute-start.13) | collective-permute-done | bytes 163872 | tf_op jit(solution)/shard_map/ppermute | solution.py:48
  20.5 1.3 collective-permute-done.12
  21.8 2.4 %collective-permute-done.11 = bf16[320,256]{1,0:T(8,128)(2,1)S(1)} collective-permute-done((bf16[320,256]{1,0:T(8,128)(2,1)S(1)}, bf16[320,256]{1,0:T(8,128)(2,1)S(1)}, u32[]{:S(2)}, u32[]{:S(2)}) %collective-permute-start.11) | collective-permute-done | bytes 163872 | tf_op jit(solution)/shard_map/ppermute | solution.py:48
  24.4 0.9 pad_maximum_fusion
  26.1 1.3 collective-permute-start.2
  28.0 4.1 %collective-permute-start.6 = (bf16[128,640]{1,0:T(8,128)(2,1)S(1)}, bf16[128,640]{1,0:T(8,128)(2,1)S(1)}, u32[]{:S(2)}, u32[]{:S(2)}) collective-permute-start(bf16[128,640]{1,0:T(8,128)(2,1)S(1)} %pad_maximum_fusion.3), channel_id=1, source_target_pairs={{0,64},{64,128},{128,192},{1,65},{65,129},{129,193},{2,66},{66,130... | collective-permute-start | bytes 491528 | tf_op jit(solution)/shard_map/ppermute | solution.py:22
  32.1 1.3 collective-permute-start.5
  33.4 2.9 %collective-permute-done.2 = bf16[128,512]{1,0:T(8,128)(2,1)S(1)} collective-permute-done((bf16[128,512]{1,0:T(8,128)(2,1)S(1)}, bf16[128,512]{1,0:T(8,128)(2,1)S(1)}, u32[]{:S(2)}, u32[]{:S(2)}) %collective-permute-start.2) | collective-permute-done | bytes 131104 | tf_op jit(solution)/shard_map/ppermute | solution.py:22
  36.4 3.4 %collective-permute-done.5 = bf16[128,640]{1,0:T(8,128)(2,1)S(1)} collective-permute-done((bf16[128,640]{1,0:T(8,128)(2,1)S(1)}, bf16[128,640]{1,0:T(8,128)(2,1)S(1)}, u32[]{:S(2)}, u32[]{:S(2)}) %collective-permute-start.5) | collective-permute-done | bytes 163872 | tf_op jit(solution)/shard_map/ppermute | solution.py:22
  40.6 0.8 collective-permute-done.7
  42.7 26.2 %all_to_all.15 = bf16[32,8,640]{2,1,0:T(8,128)(2,1)S(1)} all-to-all(bf16[32,8,640]{2,1,0:T(8,128)(2,1)S(1)} %bitcast.71), channel_id=1, replica_groups=mesh['y'=4,'x'=4,'z'=8,'c'=2] {'x','z'}, dimensions={0} | all-to-all | bytes 655360 | tf_op jit(solution)/shard_map/all_to_all | solution.py:131
  68.9 0.8 broadcast_in_dim.44
  69.7 5.3 %all-to-all-start.1 = ((bf16[32,8,640]{2,1,0:T(8,128)(2,1)}), bf16[32,8,640]{2,1,0:T(8,128)(2,1)S(1)}, u32[]{:S(2)}, u32[]{:S(2)}) async-start(bf16[32,8,640]{2,1,0:T(8,128)(2,1)} %broadcast_in_dim.44), calls=%async_computation.1 | async-start | bytes 655360 | tf_op jit(solution)/shard_map/all_to_all | solution.py:133
  75.2 3.2 %convolution_convert_fusion.1 = bf16[128,64]{1,0:T(8,128)(2,1)} fusion(bf16[1,8192,64]{1,2,0:T(8,128)(2,1)} %param.14, bf16[1,128,8192]{2,1,0:T(8,128)(2,1)} %param.10), kind=kOutput, calls=%fused_computation.6 | convolution fusion | flops 134225920 | bytes 3162112 | tf_op jit(solution)/shard_map/dot_general | solution.py:16
  78.8 12.9 %all-to-all-done.1 = bf16[32,8,640]{2,1,0:T(8,128)(2,1)S(1)} async-done(((bf16[32,8,640]{2,1,0:T(8,128)(2,1)}), bf16[32,8,640]{2,1,0:T(8,128)(2,1)S(1)}, u32[]{:S(2)}, u32[]{:S(2)}) %all-to-all-start.1) | async-done | bytes 327712 | tf_op jit(solution)/shard_map/all_to_all | solution.py:133
  91.8 1.4 collective-permute-start.15
  93.2 1.5 fusion.5
  95.8 3.2 %collective-permute-start.17 = (bf16[256,640]{1,0:T(8,128)(2,1)S(1)}, bf16[256,640]{1,0:T(8,128)(2,1)S(1)}, u32[]{:S(2)}, u32[]{:S(2)}) collective-permute-start(bf16[256,640]{1,0:T(8,128)(2,1)S(1)} %bitcast.63), channel_id=1, source_target_pairs={{0,192},{1,193},{2,194},{3,195},{4,196},{5,197},{6,198},{7,199},{8... | collective-permute-start | bytes 983048 | tf_op jit(solution)/shard_map/ppermute | solution.py:22
  99.7 1.0 broadcast_select_fusion
  100.7 1.0 fusion.21
  102.5 0.7 collective-permute-done.16
  103.9 6.5 %collective-permute-done.17 = bf16[256,640]{1,0:T(8,128)(2,1)S(1)} collective-permute-done((bf16[256,640]{1,0:T(8,128)(2,1)S(1)}, bf16[256,640]{1,0:T(8,128)(2,1)S(1)}, u32[]{:S(2)}, u32[]{:S(2)}) %collective-permute-start.17) | collective-permute-done | bytes 327712 | tf_op jit(solution)/shard_map/ppermute | solution.py:22
  110.4 0.8 fusion.46
  111.5 0.9 fusion.44
  112.3 1.3 copy-done.4
  113.7 1.4 copy-done.6
  115.0 1.6 copy-done.2
  116.6 2.5 %copy-done.3 = bf16[32,320,256]{2,1,0:T(8,128)(2,1)S(1)} copy-done((bf16[32,320,256]{2,1,0:T(8,128)(2,1)S(1)}, bf16[32,320,256]{2,1,0:T(8,128)(2,1)}, u32[]{:S(2)}) %copy-start.3) | copy-done | bytes 5242904
  119.1 1.6 copy-done.5
  120.7 1.6 copy-done.7
  122.3 3.6 %shard_map.100 = (bf16[256,256]{1,0:T(8,128)(2,1)S(1)}, bf16[256,64]{1,0:T(8,128)(2,1)S(1)}) custom-call(bf16[128,8192]{1,0:T(8,128)(2,1)S(1)} %copy-done.1, bf16[128,8192]{1,0:T(8,128)(2,1)S(1)} %copy-done.5, bf16[128,8192]{1,0:T(8,128)(2,1)S(1)} %bitcast.60, bf16[128,8192]{1,0:T(8,128)(2,1)S(1)} %copy-done.7, bf16[32,320,256]{2,1,0:T(8,128)(2,1)S(1)} %copy-done.3), custom_call_target="tpu_custom_call" | custom-call | flops 1342177280 | bytes 5242880 | tf_op jit(solution)/shard_map/pallas_call | solution.py:91
  125.9 1.1 convolution_convert_fusion
  127.1 1.3 collective-permute-start.19
  128.4 1.3 collective-permute-start.21
  129.7 1.3 collective-permute-start.20
  131.1 2.1 %collective-permute-done.19 = bf16[256,128]{0,1:T(8,128)(2,1)S(1)} collective-permute-done((bf16[256,128]{0,1:T(8,128)(2,1)S(1)}, bf16[256,128]{0,1:T(8,128)(2,1)S(1)}, u32[]{:S(2)}, u32[]{:S(2)}) %collective-permute-start.19) | collective-permute-done | bytes 65568 | tf_op jit(solution)/shard_map/ppermute | solution.py:22
  133.2 4.7 %collective-permute-done.21 = bf16[256,128]{0,1:T(8,128)(2,1)S(1)} collective-permute-done((bf16[256,128]{0,1:T(8,128)(2,1)S(1)}, bf16[256,128]{0,1:T(8,128)(2,1)S(1)}, u32[]{:S(2)}, u32[]{:S(2)}) %collective-permute-start.21) | collective-permute-done | bytes 65568 | tf_op jit(solution)/shard_map/ppermute | solution.py:22
  138.0 0.8 fusion.32
  139.1 0.9 pad_maximum_fusion.12
  140.3 0.7 fusion
  141.0 23.4 %all_to_all.16 = bf16[32,64,128]{2,1,0:T(8,128)(2,1)S(1)} all-to-all(bf16[32,64,128]{2,1,0:T(8,128)(2,1)S(1)} %fusion.4), channel_id=1, replica_groups=mesh['y'=4,'x'=4,'z'=8,'c'=2] {'x','z'}, dimensions={0} | all-to-all | bytes 1048576 | tf_op jit(solution)/shard_map/all_to_all | solution.py:211
  164.6 0.7 reshape.65
  (102 shorter events, 9.3 us)
Async XLA Ops:
  6.5 21.0 %copy-start = (bf16[1,8192,64]{1,2,0:T(8,128)(2,1)S(1)}, bf16[1,8192,64]{1,2,0:T(8,128)(2,1)}, u32[]{:S(2)}) copy-start(bf16[1,8192,64]{1,2,0:T(8,128)(2,1)} %param.17) | copy-start | bytes 3145732
  6.5 108.5 %all-gather.2.cloned.1.call-start = ((), (), s32[]{:S(2)}) async-start(), calls=%async_computation.3 | async-start | bytes 5898240 | tf_op jit(solution)/shard_map/all_gather | solution.py:58
  8.7 1.4 collective-permute-start.10
  10.3 15.1 %copy-start.9 = (bf16[1,128,512]{2,1,0:T(8,128)(2,1)S(1)}, bf16[1,128,512]{2,1,0:T(8,128)(2,1)}, u32[]{:S(2)}) copy-start(bf16[1,128,512]{2,1,0:T(8,128)(2,1)} %param.12) | copy-start | bytes 393220
  10.3 17.1 %copy-start.8 = (bf16[1,128,512]{2,1,0:T(8,128)(2,1)S(1)}, bf16[1,128,512]{2,1,0:T(8,128)(2,1)}, u32[]{:S(2)}) copy-start(bf16[1,128,512]{2,1,0:T(8,128)(2,1)} %param.13) | copy-start | bytes 393220
  10.3 17.1 %copy-start.10 = (bf16[1,512,64]{1,2,0:T(8,128)(2,1)S(1)}, bf16[1,512,64]{1,2,0:T(8,128)(2,1)}, u32[]{:S(2)}) copy-start(bf16[1,512,64]{1,2,0:T(8,128)(2,1)} %param.15) | copy-start | bytes 196612
  10.3 10.2 %collective-permute-start.13 = (bf16[320,256]{1,0:T(8,128)(2,1)S(1)}, bf16[320,256]{1,0:T(8,128)(2,1)S(1)}, u32[]{:S(2)}, u32[]{:S(2)}) collective-permute-start(bf16[320,256]{1,0:T(8,128)(2,1)S(1)} %pad_maximum_fusion.4), channel_id=1, source_target_pairs={{0,48},{16,0},{32,16},{48,32},{1,49},{17,1},{33,17},{49,33},{2,50}... | collective-permute-start | bytes 491528 | tf_op jit(solution)/shard_map/ppermute | solution.py:48
  13.2 8.6 %collective-permute-start.12 = (bf16[320,256]{1,0:T(8,128)(2,1)S(1)}, bf16[320,256]{1,0:T(8,128)(2,1)S(1)}, u32[]{:S(2)}, u32[]{:S(2)}) collective-permute-start(bf16[320,256]{1,0:T(8,128)(2,1)S(1)} %pad_maximum_fusion.4), channel_id=1, source_target_pairs={{0,32},{16,48},{32,0},{48,16},{1,33},{17,49},{33,1},{49,17},{2,34}... | collective-permute-start | bytes 491528 | tf_op jit(solution)/shard_map/ppermute | solution.py:48
  14.0 10.2 %collective-permute-start.11 = (bf16[320,256]{1,0:T(8,128)(2,1)S(1)}, bf16[320,256]{1,0:T(8,128)(2,1)S(1)}, u32[]{:S(2)}, u32[]{:S(2)}) collective-permute-start(bf16[320,256]{1,0:T(8,128)(2,1)S(1)} %pad_maximum_fusion.4), channel_id=1, source_target_pairs={{0,16},{16,32},{32,48},{48,0},{1,17},{17,33},{33,49},{49,1},{2,18}... | collective-permute-start | bytes 491528 | tf_op jit(solution)/shard_map/ppermute | solution.py:48
  25.4 10.9 %collective-permute-start.3 = (bf16[128,512]{1,0:T(8,128)(2,1)S(1)}, bf16[128,512]{1,0:T(8,128)(2,1)S(1)}, u32[]{:S(2)}, u32[]{:S(2)}) collective-permute-start(bf16[128,512]{1,0:T(8,128)(2,1)S(1)} %bitcast.69), channel_id=1, source_target_pairs={{192,64},{193,65},{194,66},{195,67},{196,68},{197,69},{198,70},{19... | collective-permute-start | bytes 393224 | tf_op jit(solution)/shard_map/ppermute | solution.py:22
  26.1 10.2 %collective-permute-start.2 = (bf16[128,512]{1,0:T(8,128)(2,1)S(1)}, bf16[128,512]{1,0:T(8,128)(2,1)S(1)}, u32[]{:S(2)}, u32[]{:S(2)}) collective-permute-start(bf16[128,512]{1,0:T(8,128)(2,1)S(1)} %bitcast.70), channel_id=1, source_target_pairs={{192,0},{128,64},{193,1},{129,65},{194,2},{130,66},{195,3},{131,67... | collective-permute-start | bytes 393224 | tf_op jit(solution)/shard_map/ppermute | solution.py:22
  28.0 8.4 %collective-permute-start.6 = (bf16[128,640]{1,0:T(8,128)(2,1)S(1)}, bf16[128,640]{1,0:T(8,128)(2,1)S(1)}, u32[]{:S(2)}, u32[]{:S(2)}) collective-permute-start(bf16[128,640]{1,0:T(8,128)(2,1)S(1)} %pad_maximum_fusion.3), channel_id=1, source_target_pairs={{0,64},{64,128},{128,192},{1,65},{65,129},{129,193},{2,66},{66,130... | collective-permute-start | bytes 491528 | tf_op jit(solution)/shard_map/ppermute | solution.py:22
  32.1 7.7 %collective-permute-start.5 = (bf16[128,640]{1,0:T(8,128)(2,1)S(1)}, bf16[128,640]{1,0:T(8,128)(2,1)S(1)}, u32[]{:S(2)}, u32[]{:S(2)}) collective-permute-start(bf16[128,640]{1,0:T(8,128)(2,1)S(1)} %pad_maximum_fusion.3), channel_id=1, source_target_pairs={{64,0},{65,1},{66,2},{67,3},{68,4},{69,5},{70,6},{71,7},{72,8},{73... | collective-permute-start | bytes 491528 | tf_op jit(solution)/shard_map/ppermute | solution.py:22
  39.8 1.5 collective-permute-start.7
  40.0 1.6 collective-permute-start.4
  42.3 32.6 %copy-start.11 = (s32[64]{0:T(128)S(1)}, s32[64]{0:T(128)}, u32[]{:S(2)}) copy-start(s32[64]{0:T(128)} %param.19) | copy-start | bytes 772
  42.4 32.6 %copy-start.12 = (s32[128]{0:T(128)S(1)}, s32[128]{0:T(128)}, u32[]{:S(2)}) copy-start(s32[128]{0:T(128)} %param.18) | copy-start | bytes 1540
  68.9 24.3 %copy-start.1 = (bf16[128,8192]{1,0:T(8,128)(2,1)S(1)}, bf16[128,8192]{1,0:T(8,128)(2,1)}, u32[]{:S(2)}) copy-start(bf16[128,8192]{1,0:T(8,128)(2,1)} %refs_0_.1) | copy-start | bytes 6291460
  69.7 22.1 %all-to-all-start.1 = ((bf16[32,8,640]{2,1,0:T(8,128)(2,1)}), bf16[32,8,640]{2,1,0:T(8,128)(2,1)S(1)}, u32[]{:S(2)}, u32[]{:S(2)}) async-start(bf16[32,8,640]{2,1,0:T(8,128)(2,1)} %broadcast_in_dim.44), calls=%async_computation.1 | async-start | bytes 655360 | tf_op jit(solution)/shard_map/all_to_all | solution.py:133
  75.1 19.6 %collective-permute-start = (s32[128]{0:T(128)S(1)}, s32[128]{0:T(128)}, u32[]{:S(2)}, u32[]{:S(2)}) collective-permute-start(s32[128]{0:T(128)S(1)} %select_reduce_fusion), channel_id=1, source_target_pairs={{0,1},{1,0},{2,3},{3,2},{4,5},{5,4},{6,7},{7,6},{8,9},{9,8},{10,11... | collective-permute-start | bytes 1544 | tf_op jit(solution)/shard_map/ppermute | solution.py:26
  78.3 60.7 %collective-permute-start.1 = (bf16[128,64]{1,0:T(8,128)(2,1)}, bf16[128,64]{1,0:T(8,128)(2,1)}, u32[]{:S(2)}, u32[]{:S(2)}) collective-permute-start(bf16[128,64]{1,0:T(8,128)(2,1)} %convolution_convert_fusion.1), channel_id=1, source_target_pairs={{0,1},{1,0},{2,3},{3,2},{4,5},{5,4},{6,7},{7,6},{8,9},{9,8},{10,11... | collective-permute-start | bytes 49160 | tf_op jit(solution)/shard_map/ppermute | solution.py:26
  91.8 7.2 %collective-permute-start.15 = (bf16[256,640]{1,0:T(8,128)(2,1)S(1)}, bf16[256,640]{1,0:T(8,128)(2,1)}, u32[]{:S(2)}, u32[]{:S(2)}) collective-permute-start(bf16[256,640]{1,0:T(8,128)(2,1)S(1)} %bitcast.61), channel_id=1, source_target_pairs={{64,128},{128,192},{65,129},{129,193},{66,130},{130,194},{67,131},... | collective-permute-start | bytes 983048 | tf_op jit(solution)/shard_map/ppermute | solution.py:22
  95.3 17.1 %collective-permute-start.8 = (bf16[128,8192]{1,0:T(8,128)(2,1)S(1)}, bf16[128,8192]{1,0:T(8,128)(2,1)S(1)}, u32[]{:S(2)}, u32[]{:S(2)}) collective-permute-start(bf16[128,8192]{1,0:T(8,128)(2,1)S(1)} %copy-done.1), channel_id=1, source_target_pairs={{0,1},{1,0},{2,3},{3,2},{4,5},{5,4},{6,7},{7,6},{8,9},{9,8},{10,11... | collective-permute-start | bytes 6291464 | tf_op jit(solution)/shard_map/ppermute | solution.py:26
  95.3 18.4 %collective-permute-start.9 = (bf16[128,8192]{1,0:T(8,128)(2,1)}, bf16[128,8192]{1,0:T(8,128)(2,1)S(1)}, u32[]{:S(2)}, u32[]{:S(2)}) collective-permute-start(bf16[128,8192]{1,0:T(8,128)(2,1)} %bitcast.59), channel_id=1, source_target_pairs={{0,1},{1,0},{2,3},{3,2},{4,5},{5,4},{6,7},{7,6},{8,9},{9,8},{10,11... | collective-permute-start | bytes 6291464 | tf_op jit(solution)/shard_map/ppermute | solution.py:26
  95.8 14.6 %collective-permute-start.17 = (bf16[256,640]{1,0:T(8,128)(2,1)S(1)}, bf16[256,640]{1,0:T(8,128)(2,1)S(1)}, u32[]{:S(2)}, u32[]{:S(2)}) collective-permute-start(bf16[256,640]{1,0:T(8,128)(2,1)S(1)} %bitcast.63), channel_id=1, source_target_pairs={{0,192},{1,193},{2,194},{3,195},{4,196},{5,197},{6,198},{7,199},{8... | collective-permute-start | bytes 983048 | tf_op jit(solution)/shard_map/ppermute | solution.py:22
  99.0 1.7 collective-permute-start.14
  101.8 1.4 collective-permute-start.16
  103.5 8.0 %collective-permute-start.18 = (bf16[256,128]{1,0:T(8,128)(2,1)S(1)}, bf16[256,128]{1,0:T(8,128)(2,1)S(1)}, u32[]{:S(2)}, u32[]{:S(2)}) collective-permute-start(bf16[256,128]{1,0:T(8,128)(2,1)S(1)} %add_convert_fusion.3), channel_id=1, source_target_pairs={{0,1},{1,0},{2,3},{3,2},{4,5},{5,4},{6,7},{7,6},{8,9},{9,8},{10,11... | collective-permute-start | bytes 196616 | tf_op jit(solution)/shard_map/ppermute | solution.py:26
  112.3 1.3 copy-start.4
  113.7 1.4 copy-start.6
  115.0 1.6 copy-start.2
  116.6 2.5 %copy-start.3 = (bf16[32,320,256]{2,1,0:T(8,128)(2,1)S(1)}, bf16[32,320,256]{2,1,0:T(8,128)(2,1)}, u32[]{:S(2)}) copy-start(bf16[32,320,256]{2,1,0:T(8,128)(2,1)} %all-gather.2.cloned.1.call-done.refs_4_) | copy-start | bytes 15728644
  119.1 1.6 copy-start.5
  120.7 1.6 copy-start.7
  122.3 3.6 %copy-start.13 = (bf16[256,128]{1,0:T(8,128)(2,1)S(1)}, bf16[256,128]{1,0:T(8,128)(2,1)}, u32[]{:S(2)}) copy-start(bf16[256,128]{1,0:T(8,128)(2,1)} %fusion.44) | copy-start | bytes 196612
  127.1 6.2 %collective-permute-start.19 = (bf16[256,128]{0,1:T(8,128)(2,1)S(1)}, bf16[256,128]{0,1:T(8,128)(2,1)S(1)}, u32[]{:S(2)}, u32[]{:S(2)}) collective-permute-start(bf16[256,128]{0,1:T(8,128)(2,1)S(1)} %get-tuple-element.20), channel_id=1, source_target_pairs={{64,0},{128,64},{192,128},{65,1},{129,65},{193,129},{66,2},{130,66... | collective-permute-start | bytes 196616 | tf_op jit(solution)/shard_map/ppermute | solution.py:22
  128.4 9.6 %collective-permute-start.21 = (bf16[256,128]{0,1:T(8,128)(2,1)S(1)}, bf16[256,128]{0,1:T(8,128)(2,1)S(1)}, u32[]{:S(2)}, u32[]{:S(2)}) collective-permute-start(bf16[256,128]{0,1:T(8,128)(2,1)S(1)} %get-tuple-element.21), channel_id=1, source_target_pairs={{192,0},{193,1},{194,2},{195,3},{196,4},{197,5},{198,6},{199,7},{2... | collective-permute-start | bytes 196616 | tf_op jit(solution)/shard_map/ppermute | solution.py:22
  129.7 8.3 %collective-permute-start.20 = (bf16[256,128]{0,1:T(8,128)(2,1)S(1)}, bf16[256,128]{0,1:T(8,128)(2,1)S(1)}, u32[]{:S(2)}, u32[]{:S(2)}) collective-permute-start(bf16[256,128]{0,1:T(8,128)(2,1)S(1)} %get-tuple-element.22), channel_id=1, source_target_pairs={{128,0},{192,64},{129,1},{193,65},{130,2},{194,66},{131,3},{195,67... | collective-permute-start | bytes 196616 | tf_op jit(solution)/shard_map/ppermute | solution.py:22
  138.8 1.4 collective-permute-start.22
Sparse Core Ops, SparseCore 0:
  25.5 77.2 all-gather.1

commit v4 on v2

v4 whole, which is shorter than its diff:
```python
import jax
import jax.numpy as jnp
from jax import lax
from jax.sharding import Mesh, PartitionSpec as P

XZ = ("x", "z")
DP = ("x", "z", "c")
SWAP = [(0, 1), (1, 0)]
BF16 = jnp.bfloat16
F32 = jnp.float32


def dot(left, right, left_dim=1):
    return lax.dot_general(
        left, right, (((left_dim,), (0,)), ((), ())), preferred_element_type=F32
    )


def send(value, pairs):
    return lax.ppermute(value, "y", pairs)


def swap(value):
    return lax.ppermute(value, "c", SWAP)


def half_of(value, core, axis=1):
    width = value.shape[axis] // 2
    return lax.dynamic_slice_in_dim(value, core * width, width, axis)


def ordered(mine, core):
    got = swap(mine)
    return jnp.concatenate([jnp.where(core == 0, mine, got), jnp.where(core == 0, got, mine)])


def from_above(value, steps):
    count = lax.axis_size("y")
    return send(value, [(i, i - steps) for i in range(steps, count)])


def along_x(items):
    count = lax.axis_size("x")
    moved = [
        lax.ppermute(items[k], "x", [(i, (i + k) % count) for i in range(count)])
        for k in range(1, count)
    ]
    return jnp.concatenate([items[0]] + moved, axis=0)


def both_cores(value):
    return jnp.concatenate([value, swap(value)], axis=0)


def grams(wv, right, plane, core):
    kv, columns = wv.shape[1], right.shape[1]
    width = kv // 2
    near, far = send(wv, [(2, 0), (3, 1), (1, 2)]), send(wv, [(3, 2)])
    close, wide = send(right, [(1, 0), (2, 1), (0, 2)]), send(right, [(1, 3)])
    right = jnp.where(plane == 3, wide, close)
    lefts = [jnp.where(plane == 3, wv, near), wv, far]
    got = swap(jnp.concatenate([half_of(item, 1 - core) for item in lefts], axis=1))
    mine = jnp.concatenate([half_of(item, core) for item in lefts], axis=1)
    left = jnp.concatenate([mine, got], axis=0)
    rows = both_cores(right)
    main = dot(left[:, :width], rows, 0)
    own = [dot(left[:, k * width : (k + 1) * width], rows[:, kv:], 0) for k in range(3)]
    own = jnp.concatenate(own + [jnp.zeros((width, columns - 3 * (columns - kv)), F32)], axis=1)
    parts = jnp.where(plane == 2, own, main).astype(BF16)
    ranks = lax.axis_size(XZ)
    shape = (ranks, width // ranks, columns)
    slices = lax.all_to_all(parts.reshape(shape), XZ, 0, 0)
    total = jnp.sum(slices.astype(F32), axis=0).astype(BF16)
    every = lax.all_to_all(jnp.broadcast_to(total[None], shape), XZ, 0, 0)
    return every.reshape(width, columns)


def solve(half, plane, core, kv):
    block = half.shape[1] - kv
    first = send(half[:, : 3 * block], [(2, 0)])
    near = send(half[:, kv:], [(0, 1), (1, 2)])
    far = send(half[:, kv:], [(3, 1)])
    g31 = send(half[:, :kv], [(3, 0)])
    g32 = send(half[:, :kv], [(1, 0)])
    one = ordered(jnp.where(plane == 0, first[:, :block], near), core)
    two = jnp.where(plane == 0, first[:, block : 2 * block], far).astype(F32)
    two = ordered((two + dot(half[:, :kv], one)).astype(BF16), core)
    three = first[:, 2 * block :].astype(F32) + dot(g31, one) + dot(g32, two)
    return one, two, ordered(three.astype(BF16), core)


def full_rows(own, core):
    count = lax.axis_size("z")
    mine = lax.all_to_all(jnp.broadcast_to(own[None], (count, *own.shape)), "z", 0, 0)
    got = swap(mine)
    both = jnp.stack([jnp.where(core == 0, mine, got), jnp.where(core == 0, got, mine)], axis=1)
    return both.reshape(-1, own.shape[1])


def doc_sums(left, right, slots, core, rank):
    owners = lax.axis_size(XZ)
    named = 2 * jnp.arange(owners, dtype=jnp.int32) + core
    onehot = (slots[:, None] == named[None, :]).astype(BF16)
    spread = (onehot[:, :, None] * left[:, None, :]).reshape(left.shape[0], owners * 2 * rank)
    table = dot(spread, right, 0).reshape(owners, 2 * rank, 2 * rank)
    lane = lax.broadcasted_iota(jnp.int32, (1, rank, 2 * rank), 2)
    return jnp.where(lane < rank, table[:, :rank], table[:, rank:]).astype(BF16)


def body(
    hidden, cotangent, w_value, w_out_t, p_in, p_value_out, p_value_in, p_out, segments, owner_slot
):
    plane, core = lax.axis_index("y"), lax.axis_index("c")
    device = lax.axis_index(DP)
    wv, wo, acts = w_value[0], w_out_t[0], hidden[0]
    rows, kv = wv.shape
    rank = p_in.shape[2]
    documents = owner_slot.shape[0]

    projected = dot(wv, p_value_in[0]).astype(BF16)
    projected = lax.all_gather(projected, DP, axis=0, tiled=True)

    out_rows = lax.dynamic_slice_in_dim(p_out[0], device * rows, rows, 0)
    ends = jnp.concatenate([dot(wo, p_value_out[0]).astype(BF16), out_rows], axis=1)
    half = grams(wv, jnp.concatenate([wo, ends], axis=1), plane, core)

    places, place = lax.axis_size("x"), lax.axis_index("x")
    quarter = cotangent.shape[1] // places
    items = [
        lax.dynamic_slice_in_dim(cotangent, ((place + k) % places) * quarter, quarter, 1)
        for k in range(places)
    ]
    cot = along_x(items)
    cot_got = swap(cot)
    match = segments[:, None] == jnp.arange(documents, dtype=jnp.int32)[None, :]
    slots = jnp.sum(jnp.where(match, owner_slot[None, :], 0), axis=1)
    known = [dot(acts, p_in[0]), dot(acts, projected), slots.astype(F32)[:, None]]
    known = along_x([jnp.concatenate(known, axis=1).astype(BF16)] * places)
    known = both_cores(known)
    left, slots = known[:, : 2 * rank], known[:, 2 * rank].astype(jnp.int32)

    spread = solve(half, plane, core, kv)
    own = ends.astype(F32)
    for k in range(3):
        own = own + dot(from_above(wo, k + 1), spread[k])
    table = full_rows(own.astype(BF16), core)
    right = jnp.concatenate([dot(cot, table), dot(cot_got, table)], axis=0).astype(BF16)
    parts = lax.all_to_all(doc_sums(left, right, slots, core, rank), XZ, 0, 0)
    total = jnp.sum(parts.astype(F32), axis=0)
    tables = total.reshape(rank, 2, rank).transpose(1, 0, 2)
    return tables.reshape(1, 2, 1, rank * rank)


def solution(mesh):
    grid = Mesh(mesh.devices.reshape(4, 4, 8, 2), ("y", "x", "z", "c"))
    placed = (
        P("y", DP, None),
        P(DP, None),
        P("y", DP, None),
        P("y", DP, None),
        P("y", None, None),
        P("y", None, None),
        P("y", None, None),
        P("y", None, None),
        P(DP),
        P(),
    )
    return jax.shard_map(
        body, mesh=grid, in_specs=placed, out_specs=P("y", None, DP, None), check_vma=False
    )
```

time: 156 us -> 191 us (1.22)
  waiting for transfers between devices: 22.5 us -> 71.1 us
  blocking collectives: 66.7 us -> 22.4 us
  starting transfers between devices: 22.4 us -> 53.4 us
  local copies, waits for them, and re-layouts: 3.64 us -> 7.34 us
  other arithmetic: 7.72 us -> 5.52 us
    all_to_all x3 -> x1, blocking collectives: 66.7 us -> 22.4 us  [body(): parts = lax.all_to_all(doc_sums(left, right, slots, core, rank), XZ, 0, 0)]
    all_to_all x0 -> x3, waiting for transfers between devices: none -> 26.9 us  [the longest x1 13.7 us: grams(): every = lax.all_to_all(jnp.broadcast_to(total[None], shape), XZ, 0, 0)]
    all_to_all x0 -> x3, starting transfers between devices: none -> 21.6 us  [the longest x1 11.2 us: grams(): slices = lax.all_to_all(parts.reshape(shape), XZ, 0, 0)]
    all_gather x1, waiting for transfers between devices: 0.02 us -> 12.7 us  [body(): projected = lax.all_gather(projected, DP, axis=0, tiled=True)]
    ppermute x5 -> x14, starting transfers between devices: 1.51 us -> 12.4 us  [the longest x6 11.3 us: along_x(): lax.ppermute(items[k], 'x', [(i, (i + k) % count) for i in range(count)])]
    ppermute x5 -> x14, waiting for transfers between devices: 1.18 us -> 7.1 us  [the longest x8 7.09 us: swap(): return lax.ppermute(value, 'c', SWAP)]
    ppermute x10 -> x12, waiting for transfers between devices: 21.3 us -> 24.5 us  [send(): return lax.ppermute(value, 'y', pairs)]
    dynamic_slice x2 -> x4, local copies, waits for them, and re-layouts: 0.91 us -> 3.78 us  [the longest x1 2.85 us: body(): lax.dynamic_slice_in_dim(cotangent, (place + k) % places * quarter, quart...]
  transfers between devices with their start and end apart: 16 -> 30, of which waited for: 6 -> 15; matrix products, arithmetic and copies ran while one was open for 9% -> 11% of each run, Pallas kernels for 0% -> 0%
where the time goes in v4:
time: 191 us; the launch traced here: 190 us
  waiting for transfers between devices  71.1 us (37%)
  starting transfers between devices  53.4 us (28%)
  blocking collectives  22.4 us (12%)
  matrix products  15.9 us (8%)
  between operations  14.1 us (7%)
  local copies, waits for them, and re-layouts  7.34 us (4%)
  other arithmetic  5.52 us (3%)
    ppermute x12, waiting for transfers between devices, send(): return lax.ppermute(value, 'y', pairs)  24.5 us
    all_to_all x1, blocking collectives, body(): parts = lax.all_to_all(doc_sums(left, right, slots, core, rank), XZ, 0, 0)  22.4 us
    ppermute x12, starting transfers between devices, send(): return lax.ppermute(value, 'y', pairs)  19.4 us
    dot_general x17, matrix products, dot(): lax.dot_general(left, right, (((left_dim,), (0,)), ((), ())), preferred_e...  15.9 us
    all_to_all x1, waiting for transfers between devices, grams(): every = lax.all_to_all(jnp.broadcast_to(total[None], shape), XZ, 0, 0)  13.7 us
    all_gather x1, waiting for transfers between devices, body(): projected = lax.all_gather(projected, DP, axis=0, tiled=True)  12.7 us
    ppermute x6, starting transfers between devices, along_x(): lax.ppermute(items[k], 'x', [(i, (i + k) % count) for i in range(count)])  11.3 us
    all_to_all x1, starting transfers between devices, grams(): slices = lax.all_to_all(parts.reshape(shape), XZ, 0, 0)  11.2 us
  transfers between devices with their start and end apart: 30, of which 15 were waited for; matrix products, arithmetic and copies ran while one was open for 11% of the time, Pallas kernels for 0%

profile of v4, /device:TPU:32, one launch (start us, length us, event | category | flops | bytes accessed | tf_op | source)
XLA Modules:
  0.0 189.9 jit_solution(17707380291803786705)
XLA Ops:
  6.5 1.4 collective-permute-start.7
  9.5 1.1 convolution_convert_fusion.2
  10.7 1.0 pad_maximum_fusion.4
  12.4 6.7 %collective-permute-start.11 = (bf16[128,640]{1,0:T(8,128)(2,1)S(1)}, bf16[128,640]{1,0:T(8,128)(2,1)S(1)}, u32[]{:S(2)}, u32[]{:S(2)}) collective-permute-start(bf16[128,640]{1,0:T(8,128)(2,1)S(1)} %pad_maximum_fusion.4), channel_id=1, source_target_pairs={{64,0},{128,64},{0,128},{65,1},{129,65},{1,129},{66,2},{130,66},{2... | collective-permute-start | bytes 491528 | tf_op jit(solution)/shard_map/ppermute | solution.py:20
  19.1 0.9 dynamic-slice_bitcast_fusion.1
  20.0 0.9 broadcast_select_fusion.1
  21.0 6.3 %collective-permute-done.11 = bf16[128,640]{1,0:T(8,128)(2,1)S(1)} collective-permute-done((bf16[128,640]{1,0:T(8,128)(2,1)S(1)}, bf16[128,640]{1,0:T(8,128)(2,1)S(1)}, u32[]{:S(2)}, u32[]{:S(2)}) %collective-permute-start.11) | collective-permute-done | bytes 163872 | tf_op jit(solution)/shard_map/ppermute | solution.py:20
  28.0 0.8 collective-permute-done.12
  29.8 1.0 fusion.10
  30.8 11.2 %all-to-all-start = ((bf16[32,8,640]{2,1,0:T(8,128)(2,1)}), bf16[32,8,640]{2,1,0:T(8,128)(2,1)S(1)}, u32[]{:S(2)}, u32[]{:S(2)}) async-start(bf16[32,8,640]{2,1,0:T(8,128)(2,1)} %fusion.10), calls=%async_computation | async-start | bytes 655360 | tf_op jit(solution)/shard_map/all_to_all | solution.py:72
  42.2 2.9 %constant_dynamic-slice_fusion.6 = (bf16[128,2048]{1,0:T(8,128)(2,1)S(1)}, bf16[128,2048]{1,0:T(8,128)(2,1)}, bf16[128,2048]{1,0:T(8,128)(2,1)}, bf16[128,2048]{1,0:T(8,128)(2,1)}) fusion(bf16[128,8192]{1,0:T(8,128)(2,1)} %param.11, s32[]{:T(128)S(6)} %select_n.128, s32[]{:T(128)S(6)} %select_n.130, s32[]{:T(128)S(6)} %select_n.134, s32[]{:T(128)S(6)} %select_n.132), kind=kLoop, calls=%fused_computation.93 | loop fusion | bytes 4194320 | tf_op jit(solution)/shard_map/dynamic_slice | solution.py:130
  45.0 1.5 collective-permute-start.4
  46.5 2.7 %collective-permute-start.5 = (bf16[128,2048]{1,0:T(8,128)(2,1)}, bf16[128,2048]{1,0:T(8,128)(2,1)}, u32[]{:S(2)}, u32[]{:S(2)}) collective-permute-start(bf16[128,2048]{1,0:T(8,128)(2,1)} %get-tuple-element.8), channel_id=1, source_target_pairs={{0,32},{16,48},{32,0},{48,16},{1,33},{17,49},{33,1},{49,17},{2,34}... | collective-permute-start | bytes 1572872 | tf_op jit(solution)/shard_map/ppermute | solution.py:45
  49.2 1.4 collective-permute-start.6
  50.7 0.8 convolution_convert_fusion.3
  51.4 4.7 %all-to-all-done = bf16[32,8,640]{2,1,0:T(8,128)(2,1)S(1)} async-done(((bf16[32,8,640]{2,1,0:T(8,128)(2,1)}), bf16[32,8,640]{2,1,0:T(8,128)(2,1)S(1)}, u32[]{:S(2)}, u32[]{:S(2)}) %all-to-all-start) | async-done | bytes 327712 | tf_op jit(solution)/shard_map/all_to_all | solution.py:72
  56.2 0.8 broadcast_in_dim.27
  57.0 4.8 %all-to-all-start.1 = ((bf16[32,8,640]{2,1,0:T(8,128)(2,1)}), bf16[32,8,640]{2,1,0:T(8,128)(2,1)S(1)}, u32[]{:S(2)}, u32[]{:S(2)}) async-start(bf16[32,8,640]{2,1,0:T(8,128)(2,1)} %broadcast_in_dim.27), calls=%async_computation.1 | async-start | bytes 655360 | tf_op jit(solution)/shard_map/all_to_all | solution.py:74
  61.9 2.1 %fusion.15 = bf16[128,64]{0,1:T(8,128)(2,1)S(1)} fusion(bf16[1,128,8192]{2,1,0:T(8,128)(2,1)S(1)} %copy-done, bf16[1,8192,64]{1,2,0:T(8,128)(2,1)} %param.14), kind=kOutput, calls=%fused_computation.22 | convolution fusion | flops 134225920 | bytes 3162112 | tf_op jit(solution)/shard_map/dot_general | solution.py:14
  64.0 13.7 %all-to-all-done.1 = bf16[32,8,640]{2,1,0:T(8,128)(2,1)S(1)} async-done(((bf16[32,8,640]{2,1,0:T(8,128)(2,1)}), bf16[32,8,640]{2,1,0:T(8,128)(2,1)S(1)}, u32[]{:S(2)}, u32[]{:S(2)}) %all-to-all-start.1) | async-done | bytes 327712 | tf_op jit(solution)/shard_map/all_to_all | solution.py:74
  77.7 1.3 collective-permute-start.13
  79.0 1.6 collective-permute-start.14
  80.6 1.9 collective-permute-done.14
  82.5 1.3 collective-permute-start.19
  83.7 3.3 %collective-permute-done.13 = bf16[256,384]{1,0:T(8,128)(2,1)S(1)} collective-permute-done((bf16[256,384]{1,0:T(8,128)(2,1)S(1)}, bf16[256,384]{1,0:T(8,128)(2,1)S(1)}, u32[]{:S(2)}, u32[]{:S(2)}) %collective-permute-start.13) | collective-permute-done | bytes 196640 | tf_op jit(solution)/shard_map/ppermute | solution.py:20
  87.1 1.3 collective-permute-start.23
  88.4 1.3 collective-permute-start.16
  89.8 2.9 %pad_maximum_fusion = bf16[512,2048]{1,0:T(8,128)(2,1)} fusion(bf16[128,2048]{1,0:T(8,128)(2,1)} %collective-permute-done.6, bf16[128,2048]{1,0:T(8,128)(2,1)} %collective-permute-done.5, bf16[128,2048]{1,0:T(8,128)(2,1)} %collective-permute-done.4, bf16[128,2048]{1,0:T(8,128)(2,1)S(1)} %get-tuple-element.5), kind=kLoop, calls=%fused_computation.5 | loop fusion | flops 8388608 | bytes 4194304 | tf_op jit(solution)/shard_map/concatenate | solution.py:48
  93.5 1.3 collective-permute-start.20
  94.8 1.3 collective-permute-start.21
  96.3 11.7 %collective-permute-done.20 = bf16[256,512]{1,0:T(8,128)(2,1)S(1)} collective-permute-done((bf16[256,512]{1,0:T(8,128)(2,1)S(1)}, bf16[256,512]{1,0:T(8,128)(2,1)S(1)}, u32[]{:S(2)}, u32[]{:S(2)}) %collective-permute-start.20) | collective-permute-done | bytes 262176 | tf_op jit(solution)/shard_map/ppermute | solution.py:20
  108.2 1.0 collective-permute-done.18
  109.4 1.3 collective-permute-done.21
  111.3 2.3 %collective-permute-done.22 = bf16[256,128]{1,0:T(8,128)(2,1)S(1)} collective-permute-done((bf16[256,128]{1,0:T(8,128)(2,1)S(1)}, bf16[256,128]{1,0:T(8,128)(2,1)S(1)}, u32[]{:S(2)}, u32[]{:S(2)}) %collective-permute-start.22) | collective-permute-done | bytes 65568 | tf_op jit(solution)/shard_map/ppermute | solution.py:24
  113.8 12.7 %all-gather.2.cloned.1.call-done = bf16[8192,64]{0,1:T(8,128)(2,1)} async-done(((bf16[128,64]{0,1:T(8,128)(2,1)}), bf16[8192,64]{0,1:T(8,128)(2,1)}) %all-gather.2.cloned.1.call-update) | async-done | bytes 1048592 | tf_op jit(solution)/shard_map/all_gather | solution.py:121
  126.5 2.1 %fusion.21 = bf16[128,64]{0,1:T(8,128)(2,1)S(1)} fusion(bf16[8192,64]{0,1:T(8,128)(2,1)} %all-gather.2.cloned.1.call-done, bf16[1,128,8192]{2,1,0:T(8,128)(2,1)S(1)} %copy-done), kind=kOutput, calls=%fused_computation.26 | convolution fusion | flops 134225920 | bytes 3162112 | tf_op jit(solution)/shard_map/dot_general | solution.py:14
  128.6 1.6 collective-permute-start
  130.2 2.8 %collective-permute-start.1 = (bf16[128,129]{0,1:T(8,128)(2,1)S(1)}, bf16[128,129]{0,1:T(8,128)(2,1)S(1)}, u32[]{:S(2)}, u32[]{:S(2)}) collective-permute-start(bf16[128,129]{0,1:T(8,128)(2,1)S(1)} %get-tuple-element.23), channel_id=1, source_target_pairs={{0,32},{16,48},{32,0},{48,16},{1,33},{17,49},{33,1},{49,17},{2,34}... | collective-permute-start | bytes 99080 | tf_op jit(solution)/shard_map/ppermute | solution.py:45
  133.0 1.3 collective-permute-start.2
  134.6 0.8 broadcast_in_dim.48
  135.4 5.6 %all-to-all-start.2 = ((bf16[8,128,128]{2,1,0:T(8,128)(2,1)}), bf16[8,128,128]{2,1,0:T(8,128)(2,1)S(1)}, u32[]{:S(2)}, u32[]{:S(2)}) async-start(bf16[8,128,128]{2,1,0:T(8,128)(2,1)} %broadcast_in_dim.48), calls=%async_computation.2 | async-start | bytes 524288 | tf_op jit(solution)/shard_map/all_to_all | solution.py:94
  141.2 1.3 collective-permute-done.3
  142.5 8.5 %all-to-all-done.2 = bf16[8,128,128]{2,1,0:T(8,128)(2,1)S(1)} async-done(((bf16[8,128,128]{2,1,0:T(8,128)(2,1)}), bf16[8,128,128]{2,1,0:T(8,128)(2,1)S(1)}, u32[]{:S(2)}, u32[]{:S(2)}) %all-to-all-start.2) | async-done | bytes 262176 | tf_op jit(solution)/shard_map/all_to_all | solution.py:94
  151.1 1.4 collective-permute-done.24
  152.6 2.3 %convolution_convert_fusion.1 = bf16[512,128]{1,0:T(8,128)(2,1)S(1)} fusion(bf16[512,2048]{1,0:T(8,128)(2,1)} %pad_maximum_fusion, bf16[2048,128]{1,0:T(8,128)(2,1)S(1)} %bitcast.86), kind=kOutput, calls=%fused_computation.14 | convolution fusion | flops 268500992 | bytes 2752512 | tf_op jit(solution)/shard_map/dot_general | solution.py:14
  155.0 2.3 %convolution_convert_fusion = bf16[512,128]{1,0:T(8,128)(2,1)S(1)} fusion(bf16[512,2048]{1,0:T(8,128)(2,1)} %collective-permute-done.25, bf16[2048,128]{1,0:T(8,128)(2,1)S(1)} %bitcast.87), kind=kOutput, calls=%fused_computation.13 | convolution fusion | flops 268500992 | bytes 2752512 | tf_op jit(solution)/shard_map/dot_general | solution.py:14
  157.3 2.4 %fusion = bf16[32,128,128]{2,1,0:T(8,128)(2,1)S(1)} fusion(bf16[1024,128]{0,1:T(8,128)(2,1)S(1)} %slice.63, bf16[1024,32]{0,1:T(8,128)(2,1)S(1)} %compare_convert_fusion, bf16[512,128]{1,0:T(8,128)(2,1)S(1)} %convolution_convert_fusion, bf16[512,128]{1,0:T(8,128)(2,1)S(1)} %convolution_convert_fusion.1), kind=kOutput, calls=%fused_computation | convolution fusion | flops 1078460416 | bytes 1638400 | tf_op jit(solution)/shard_map/dot_general | solution.py:14
  159.7 22.4 %all_to_all.20 = bf16[32,64,128]{2,1,0:T(8,128)(2,1)S(1)} all-to-all(bf16[32,64,128]{2,1,0:T(8,128)(2,1)S(1)} %fusion.24), channel_id=1, replica_groups=mesh['y'=4,'x'=4,'z'=8,'c'=2] {'x','z'}, dimensions={0} | all-to-all | bytes 1048576 | tf_op jit(solution)/shard_map/all_to_all | solution.py:148
  (90 shorter events, 8.2 us)
Async XLA Ops:
  6.5 55.4 %copy-start = (bf16[1,128,8192]{2,1,0:T(8,128)(2,1)S(1)}, bf16[1,128,8192]{2,1,0:T(8,128)(2,1)}, u32[]{:S(2)}) copy-start(bf16[1,128,8192]{2,1,0:T(8,128)(2,1)} %param.10) | copy-start | bytes 6291460
  6.5 13.4 %collective-permute-start.7 = (bf16[128,512]{1,0:T(8,128)(2,1)}, bf16[128,512]{1,0:T(8,128)(2,1)S(1)}, u32[]{:S(2)}, u32[]{:S(2)}) collective-permute-start(bf16[128,512]{1,0:T(8,128)(2,1)} %bitcast.92), channel_id=1, source_target_pairs={{128,0},{192,64},{64,128},{129,1},{193,65},{65,129},{130,2},{194,6... | collective-permute-start | bytes 393224 | tf_op jit(solution)/shard_map/ppermute | solution.py:20
  8.0 13.0 %collective-permute-start.8 = (bf16[128,512]{1,0:T(8,128)(2,1)}, bf16[128,512]{1,0:T(8,128)(2,1)S(1)}, u32[]{:S(2)}, u32[]{:S(2)}) collective-permute-start(bf16[128,512]{1,0:T(8,128)(2,1)} %bitcast.93), channel_id=1, source_target_pairs={{192,128},{193,129},{194,130},{195,131},{196,132},{197,133},{198,1... | collective-permute-start | bytes 393224 | tf_op jit(solution)/shard_map/ppermute | solution.py:20
  11.7 9.3 %collective-permute-start.10 = (bf16[128,640]{1,0:T(8,128)(2,1)S(1)}, bf16[128,640]{1,0:T(8,128)(2,1)S(1)}, u32[]{:S(2)}, u32[]{:S(2)}) collective-permute-start(bf16[128,640]{1,0:T(8,128)(2,1)S(1)} %pad_maximum_fusion.4), channel_id=1, source_target_pairs={{64,192},{65,193},{66,194},{67,195},{68,196},{69,197},{70,198},{71... | collective-permute-start | bytes 491528 | tf_op jit(solution)/shard_map/ppermute | solution.py:20
  12.4 14.9 %collective-permute-start.11 = (bf16[128,640]{1,0:T(8,128)(2,1)S(1)}, bf16[128,640]{1,0:T(8,128)(2,1)S(1)}, u32[]{:S(2)}, u32[]{:S(2)}) collective-permute-start(bf16[128,640]{1,0:T(8,128)(2,1)S(1)} %pad_maximum_fusion.4), channel_id=1, source_target_pairs={{64,0},{128,64},{0,128},{65,1},{129,65},{1,129},{66,2},{130,66},{2... | collective-permute-start | bytes 491528 | tf_op jit(solution)/shard_map/ppermute | solution.py:20
  27.3 1.5 collective-permute-start.12
  27.4 1.6 collective-permute-start.9
  30.8 25.3 %all-to-all-start = ((bf16[32,8,640]{2,1,0:T(8,128)(2,1)}), bf16[32,8,640]{2,1,0:T(8,128)(2,1)S(1)}, u32[]{:S(2)}, u32[]{:S(2)}) async-start(bf16[32,8,640]{2,1,0:T(8,128)(2,1)} %fusion.10), calls=%async_computation | async-start | bytes 655360 | tf_op jit(solution)/shard_map/all_to_all | solution.py:72
  42.0 84.5 %all-gather.2.cloned.1.call-start = ((), (), s32[]{:S(2)}) async-start(), calls=%async_computation.4 | async-start | bytes 1064960 | tf_op jit(solution)/shard_map/all_gather | solution.py:121
  42.1 8.5 %copy-start.1 = (bf16[1,128,512]{2,1,0:T(8,128)(2,1)S(1)}, bf16[1,128,512]{2,1,0:T(8,128)(2,1)}, u32[]{:S(2)}) copy-start(bf16[1,128,512]{2,1,0:T(8,128)(2,1)} %param.12) | copy-start | bytes 393220
  42.2 8.5 %copy-start.3 = (bf16[1,512,64]{1,2,0:T(8,128)(2,1)S(1)}, bf16[1,512,64]{1,2,0:T(8,128)(2,1)}, u32[]{:S(2)}) copy-start(bf16[1,512,64]{1,2,0:T(8,128)(2,1)} %param.16) | copy-start | bytes 196612
  42.2 19.6 %copy-start.4 = (s32[64]{0:T(128)S(1)}, s32[64]{0:T(128)}, u32[]{:S(2)}) copy-start(s32[64]{0:T(128)} %param.19) | copy-start | bytes 772
  42.2 19.6 %copy-start.5 = (s32[128]{0:T(128)S(1)}, s32[128]{0:T(128)}, u32[]{:S(2)}) copy-start(s32[128]{0:T(128)} %param.18) | copy-start | bytes 1540
  45.0 43.4 %collective-permute-start.4 = (bf16[128,2048]{1,0:T(8,128)(2,1)}, bf16[128,2048]{1,0:T(8,128)(2,1)}, u32[]{:S(2)}, u32[]{:S(2)}) collective-permute-start(bf16[128,2048]{1,0:T(8,128)(2,1)} %get-tuple-element.6), channel_id=1, source_target_pairs={{0,16},{16,32},{32,48},{48,0},{1,17},{17,33},{33,49},{49,1},{2,18}... | collective-permute-start | bytes 1572872 | tf_op jit(solution)/shard_map/ppermute | solution.py:45
  46.5 43.2 %collective-permute-start.5 = (bf16[128,2048]{1,0:T(8,128)(2,1)}, bf16[128,2048]{1,0:T(8,128)(2,1)}, u32[]{:S(2)}, u32[]{:S(2)}) collective-permute-start(bf16[128,2048]{1,0:T(8,128)(2,1)} %get-tuple-element.8), channel_id=1, source_target_pairs={{0,32},{16,48},{32,0},{48,16},{1,33},{17,49},{33,1},{49,17},{2,34}... | collective-permute-start | bytes 1572872 | tf_op jit(solution)/shard_map/ppermute | solution.py:45
  49.2 40.6 %collective-permute-start.6 = (bf16[128,2048]{1,0:T(8,128)(2,1)}, bf16[128,2048]{1,0:T(8,128)(2,1)}, u32[]{:S(2)}, u32[]{:S(2)}) collective-permute-start(bf16[128,2048]{1,0:T(8,128)(2,1)} %get-tuple-element.7), channel_id=1, source_target_pairs={{0,48},{16,0},{32,16},{48,32},{1,49},{17,1},{33,17},{49,33},{2,50}... | collective-permute-start | bytes 1572872 | tf_op jit(solution)/shard_map/ppermute | solution.py:45
  57.0 25.5 %copy-start.2 = (bf16[1,128,512]{2,1,0:T(8,128)(2,1)S(1)}, bf16[1,128,512]{2,1,0:T(8,128)(2,1)}, u32[]{:S(2)}) copy-start(bf16[1,128,512]{2,1,0:T(8,128)(2,1)} %param.13) | copy-start | bytes 393220
  57.0 20.7 %all-to-all-start.1 = ((bf16[32,8,640]{2,1,0:T(8,128)(2,1)}), bf16[32,8,640]{2,1,0:T(8,128)(2,1)S(1)}, u32[]{:S(2)}, u32[]{:S(2)}) async-start(bf16[32,8,640]{2,1,0:T(8,128)(2,1)} %broadcast_in_dim.27), calls=%async_computation.1 | async-start | bytes 655360 | tf_op jit(solution)/shard_map/all_to_all | solution.py:74
  77.7 9.4 %collective-permute-start.13 = (bf16[256,384]{1,0:T(8,128)(2,1)S(1)}, bf16[256,384]{1,0:T(8,128)(2,1)S(1)}, u32[]{:S(2)}, u32[]{:S(2)}) collective-permute-start(bf16[256,384]{1,0:T(8,128)(2,1)S(1)} %slice.67), channel_id=1, source_target_pairs={{128,0},{129,1},{130,2},{131,3},{132,4},{133,5},{134,6},{135,7},{1... | collective-permute-start | bytes 589832 | tf_op jit(solution)/shard_map/ppermute | solution.py:20
  79.0 3.5 %collective-permute-start.14 = (bf16[256,128]{1,0:T(8,128)(2,1)S(1)}, bf16[256,128]{1,0:T(8,128)(2,1)S(1)}, u32[]{:S(2)}, u32[]{:S(2)}) collective-permute-start(bf16[256,128]{1,0:T(8,128)(2,1)S(1)} %slice.69), channel_id=1, source_target_pairs={{0,64},{64,128},{1,65},{65,129},{2,66},{66,130},{3,67},{67,131},{4... | collective-permute-start | bytes 196616 | tf_op jit(solution)/shard_map/ppermute | solution.py:20
  82.5 28.6 %collective-permute-start.19 = (bf16[128,512]{1,0:T(8,128)(2,1)S(1)}, bf16[128,512]{1,0:T(8,128)(2,1)S(1)}, u32[]{:S(2)}, u32[]{:S(2)}) collective-permute-start(bf16[128,512]{1,0:T(8,128)(2,1)S(1)} %bitcast.95), channel_id=1, source_target_pairs={{128,0},{192,64},{129,1},{193,65},{130,2},{194,66},{131,3},{195,67... | collective-permute-start | bytes 393224 | tf_op jit(solution)/shard_map/ppermute | solution.py:20
  87.1 26.5 %collective-permute-start.23 = (bf16[128,512]{1,0:T(8,128)(2,1)S(1)}, bf16[128,512]{1,0:T(8,128)(2,1)S(1)}, u32[]{:S(2)}, u32[]{:S(2)}) collective-permute-start(bf16[128,512]{1,0:T(8,128)(2,1)S(1)} %bitcast.96), channel_id=1, source_target_pairs={{192,0},{193,1},{194,2},{195,3},{196,4},{197,5},{198,6},{199,7},{2... | collective-permute-start | bytes 393224 | tf_op jit(solution)/shard_map/ppermute | solution.py:20
  88.4 45.9 %collective-permute-start.16 = (bf16[128,512]{1,0:T(8,128)(2,1)S(1)}, bf16[128,512]{1,0:T(8,128)(2,1)S(1)}, u32[]{:S(2)}, u32[]{:S(2)}) collective-permute-start(bf16[128,512]{1,0:T(8,128)(2,1)S(1)} %bitcast.97), channel_id=1, source_target_pairs={{64,0},{128,64},{192,128},{65,1},{129,65},{193,129},{66,2},{130,66... | collective-permute-start | bytes 393224 | tf_op jit(solution)/shard_map/ppermute | solution.py:20
  89.7 3.7 %collective-permute-start.15 = (bf16[256,128]{1,0:T(8,128)(2,1)S(1)}, bf16[256,128]{1,0:T(8,128)(2,1)S(1)}, u32[]{:S(2)}, u32[]{:S(2)}) collective-permute-start(bf16[256,128]{1,0:T(8,128)(2,1)S(1)} %slice_select_fusion.2), channel_id=1, source_target_pairs={{0,1},{1,0},{2,3},{3,2},{4,5},{5,4},{6,7},{7,6},{8,9},{9,8},{10,11... | collective-permute-start | bytes 196616 | tf_op jit(solution)/shard_map/ppermute | solution.py:24
  92.8 2.0 %collective-permute-start.17 = (bf16[256,128]{1,0:T(8,128)(2,1)S(1)}, bf16[256,128]{1,0:T(8,128)(2,1)S(1)}, u32[]{:S(2)}, u32[]{:S(2)}) collective-permute-start(bf16[256,128]{1,0:T(8,128)(2,1)S(1)} %slice.69), channel_id=1, source_target_pairs={{192,64},{193,65},{194,66},{195,67},{196,68},{197,69},{198,70},{19... | collective-permute-start | bytes 196616 | tf_op jit(solution)/shard_map/ppermute | solution.py:20
  93.5 14.5 %collective-permute-start.20 = (bf16[256,512]{1,0:T(8,128)(2,1)S(1)}, bf16[256,512]{1,0:T(8,128)(2,1)S(1)}, u32[]{:S(2)}, u32[]{:S(2)}) collective-permute-start(bf16[256,512]{1,0:T(8,128)(2,1)S(1)} %slice.71), channel_id=1, source_target_pairs={{192,0},{193,1},{194,2},{195,3},{196,4},{197,5},{198,6},{199,7},{2... | collective-permute-start | bytes 786440 | tf_op jit(solution)/shard_map/ppermute | solution.py:20
  94.8 15.9 %collective-permute-start.21 = (bf16[256,512]{1,0:T(8,128)(2,1)S(1)}, bf16[256,512]{1,0:T(8,128)(2,1)S(1)}, u32[]{:S(2)}, u32[]{:S(2)}) collective-permute-start(bf16[256,512]{1,0:T(8,128)(2,1)S(1)} %slice.71), channel_id=1, source_target_pairs={{64,0},{65,1},{66,2},{67,3},{68,4},{69,5},{70,6},{71,7},{72,8},{73... | collective-permute-start | bytes 786440 | tf_op jit(solution)/shard_map/ppermute | solution.py:20
  108.0 1.3 collective-permute-start.18
  109.2 45.7 %collective-permute-start.25 = (bf16[512,2048]{1,0:T(8,128)(2,1)}, bf16[512,2048]{1,0:T(8,128)(2,1)}, u32[]{:S(2)}, u32[]{:S(2)}) collective-permute-start(bf16[512,2048]{1,0:T(8,128)(2,1)} %pad_maximum_fusion), channel_id=1, source_target_pairs={{0,1},{1,0},{2,3},{3,2},{4,5},{5,4},{6,7},{7,6},{8,9},{9,8},{10,11... | collective-permute-start | bytes 6291464 | tf_op jit(solution)/shard_map/ppermute | solution.py:24
  111.0 2.6 %collective-permute-start.22 = (bf16[256,128]{1,0:T(8,128)(2,1)S(1)}, bf16[256,128]{1,0:T(8,128)(2,1)S(1)}, u32[]{:S(2)}, u32[]{:S(2)}) collective-permute-start(bf16[256,128]{1,0:T(8,128)(2,1)S(1)} %add_convert_fusion), channel_id=1, source_target_pairs={{0,1},{1,0},{2,3},{3,2},{4,5},{5,4},{6,7},{7,6},{8,9},{9,8},{10,11... | collective-permute-start | bytes 196616 | tf_op jit(solution)/shard_map/ppermute | solution.py:24
  128.6 12.4 %collective-permute-start = (bf16[128,129]{0,1:T(8,128)(2,1)S(1)}, bf16[128,129]{0,1:T(8,128)(2,1)S(1)}, u32[]{:S(2)}, u32[]{:S(2)}) collective-permute-start(bf16[128,129]{0,1:T(8,128)(2,1)S(1)} %get-tuple-element.23), channel_id=1, source_target_pairs={{0,16},{16,32},{32,48},{48,0},{1,17},{17,33},{33,49},{49,1},{2,18}... | collective-permute-start | bytes 99080 | tf_op jit(solution)/shard_map/ppermute | solution.py:45
  130.2 10.9 %collective-permute-start.1 = (bf16[128,129]{0,1:T(8,128)(2,1)S(1)}, bf16[128,129]{0,1:T(8,128)(2,1)S(1)}, u32[]{:S(2)}, u32[]{:S(2)}) collective-permute-start(bf16[128,129]{0,1:T(8,128)(2,1)S(1)} %get-tuple-element.23), channel_id=1, source_target_pairs={{0,32},{16,48},{32,0},{48,16},{1,33},{17,49},{33,1},{49,17},{2,34}... | collective-permute-start | bytes 99080 | tf_op jit(solution)/shard_map/ppermute | solution.py:45
  133.0 8.0 %collective-permute-start.2 = (bf16[128,129]{0,1:T(8,128)(2,1)S(1)}, bf16[128,129]{0,1:T(8,128)(2,1)S(1)}, u32[]{:S(2)}, u32[]{:S(2)}) collective-permute-start(bf16[128,129]{0,1:T(8,128)(2,1)S(1)} %get-tuple-element.23), channel_id=1, source_target_pairs={{0,48},{16,0},{32,16},{48,32},{1,49},{17,1},{33,17},{49,33},{2,50}... | collective-permute-start | bytes 99080 | tf_op jit(solution)/shard_map/ppermute | solution.py:45
  135.4 15.6 %all-to-all-start.2 = ((bf16[8,128,128]{2,1,0:T(8,128)(2,1)}), bf16[8,128,128]{2,1,0:T(8,128)(2,1)S(1)}, u32[]{:S(2)}, u32[]{:S(2)}) async-start(bf16[8,128,128]{2,1,0:T(8,128)(2,1)} %broadcast_in_dim.48), calls=%async_computation.2 | async-start | bytes 524288 | tf_op jit(solution)/shard_map/all_to_all | solution.py:94
  141.1 1.4 collective-permute-start.3
  151.0 1.5 collective-permute-start.24
Sparse Core Ops, SparseCore 0:
  51.6 74.8 all-gather.1

commit v5 on v3

v5 whole, which is shorter than its diff:
```python
import jax
import jax.numpy as jnp
from jax import lax
from jax.experimental import pallas as pl
from jax.experimental.pallas import tpu as pltpu
from jax.sharding import Mesh, PartitionSpec as P

XZ = ("x", "z")
DP = ("x", "z", "c")
SWAP = [(0, 1), (1, 0)]
BF16 = jnp.bfloat16
F32 = jnp.float32


def dot(left, right, left_dim=1):
    return lax.dot_general(
        left, right, (((left_dim,), (0,)), ((), ())), preferred_element_type=F32
    )


def send(value, pairs):
    return lax.ppermute(value, "y", pairs)


def swap(value):
    return lax.ppermute(value, "c", SWAP)


def half_of(value, core, axis=1):
    width = value.shape[axis] // 2
    return lax.dynamic_slice_in_dim(value, core * width, width, axis)


def ordered(mine, core):
    got = swap(mine)
    return jnp.concatenate([jnp.where(core == 0, mine, got), jnp.where(core == 0, got, mine)])


def quarter_of(value, place, count):
    width = value.shape[1] // count
    return lax.dynamic_slice_in_dim(value, (place % count) * width, width, 1)


def along_x(value, steps):
    count = lax.axis_size("x")
    return lax.ppermute(value, "x", [(i, (i - steps) % count) for i in range(count)])


def packed_rows(wo, wv, p_value_in):
    count, place = lax.axis_size("x"), lax.axis_index("x")
    maps = lax.dot_general(
        p_value_in, wv, (((0,), (1,)), ((), ())), preferred_element_type=F32
    ).astype(BF16)
    around = [maps] + [along_x(maps, k) for k in range(1, count)]
    pieces = []
    for p in range(count):
        steps = (p - place) % count
        item = around[0]
        for k in range(1, count):
            item = jnp.where(steps == k, around[k], item)
        pieces.append(item)
    return jnp.concatenate([wo, jnp.concatenate(pieces, axis=1)], axis=0)


def product_kernel(near, one, two, three, act_0, act_1, act_2, act_3, block, parts, value, parts_sum, value_sum):
    step, last = pl.program_id(0), pl.num_programs(0) - 1
    ranks, height, kv = block.shape
    rows = near.shape[1] // ranks
    tokens = near.shape[0]

    @pl.when(step == 0)
    def _():
        parts_sum[...] = jnp.zeros_like(parts_sum)
        value_sum[...] = jnp.zeros_like(value_sum)

    left = jnp.concatenate([near[...], one[...], two[...], three[...]], axis=0)
    for k in range(0, ranks, 2):
        weights = block[k : k + 2, :rows, :].reshape(2 * rows, kv)
        parts_sum[...] += jnp.dot(
            left[:, k * rows : (k + 2) * rows], weights, preferred_element_type=F32
        )
        for x, act in enumerate((act_0, act_1, act_2, act_3)):
            maps = jnp.concatenate(
                [block[k + i, rows:, x * rows : (x + 1) * rows] for i in range(2)], axis=1
            )
            value_sum[...] += lax.dot_general(
                act[:, k * rows : (k + 2) * rows],
                maps,
                (((1,), (1,)), ((), ())),
                preferred_element_type=F32,
            )

    @pl.when(step == last)
    def _():
        parts[...] = parts_sum[...].astype(BF16)
        value[...] = value_sum[...].astype(BF16)


def products(moved, act, full):
    tokens, quarter = moved[0].shape
    count, height, kv = full.shape
    rows = quarter // count
    rank = height - rows
    ranks = 4
    steps = count // ranks
    places = len(moved)
    token_spec = pl.BlockSpec((tokens, ranks * rows), lambda i: (0, i))
    act_specs = [
        pl.BlockSpec((tokens, ranks * rows), lambda i, x=x: (0, x * steps + i)) for x in range(places)
    ]
    return pl.pallas_call(
        product_kernel,
        grid=(steps,),
        in_specs=[token_spec] * places + act_specs + [
            pl.BlockSpec((ranks, height, kv), lambda i: (i, 0, 0))
        ],
        out_specs=[
            pl.BlockSpec((places * tokens, kv), lambda i: (0, 0)),
            pl.BlockSpec((tokens, rank), lambda i: (0, 0)),
        ],
        out_shape=[
            jax.ShapeDtypeStruct((places * tokens, kv), BF16),
            jax.ShapeDtypeStruct((tokens, rank), BF16),
        ],
        scratch_shapes=[
            pltpu.VMEM((places * tokens, kv), F32),
            pltpu.VMEM((tokens, rank), F32),
        ],
        compiler_params=pltpu.CompilerParams(
            dimension_semantics=("arbitrary",), vmem_limit_bytes=32 * 1024 * 1024
        ),
        cost_estimate=pl.CostEstimate(
            flops=2 * places * tokens * quarter * (kv + rank),
            bytes_accessed=2 * (full.size + act.size + 4 * moved[0].size),
            transcendentals=0,
        ),
    )(*moved, act, act, act, act, full)


def exchanged(items):
    return [items[0]] + [along_x(items[k], -k) for k in range(1, len(items))]


def together(value, others):
    value, *others = lax.optimization_barrier((value, *others))
    return value, others


def grams(wv, right, plane, core, first, second, work):
    kv, columns = wv.shape[1], right.shape[1]
    width = kv // 2
    near, far = send(wv, [(3, 0), (2, 1)]), send(wv, [(3, 1)])
    above, below = send(right, [(0, 1), (1, 2), (2, 3)]), send(right, [(1, 0)])
    right = jnp.where(plane == 0, below, above)
    lefts = [jnp.where(plane == 0, near, wv), near, far]
    got = swap(jnp.concatenate([half_of(item, 1 - core) for item in lefts], axis=1))
    mine = jnp.concatenate([half_of(item, core) for item in lefts], axis=1)
    left = jnp.concatenate([mine, got], axis=0)
    rows = jnp.concatenate([right, swap(right)], axis=0)
    main = dot(left[:, :width], rows, 0)
    own = [dot(left[:, k * width : (k + 1) * width], rows[:, kv:], 0) for k in range(3)]
    own = jnp.concatenate(own + [jnp.zeros((width, columns - 3 * (columns - kv)), F32)], axis=1)
    parts = jnp.where(plane == 1, own, main).astype(BF16)
    parts, first = together(parts, first)
    ranks = lax.axis_size(XZ)
    shape = (ranks, width // ranks, columns)
    slices = lax.all_to_all(parts.reshape(shape), XZ, 0, 0)
    total = jnp.sum(slices.astype(F32), axis=0).astype(BF16)
    total, second = together(total, second)
    every = lax.all_to_all(jnp.broadcast_to(total[None], shape), XZ, 0, 0)
    every, done = together(every, work(first, second))
    return every.reshape(width, columns), second, done


def solve(half, plane, core, kv, parts):
    block = half.shape[1] - kv
    above = send(half, [(1, 2), (2, 3)])
    wrap = send(half, [(0, 3)])
    twice = send(half[:, : 3 * block], [(1, 3)])
    first = jnp.where(plane == 1, half[:, : 3 * block], above[:, : 3 * block])
    first = jnp.where(plane == 3, twice, first)
    second = jnp.where(plane == 2, half, above)
    f01, f02, f03 = (first[:, k * block : (k + 1) * block] for k in range(3))
    g21, g31, g32 = second[:, :kv], wrap[:, :kv], half[:, :kv]
    f12, f13, f23 = second[:, kv:], wrap[:, kv:], half[:, kv:]
    known = ordered(jnp.concatenate([f01, f12], axis=1), core)
    back = [along_x(item, k + 1) for k, item in enumerate(parts)]
    f01_all, f12_all = known[:, :block], known[:, block:]
    e02 = (f02.astype(F32) + dot(g21, f01_all)).astype(BF16)
    e02_all, back = together(ordered(e02, core), back)
    e13 = (f13.astype(F32) + dot(g32, f12_all)).astype(BF16)
    e03 = (f03.astype(F32) + dot(g31, f01_all) + dot(g32, e02_all)).astype(BF16)
    zero = jnp.zeros_like(f01)
    columns = (
        jnp.where(plane == 1, f01, jnp.where(plane == 2, e02, e03)),
        jnp.where(plane == 2, f12, jnp.where(plane == 3, e13, zero)),
        jnp.where(plane == 3, f23, zero),
    )
    return jnp.concatenate(columns, axis=1), back


def doc_sums(left, right, slots, core, rank):
    owners = lax.axis_size(XZ)
    named = 2 * jnp.arange(owners, dtype=jnp.int32) + core
    onehot = (slots[:, None] == named[None, :]).astype(BF16)
    spread = (onehot[:, :, None] * left[:, None, :]).reshape(left.shape[0], owners * 2 * rank)
    table = dot(spread, right, 0).reshape(owners, 2 * rank, 2 * rank)
    lane = lax.broadcasted_iota(jnp.int32, (1, rank, 2 * rank), 2)
    return jnp.where(lane < rank, table[:, :rank], table[:, rank:]).astype(BF16)


def body(
    hidden, cotangent, w_value, w_out_t, p_in, p_value_out, p_value_in, p_out, segments, owner_slot
):
    plane, core = lax.axis_index("y"), lax.axis_index("c")
    device = lax.axis_index(DP)
    wv, wo, acts = w_value[0], w_out_t[0], hidden[0]
    rows, kv = wv.shape
    rank = p_in.shape[2]
    documents = owner_slot.shape[0]

    places, place = lax.axis_size("x"), lax.axis_index("x")
    items = [quarter_of(cotangent, place + k, places) for k in range(places)]
    wv, items = together(wv, items)
    moved = exchanged(items)
    mixed = packed_rows(wo, wv, p_value_in[0])
    wv, (wo, mixed) = together(wv, [wo, mixed])
    full = lax.all_gather(mixed[None], ("z", "c"), axis=0, tiled=True)

    match = segments[:, None] == jnp.arange(documents, dtype=jnp.int32)[None, :]
    slots = jnp.sum(jnp.where(match, owner_slot[None, :], 0), axis=1)
    first_in = dot(acts, p_in[0]).astype(BF16)
    direct_out = dot(cotangent, p_out[0])
    out_rows = lax.dynamic_slice_in_dim(p_out[0], device * rows, rows, 0)
    right_rows = jnp.concatenate([wo, dot(wo, p_value_out[0]).astype(BF16), out_rows], axis=1)
    early = [first_in, direct_out, jnp.concatenate([slots, swap(slots)]), moved[2]]

    def work(near, early):
        tokens = acts.shape[0]
        parts, value = products([near[0], near[1], early[3], near[2]], acts, full)
        return [value] + [parts[k * tokens : (k + 1) * tokens] for k in range(places)]

    half, early, done = grams(
        wv, right_rows, plane, core, [moved[0], moved[1], moved[3]], early, work
    )
    first_in, direct_out, slots, far = early
    second_in, upd = done[0], done[1]
    spread_e, back = solve(half, plane, core, kv, done[2:])
    spread_e = ordered(spread_e, core)
    upd = (upd.astype(F32) + sum(item.astype(F32) for item in back)).astype(BF16)
    right = jnp.concatenate([dot(upd, p_value_out[0]), direct_out], axis=1)
    below = dot(upd, spread_e).astype(BF16)
    count = lax.axis_size("y")
    for k in range(1, count):
        start = jnp.maximum(plane - k, 0) * 2 * rank
        item = lax.dynamic_slice_in_dim(below, start, 2 * rank, 1)
        right = right + send(item, [(i, i - k) for i in range(k, count)]).astype(F32)
    packed = jnp.concatenate([first_in, second_in, right.astype(BF16)], axis=1)
    packed = jnp.concatenate([packed, swap(packed)], axis=0)
    left, right = packed[:, : 2 * rank], packed[:, 2 * rank :]
    parts = lax.all_to_all(doc_sums(left, right, slots, core, rank), XZ, 0, 0)
    total = jnp.sum(parts.astype(F32), axis=0)
    tables = total.reshape(rank, 2, rank).transpose(1, 0, 2)
    return tables.reshape(1, 2, 1, rank * rank)


def solution(mesh):
    grid = Mesh(mesh.devices.reshape(4, 4, 8, 2), ("y", "x", "z", "c"))
    placed = (
        P("y", DP, None),
        P(DP, None),
        P("y", DP, None),
        P("y", DP, None),
        P("y", None, None),
        P("y", None, None),
        P("y", None, None),
        P("y", None, None),
        P(DP),
        P(),
    )
    return jax.shard_map(
        body, mesh=grid, in_specs=placed, out_specs=P("y", None, DP, None), check_vma=False
    )
```

time: 173 us -> 147 us (0.85)
  blocking collectives: 49.6 us -> 22.3 us
  starting transfers between devices: 28.8 us -> 45.5 us
  local copies, waits for them, and re-layouts: 13.4 us -> 8.03 us
  other arithmetic: 6.86 us -> 2.26 us
  matrix products: 11 us -> 7.43 us
  waiting for transfers between devices: 45 us -> 42.8 us
    all_to_all x1 -> x0, blocking collectives: 26.2 us -> none  [grams(): slices = lax.all_to_all(parts.reshape(shape), XZ, 0, 0)]
    all_to_all x0 -> x1, starting transfers between devices: none -> 8.73 us  [grams(): slices = lax.all_to_all(parts.reshape(shape), XZ, 0, 0)]
    ppermute x3 -> x9, starting transfers between devices: 4.52 us -> 13.2 us  [along_x(): lax.ppermute(value, 'x', [(i, (i - steps) % count) for i in range(count)])]
    all_to_all x1, waiting for transfers between devices: 12.9 us -> 4.66 us  [grams(): every = lax.all_to_all(jnp.broadcast_to(total[None], shape), XZ, 0, 0)]
    all_to_all x0 -> x1, waiting for transfers between devices: none -> 8.11 us  [grams(): slices = lax.all_to_all(parts.reshape(shape), XZ, 0, 0)]
    unnamed x28 -> x26, local copies, waits for them, and re-layouts: 10 us -> 2.98 us
    ppermute x10, waiting for transfers between devices: 19.7 us -> 13.8 us  [send(): return lax.ppermute(value, 'y', pairs)]
    dot_general x15 -> x14, matrix products: 11 us -> 7.27 us  [dot(): lax.dot_general(left, right, (((left_dim,), (0,)), ((), ())), preferred_e...]
  transfers between devices with their start and end apart: 25 -> 29, of which waited for: 14 -> 18; matrix products, arithmetic and copies ran while one was open for 9% -> 6% of each run, Pallas kernels for 2% -> 3%
where the time goes in v5:
time: 147 us
  starting transfers between devices  45.5 us (31%)
  waiting for transfers between devices  42.8 us (29%)
  blocking collectives  22.3 us (15%)
  between operations  14.1 us (10%)
  local copies, waits for them, and re-layouts  8.03 us (5%)
  matrix products  7.43 us (5%)
  Pallas kernels  4.25 us (3%)
  other arithmetic  2.26 us (2%)
    all_to_all x1, blocking collectives, body(): parts = lax.all_to_all(doc_sums(left, right, slots, core, rank), XZ, 0, 0)  22.3 us
    ppermute x10, starting transfers between devices, send(): return lax.ppermute(value, 'y', pairs)  16.7 us
    ppermute x10, waiting for transfers between devices, send(): return lax.ppermute(value, 'y', pairs)  13.8 us
    ppermute x9, starting transfers between devices, along_x(): lax.ppermute(value, 'x', [(i, (i - steps) % count) for i in range(count)])  13.2 us
    ppermute x9, waiting for transfers between devices, along_x(): lax.ppermute(value, 'x', [(i, (i - steps) % count) for i in range(count)])  11.5 us
    all_to_all x1, starting transfers between devices, grams(): slices = lax.all_to_all(parts.reshape(shape), XZ, 0, 0)  8.73 us
    all_to_all x1, waiting for transfers between devices, grams(): slices = lax.all_to_all(parts.reshape(shape), XZ, 0, 0)  8.11 us
    dot_general x14, matrix products, dot(): lax.dot_general(left, right, (((left_dim,), (0,)), ((), ())), preferred_e...  7.27 us
  transfers between devices with their start and end apart: 29, of which 18 were waited for; matrix products, arithmetic and copies ran while one was open for 6% of the time, Pallas kernels for 3%

profile of v5, /device:TPU:32, one launch (start us, length us, event | category | flops | bytes accessed | tf_op | source)
XLA Modules:
  0.0 146.7 jit_solution(14336538796988324225)
XLA Ops:
  6.6 3.0 %constant_dynamic-slice_fusion.9 = (bf16[128,2048]{1,0:T(8,128)(2,1)}, bf16[128,2048]{1,0:T(8,128)(2,1)}, bf16[128,2048]{1,0:T(8,128)(2,1)}, bf16[128,2048]{1,0:T(8,128)(2,1)}) fusion(bf16[128,8192]{1,0:T(8,128)(2,1)} %param.11, s32[]{:T(128)S(6)} %select_n.266, s32[]{:T(128)S(6)} %select_n.264, s32[]{:T(128)S(6)} %select_n.262, s32[]{:T(128)S(6)} %select_n.260), kind=kLoop, calls=%fused_computation.100 | loop fusion | bytes 4194320 | tf_op jit(solution)/shard_map/dynamic_slice | solution.py:41
  9.8 1.6 %collective-permute-start = (bf16[64,128]{1,0:T(8,128)(2,1)S(1)}, bf16[64,128]{1,0:T(8,128)(2,1)S(1)}, u32[]{:S(2)}, u32[]{:S(2)}) collective-permute-start(bf16[64,128]{1,0:T(8,128)(2,1)S(1)} %fusion.4), channel_id=1, source_target_pairs={{0,16},{16,32},{32,48},{48,0},{1,17},{17,33},{33,49},{49,1},{2,18}... | collective-permute-start | bytes 49160 | tf_op jit(solution)/shard_map/ppermute | solution.py:46
  11.3 2.7 %collective-permute-start.1 = (bf16[64,128]{1,0:T(8,128)(2,1)S(1)}, bf16[64,128]{1,0:T(8,128)(2,1)S(1)}, u32[]{:S(2)}, u32[]{:S(2)}) collective-permute-start(bf16[64,128]{1,0:T(8,128)(2,1)S(1)} %fusion.4), channel_id=1, source_target_pairs={{0,32},{16,48},{32,0},{48,16},{1,33},{17,49},{33,1},{49,17},{2,34}... | collective-permute-start | bytes 49160 | tf_op jit(solution)/shard_map/ppermute | solution.py:46
  14.1 1.4 collective-permute-start.2
  15.5 1.1 collective-permute-done.1
  16.6 1.2 collective-permute-done.2
  17.8 0.7 maximum_maximum_fusion
  18.6 2.7 %collective-permute-start.10 = (bf16[128,2048]{1,0:T(8,128)(2,1)}, bf16[128,2048]{1,0:T(8,128)(2,1)}, u32[]{:S(2)}, u32[]{:S(2)}) collective-permute-start(bf16[128,2048]{1,0:T(8,128)(2,1)} %get-tuple-element.39), channel_id=1, source_target_pairs={{0,48},{16,0},{32,16},{48,32},{1,49},{17,1},{33,17},{49,33},{2,50}... | collective-permute-start | bytes 1572872 | tf_op jit(solution)/shard_map/ppermute | solution.py:46
  21.4 1.3 collective-permute-start.3
  22.7 0.7 collective-permute-start.4
  23.8 1.3 collective-permute-start.6
  25.1 4.4 %collective-permute-done.3 = bf16[128,512]{1,0:T(8,128)(2,1)S(1)} collective-permute-done((bf16[128,512]{1,0:T(8,128)(2,1)S(1)}, bf16[128,512]{1,0:T(8,128)(2,1)S(1)}, u32[]{:S(2)}, u32[]{:S(2)}) %collective-permute-start.3) | collective-permute-done | bytes 131104 | tf_op jit(solution)/shard_map/ppermute | solution.py:22
  29.5 3.4 %collective-permute-start.7 = (bf16[128,640]{1,0:T(8,128)(2,1)S(1)}, bf16[128,640]{1,0:T(8,128)(2,1)S(1)}, u32[]{:S(2)}, u32[]{:S(2)}) collective-permute-start(bf16[128,640]{1,0:T(8,128)(2,1)S(1)} %pad_maximum_fusion.3), channel_id=1, source_target_pairs={{0,64},{64,128},{128,192},{1,65},{65,129},{129,193},{2,66},{66,130... | collective-permute-start | bytes 491528 | tf_op jit(solution)/shard_map/ppermute | solution.py:22
  33.0 1.6 %collective-permute-start.12 = (bf16[128,2048]{1,0:T(8,128)(2,1)}, bf16[128,2048]{1,0:T(8,128)(2,1)}, u32[]{:S(2)}, u32[]{:S(2)}) collective-permute-start(bf16[128,2048]{1,0:T(8,128)(2,1)} %get-tuple-element.41), channel_id=1, source_target_pairs={{0,32},{16,48},{32,0},{48,16},{1,33},{17,49},{33,1},{49,17},{2,34}... | collective-permute-start | bytes 1572872 | tf_op jit(solution)/shard_map/ppermute | solution.py:46
  34.6 1.1 collective-permute-done.7
  36.5 0.7 collective-permute-done.8
  38.2 1.0 fusion.3
  39.3 6.5 %collective-permute-done.9.one = bf16[128,2048]{1,0:T(8,128)(2,1)} collective-permute-done((bf16[128,2048]{1,0:T(8,128)(2,1)}, bf16[128,2048]{1,0:T(8,128)(2,1)}, u32[]{:S(2)}, u32[]{:S(2)}) %collective-permute-start.9) | collective-permute-done | bytes 524320 | tf_op jit(solution)/shard_map/ppermute | solution.py:46
  45.7 8.7 %all-to-all-start = ((bf16[32,8,640]{2,1,0:T(8,128)(2,1)}), bf16[32,8,640]{2,1,0:T(8,128)(2,1)S(1)}, u32[]{:S(2)}, u32[]{:S(2)}) async-start(bf16[32,8,640]{2,1,0:T(8,128)(2,1)} %bitcast.66), calls=%async_computation | async-start | bytes 655360 | tf_op jit(solution)/shard_map/all_to_all | solution.py:167
  54.5 2.5 %fusion.6 = f32[128,64]{0,1:T(8,128)S(1)} fusion(bf16[128,8192]{1,0:T(8,128)(2,1)} %param.11, bf16[1,8192,64]{1,2,0:T(8,128)(2,1)S(1)} %copy-done), kind=kOutput, calls=%fused_computation.12 | convolution fusion | flops 134217728 | bytes 3178496 | tf_op jit(solution)/shard_map/dot_general | solution.py:16
  57.0 0.8 convolution_convert_fusion.1
  58.5 8.1 %all-to-all-done = bf16[32,8,640]{2,1,0:T(8,128)(2,1)S(1)} async-done(((bf16[32,8,640]{2,1,0:T(8,128)(2,1)}), bf16[32,8,640]{2,1,0:T(8,128)(2,1)S(1)}, u32[]{:S(2)}, u32[]{:S(2)}) %all-to-all-start) | async-done | bytes 327712 | tf_op jit(solution)/shard_map/all_to_all | solution.py:167
  66.6 0.8 broadcast_in_dim.46
  67.4 5.6 %all-to-all-start.1 = ((bf16[32,8,640]{2,1,0:T(8,128)(2,1)}), bf16[32,8,640]{2,1,0:T(8,128)(2,1)S(1)}, u32[]{:S(2)}, u32[]{:S(2)}) async-start(bf16[32,8,640]{2,1,0:T(8,128)(2,1)} %broadcast_in_dim.46), calls=%async_computation.1 | async-start | bytes 655360 | tf_op jit(solution)/shard_map/all_to_all | solution.py:170
  73.0 1.9 %copy-done.2 = bf16[3072,512]{1,0:T(8,128)(2,1)S(1)} copy-done((bf16[3072,512]{1,0:T(8,128)(2,1)S(1)}, bf16[3072,512]{1,0:T(8,128)(2,1)}, u32[]{:S(2)}) %copy-start.2) | copy-done | bytes 3145752
  74.9 1.0 copy-done.3
  76.0 4.3 %shard_map.100 = (bf16[512,512]{1,0:T(8,128)(2,1)S(1)}, bf16[128,64]{1,0:T(8,128)(2,1)S(1)}) custom-call(bf16[128,2048]{1,0:T(8,128)(2,1)S(1)} %copy-done.3, bf16[128,2048]{1,0:T(8,128)(2,1)} %collective-permute-done.9.one, bf16[128,2048]{1,0:T(8,128)(2,1)} %collective-permute-done.12.two, bf16[128,2048]{1,0:T(8,128)(2,1)} %collective-permute-done.10.three, ...), custom_call_target="tpu_custom_call" | custom-call | flops 1207959552 | bytes 7340032 | tf_op jit(solution)/shard_map/pallas_call | solution.py:111
  80.3 4.7 %all-to-all-done.1 = bf16[32,8,640]{2,1,0:T(8,128)(2,1)S(1)} async-done(((bf16[32,8,640]{2,1,0:T(8,128)(2,1)}), bf16[32,8,640]{2,1,0:T(8,128)(2,1)S(1)}, u32[]{:S(2)}, u32[]{:S(2)}) %all-to-all-start.1) | async-done | bytes 327712 | tf_op jit(solution)/shard_map/all_to_all | solution.py:170
  84.9 0.7 collective-permute-start.14
  85.7 4.9 %collective-permute-start.20 = (bf16[256,640]{1,0:T(8,128)(2,1)S(1)}, bf16[256,640]{1,0:T(8,128)(2,1)S(1)}, u32[]{:S(2)}, u32[]{:S(2)}) collective-permute-start(bf16[256,640]{1,0:T(8,128)(2,1)S(1)} %bitcast.54), channel_id=1, source_target_pairs={{0,192},{1,193},{2,194},{3,195},{4,196},{5,197},{6,198},{7,199},{8... | collective-permute-start | bytes 983048 | tf_op jit(solution)/shard_map/ppermute | solution.py:22
  90.5 0.7 collective-permute-start.13
  91.2 1.3 collective-permute-start.17
  92.5 1.5 %collective-permute-start.18 = (bf16[128,512]{1,0:T(8,128)(2,1)S(1)}, bf16[128,512]{1,0:T(8,128)(2,1)S(1)}, u32[]{:S(2)}, u32[]{:S(2)}) collective-permute-start(bf16[128,512]{1,0:T(8,128)(2,1)S(1)} %get-tuple-element.56), channel_id=1, source_target_pairs={{0,32},{16,48},{32,0},{48,16},{1,33},{17,49},{33,1},{49,17},{2,34}... | collective-permute-start | bytes 393224 | tf_op jit(solution)/shard_map/ppermute | solution.py:46
  94.7 1.3 collective-permute-done.15
  96.5 0.7 collective-permute-done.20
  97.7 1.2 collective-permute-done.18
  98.9 1.6 %collective-permute-done.19 = bf16[128,512]{1,0:T(8,128)(2,1)S(1)} collective-permute-done((bf16[128,512]{1,0:T(8,128)(2,1)S(1)}, bf16[128,512]{1,0:T(8,128)(2,1)S(1)}, u32[]{:S(2)}, u32[]{:S(2)}) %collective-permute-start.19) | collective-permute-done | bytes 131104 | tf_op jit(solution)/shard_map/ppermute | solution.py:46
  100.9 1.4 collective-permute-done.21
  102.7 1.3 collective-permute-start.22
  104.0 1.3 collective-permute-start.23
  105.3 1.3 collective-permute-start.24
  106.8 1.7 %collective-permute-done.22 = bf16[128,128]{0,1:T(8,128)(2,1)S(1)} collective-permute-done((bf16[128,128]{0,1:T(8,128)(2,1)S(1)}, bf16[128,128]{0,1:T(8,128)(2,1)S(1)}, u32[]{:S(2)}, u32[]{:S(2)}) %collective-permute-start.22) | collective-permute-done | bytes 32800 | tf_op jit(solution)/shard_map/ppermute | solution.py:22
  108.5 2.8 %collective-permute-done.23 = bf16[128,128]{0,1:T(8,128)(2,1)S(1)} collective-permute-done((bf16[128,128]{0,1:T(8,128)(2,1)S(1)}, bf16[128,128]{0,1:T(8,128)(2,1)S(1)}, u32[]{:S(2)}, u32[]{:S(2)}) %collective-permute-start.23) | collective-permute-done | bytes 32800 | tf_op jit(solution)/shard_map/ppermute | solution.py:22
  111.4 3.1 %collective-permute-done.24 = bf16[128,128]{0,1:T(8,128)(2,1)S(1)} collective-permute-done((bf16[128,128]{0,1:T(8,128)(2,1)S(1)}, bf16[128,128]{0,1:T(8,128)(2,1)S(1)}, u32[]{:S(2)}, u32[]{:S(2)}) %collective-permute-start.24) | collective-permute-done | bytes 32800 | tf_op jit(solution)/shard_map/ppermute | solution.py:22
  114.7 1.2 collective-permute-done.25
  115.9 0.7 fusion
  116.6 22.3 %all_to_all.15 = bf16[32,64,128]{2,1,0:T(8,128)(2,1)S(1)} all-to-all(bf16[32,64,128]{2,1,0:T(8,128)(2,1)S(1)} %fusion.5), channel_id=1, replica_groups=mesh['y'=4,'x'=4,'z'=8,'c'=2] {'x','z'}, dimensions={0} | all-to-all | bytes 1048576 | tf_op jit(solution)/shard_map/all_to_all | solution.py:261
  139.2 0.7 reshape.63
  (103 shorter events, 6.4 us)
Async XLA Ops:
  6.5 14.8 %copy-start = (bf16[1,8192,64]{1,2,0:T(8,128)(2,1)S(1)}, bf16[1,8192,64]{1,2,0:T(8,128)(2,1)}, u32[]{:S(2)}) copy-start(bf16[1,8192,64]{1,2,0:T(8,128)(2,1)} %param.17) | copy-start | bytes 3145732
  6.5 66.5 %all-gather.3.cloned.1.call-start = ((), (), s32[]{:S(2)}) async-start(), calls=%async_computation.3 | async-start | bytes 3342336 | tf_op jit(solution)/shard_map/all_gather | solution.py:228
  6.5 3.0 %copy-start.6 = (bf16[1,128,512]{2,1,0:T(8,128)(2,1)S(1)}, bf16[1,128,512]{2,1,0:T(8,128)(2,1)}, u32[]{:S(2)}) copy-start(bf16[1,128,512]{2,1,0:T(8,128)(2,1)} %param.12) | copy-start | bytes 393220
  6.5 3.0 %copy-start.9 = (bf16[1,512,64]{1,2,0:T(8,128)(2,1)S(1)}, bf16[1,512,64]{1,2,0:T(8,128)(2,1)}, u32[]{:S(2)}) copy-start(bf16[1,512,64]{1,2,0:T(8,128)(2,1)} %param.16) | copy-start | bytes 196612
  6.5 11.3 %copy-start.4 = (bf16[1,128,512]{2,1,0:T(8,128)(2,1)S(1)}, bf16[1,128,512]{2,1,0:T(8,128)(2,1)}, u32[]{:S(2)}) copy-start(bf16[1,128,512]{2,1,0:T(8,128)(2,1)} %param.13) | copy-start | bytes 393220
  6.6 16.9 %copy-start.7 = (bf16[1,512,64]{1,2,0:T(8,128)(2,1)S(1)}, bf16[1,512,64]{1,2,0:T(8,128)(2,1)}, u32[]{:S(2)}) copy-start(bf16[1,512,64]{1,2,0:T(8,128)(2,1)} %param.15) | copy-start | bytes 196612
  9.6 26.8 %copy-start.11 = (s32[64]{0:T(128)S(1)}, s32[64]{0:T(128)}, u32[]{:S(2)}) copy-start(s32[64]{0:T(128)} %param.19) | copy-start | bytes 772
  9.6 26.8 %copy-start.12 = (s32[128]{0:T(128)S(1)}, s32[128]{0:T(128)}, u32[]{:S(2)}) copy-start(s32[128]{0:T(128)} %param.18) | copy-start | bytes 1540
  9.8 5.7 %collective-permute-start = (bf16[64,128]{1,0:T(8,128)(2,1)S(1)}, bf16[64,128]{1,0:T(8,128)(2,1)S(1)}, u32[]{:S(2)}, u32[]{:S(2)}) collective-permute-start(bf16[64,128]{1,0:T(8,128)(2,1)S(1)} %fusion.4), channel_id=1, source_target_pairs={{0,16},{16,32},{32,48},{48,0},{1,17},{17,33},{33,49},{49,1},{2,18}... | collective-permute-start | bytes 49160 | tf_op jit(solution)/shard_map/ppermute | solution.py:46
  11.3 5.2 %collective-permute-start.1 = (bf16[64,128]{1,0:T(8,128)(2,1)S(1)}, bf16[64,128]{1,0:T(8,128)(2,1)S(1)}, u32[]{:S(2)}, u32[]{:S(2)}) collective-permute-start(bf16[64,128]{1,0:T(8,128)(2,1)S(1)} %fusion.4), channel_id=1, source_target_pairs={{0,32},{16,48},{32,0},{48,16},{1,33},{17,49},{33,1},{49,17},{2,34}... | collective-permute-start | bytes 49160 | tf_op jit(solution)/shard_map/ppermute | solution.py:46
  14.1 3.7 %collective-permute-start.2 = (bf16[64,128]{1,0:T(8,128)(2,1)S(1)}, bf16[64,128]{1,0:T(8,128)(2,1)S(1)}, u32[]{:S(2)}, u32[]{:S(2)}) collective-permute-start(bf16[64,128]{1,0:T(8,128)(2,1)S(1)} %fusion.4), channel_id=1, source_target_pairs={{0,48},{16,0},{32,16},{48,32},{1,49},{17,1},{33,17},{49,33},{2,50}... | collective-permute-start | bytes 49160 | tf_op jit(solution)/shard_map/ppermute | solution.py:46
  18.6 20.7 %collective-permute-start.10 = (bf16[128,2048]{1,0:T(8,128)(2,1)}, bf16[128,2048]{1,0:T(8,128)(2,1)}, u32[]{:S(2)}, u32[]{:S(2)}) collective-permute-start(bf16[128,2048]{1,0:T(8,128)(2,1)} %get-tuple-element.39), channel_id=1, source_target_pairs={{0,48},{16,0},{32,16},{48,32},{1,49},{17,1},{33,17},{49,33},{2,50}... | collective-permute-start | bytes 1572872 | tf_op jit(solution)/shard_map/ppermute | solution.py:46
  21.3 24.4 %collective-permute-start.9 = (bf16[128,2048]{1,0:T(8,128)(2,1)}, bf16[128,2048]{1,0:T(8,128)(2,1)}, u32[]{:S(2)}, u32[]{:S(2)}) collective-permute-start(bf16[128,2048]{1,0:T(8,128)(2,1)} %get-tuple-element.38), channel_id=1, source_target_pairs={{0,16},{16,32},{32,48},{48,0},{1,17},{17,33},{33,49},{49,1},{2,18}... | collective-permute-start | bytes 1572872 | tf_op jit(solution)/shard_map/ppermute | solution.py:46
  21.4 8.1 %collective-permute-start.3 = (bf16[128,512]{1,0:T(8,128)(2,1)S(1)}, bf16[128,512]{1,0:T(8,128)(2,1)S(1)}, u32[]{:S(2)}, u32[]{:S(2)}) collective-permute-start(bf16[128,512]{1,0:T(8,128)(2,1)S(1)} %bitcast.63), channel_id=1, source_target_pairs={{192,0},{128,64},{193,1},{129,65},{194,2},{130,66},{195,3},{131,67... | collective-permute-start | bytes 393224 | tf_op jit(solution)/shard_map/ppermute | solution.py:22
  22.7 10.2 %collective-permute-start.4 = (bf16[128,512]{1,0:T(8,128)(2,1)S(1)}, bf16[128,512]{1,0:T(8,128)(2,1)S(1)}, u32[]{:S(2)}, u32[]{:S(2)}) collective-permute-start(bf16[128,512]{1,0:T(8,128)(2,1)S(1)} %bitcast.64), channel_id=1, source_target_pairs={{192,64},{193,65},{194,66},{195,67},{196,68},{197,69},{198,70},{19... | collective-permute-start | bytes 393224 | tf_op jit(solution)/shard_map/ppermute | solution.py:22
  23.8 10.8 %collective-permute-start.6 = (bf16[128,640]{1,0:T(8,128)(2,1)S(1)}, bf16[128,640]{1,0:T(8,128)(2,1)S(1)}, u32[]{:S(2)}, u32[]{:S(2)}) collective-permute-start(bf16[128,640]{1,0:T(8,128)(2,1)S(1)} %pad_maximum_fusion.3), channel_id=1, source_target_pairs={{64,0},{65,1},{66,2},{67,3},{68,4},{69,5},{70,6},{71,7},{72,8},{73... | collective-permute-start | bytes 491528 | tf_op jit(solution)/shard_map/ppermute | solution.py:22
  29.5 6.2 %collective-permute-start.7 = (bf16[128,640]{1,0:T(8,128)(2,1)S(1)}, bf16[128,640]{1,0:T(8,128)(2,1)S(1)}, u32[]{:S(2)}, u32[]{:S(2)}) collective-permute-start(bf16[128,640]{1,0:T(8,128)(2,1)S(1)} %pad_maximum_fusion.3), channel_id=1, source_target_pairs={{0,64},{64,128},{128,192},{1,65},{65,129},{129,193},{2,66},{66,130... | collective-permute-start | bytes 491528 | tf_op jit(solution)/shard_map/ppermute | solution.py:22
  33.0 33.7 %collective-permute-start.12 = (bf16[128,2048]{1,0:T(8,128)(2,1)}, bf16[128,2048]{1,0:T(8,128)(2,1)}, u32[]{:S(2)}, u32[]{:S(2)}) collective-permute-start(bf16[128,2048]{1,0:T(8,128)(2,1)} %get-tuple-element.41), channel_id=1, source_target_pairs={{0,32},{16,48},{32,0},{48,16},{1,33},{17,49},{33,1},{49,17},{2,34}... | collective-permute-start | bytes 1572872 | tf_op jit(solution)/shard_map/ppermute | solution.py:46
  35.7 1.5 %collective-permute-start.8 = (bf16[128,640]{1,0:T(8,128)(2,1)S(1)}, bf16[128,640]{1,0:T(8,128)(2,1)S(1)}, u32[]{:S(2)}, u32[]{:S(2)}) collective-permute-start(bf16[128,640]{1,0:T(8,128)(2,1)S(1)} %broadcast_select_fusion.3), channel_id=1, source_target_pairs={{0,1},{1,0},{2,3},{3,2},{4,5},{5,4},{6,7},{7,6},{8,9},{9,8},{10,11... | collective-permute-start | bytes 491528 | tf_op jit(solution)/shard_map/ppermute | solution.py:26
  35.8 1.7 %collective-permute-start.5 = (bf16[128,768]{1,0:T(8,128)(2,1)S(1)}, bf16[128,768]{1,0:T(8,128)(2,1)S(1)}, u32[]{:S(2)}, u32[]{:S(2)}) collective-permute-start(bf16[128,768]{1,0:T(8,128)(2,1)S(1)} %pad_maximum_fusion.1), channel_id=1, source_target_pairs={{0,1},{1,0},{2,3},{3,2},{4,5},{5,4},{6,7},{7,6},{8,9},{9,8},{10,11... | collective-permute-start | bytes 589832 | tf_op jit(solution)/shard_map/ppermute | solution.py:26
  37.2 20.7 %collective-permute-start.11 = (s32[128]{0:T(128)S(1)}, s32[128]{0:T(128)S(1)}, u32[]{:S(2)}, u32[]{:S(2)}) collective-permute-start(s32[128]{0:T(128)S(1)} %select_reduce_fusion), channel_id=1, source_target_pairs={{0,1},{1,0},{2,3},{3,2},{4,5},{5,4},{6,7},{7,6},{8,9},{9,8},{10,11... | collective-permute-start | bytes 1544 | tf_op jit(solution)/shard_map/ppermute | solution.py:26
  39.3 17.8 %copy-start.1 = (bf16[1,128,8192]{2,1,0:T(8,128)(2,1)S(1)}, bf16[1,128,8192]{2,1,0:T(8,128)(2,1)}, u32[]{:S(2)}) copy-start(bf16[1,128,8192]{2,1,0:T(8,128)(2,1)} %param.10) | copy-start | bytes 6291460
  45.7 20.9 %all-to-all-start = ((bf16[32,8,640]{2,1,0:T(8,128)(2,1)}), bf16[32,8,640]{2,1,0:T(8,128)(2,1)S(1)}, u32[]{:S(2)}, u32[]{:S(2)}) async-start(bf16[32,8,640]{2,1,0:T(8,128)(2,1)} %bitcast.66), calls=%async_computation | async-start | bytes 655360 | tf_op jit(solution)/shard_map/all_to_all | solution.py:167
  54.5 2.6 %copy-start.5 = (bf16[1,8192,64]{1,2,0:T(8,128)(2,1)S(1)}, bf16[1,8192,64]{1,2,0:T(8,128)(2,1)}, u32[]{:S(2)}) copy-start(bf16[1,8192,64]{1,2,0:T(8,128)(2,1)} %param.14) | copy-start | bytes 3145732
  67.4 17.5 %all-to-all-start.1 = ((bf16[32,8,640]{2,1,0:T(8,128)(2,1)}), bf16[32,8,640]{2,1,0:T(8,128)(2,1)S(1)}, u32[]{:S(2)}, u32[]{:S(2)}) async-start(bf16[32,8,640]{2,1,0:T(8,128)(2,1)} %broadcast_in_dim.46), calls=%async_computation.1 | async-start | bytes 655360 | tf_op jit(solution)/shard_map/all_to_all | solution.py:170
  73.0 1.9 %copy-start.2 = (bf16[3072,512]{1,0:T(8,128)(2,1)S(1)}, bf16[3072,512]{1,0:T(8,128)(2,1)}, u32[]{:S(2)}) copy-start(bf16[3072,512]{1,0:T(8,128)(2,1)} %all-gather.3.cloned.1.call-done) | copy-start | bytes 9437188
  74.9 1.0 copy-start.3
  84.9 9.1 %collective-permute-start.14 = (bf16[256,640]{1,0:T(8,128)(2,1)S(1)}, bf16[256,640]{1,0:T(8,128)(2,1)S(1)}, u32[]{:S(2)}, u32[]{:S(2)}) collective-permute-start(bf16[256,640]{1,0:T(8,128)(2,1)S(1)} %bitcast.52), channel_id=1, source_target_pairs={{64,128},{128,192},{65,129},{129,193},{66,130},{130,194},{67,131},... | collective-permute-start | bytes 983048 | tf_op jit(solution)/shard_map/ppermute | solution.py:22
  85.7 11.5 %collective-permute-start.20 = (bf16[256,640]{1,0:T(8,128)(2,1)S(1)}, bf16[256,640]{1,0:T(8,128)(2,1)S(1)}, u32[]{:S(2)}, u32[]{:S(2)}) collective-permute-start(bf16[256,640]{1,0:T(8,128)(2,1)S(1)} %bitcast.54), channel_id=1, source_target_pairs={{0,192},{1,193},{2,194},{3,195},{4,196},{5,197},{6,198},{7,199},{8... | collective-permute-start | bytes 983048 | tf_op jit(solution)/shard_map/ppermute | solution.py:22
  90.5 3.9 %collective-permute-start.13 = (bf16[256,384]{1,0:T(8,128)(2,1)S(1)}, bf16[256,384]{1,0:T(8,128)(2,1)S(1)}, u32[]{:S(2)}, u32[]{:S(2)}) collective-permute-start(bf16[256,384]{1,0:T(8,128)(2,1)S(1)} %slice.107), channel_id=1, source_target_pairs={{64,192},{65,193},{66,194},{67,195},{68,196},{69,197},{70,198},{71... | collective-permute-start | bytes 589832 | tf_op jit(solution)/shard_map/ppermute | solution.py:22
  91.2 6.5 %collective-permute-start.17 = (bf16[128,512]{1,0:T(8,128)(2,1)S(1)}, bf16[128,512]{1,0:T(8,128)(2,1)S(1)}, u32[]{:S(2)}, u32[]{:S(2)}) collective-permute-start(bf16[128,512]{1,0:T(8,128)(2,1)S(1)} %get-tuple-element.55), channel_id=1, source_target_pairs={{0,48},{16,0},{32,16},{48,32},{1,49},{17,1},{33,17},{49,33},{2,50}... | collective-permute-start | bytes 393224 | tf_op jit(solution)/shard_map/ppermute | solution.py:46
  92.5 6.5 %collective-permute-start.18 = (bf16[128,512]{1,0:T(8,128)(2,1)S(1)}, bf16[128,512]{1,0:T(8,128)(2,1)S(1)}, u32[]{:S(2)}, u32[]{:S(2)}) collective-permute-start(bf16[128,512]{1,0:T(8,128)(2,1)S(1)} %get-tuple-element.56), channel_id=1, source_target_pairs={{0,32},{16,48},{32,0},{48,16},{1,33},{17,49},{33,1},{49,17},{2,34}... | collective-permute-start | bytes 393224 | tf_op jit(solution)/shard_map/ppermute | solution.py:46
  94.1 6.4 %collective-permute-start.19 = (bf16[128,512]{1,0:T(8,128)(2,1)S(1)}, bf16[128,512]{1,0:T(8,128)(2,1)S(1)}, u32[]{:S(2)}, u32[]{:S(2)}) collective-permute-start(bf16[128,512]{1,0:T(8,128)(2,1)S(1)} %get-tuple-element.57), channel_id=1, source_target_pairs={{0,16},{16,32},{32,48},{48,0},{1,17},{17,33},{33,49},{49,1},{2,18}... | collective-permute-start | bytes 393224 | tf_op jit(solution)/shard_map/ppermute | solution.py:46
  94.5 1.4 collective-permute-start.15
  96.3 1.4 collective-permute-start.16
  97.6 9.0 %copy-start.8 = (bf16[1,512,64]{1,2,0:T(8,128)(2,1)S(1)}, bf16[1,512,64]{1,2,0:T(8,128)(2,1)}, u32[]{:S(2)}) copy-start(bf16[1,512,64]{1,2,0:T(8,128)(2,1)} %param.15) | copy-start | bytes 196612
  97.7 16.9 %copy-start.10 = (s32[256]{0:T(256)S(1)}, s32[256]{0:T(256)}, u32[]{:S(2)}) copy-start(s32[256]{0:T(256)} %pad_add_fusion) | copy-start | bytes 3076
  100.8 1.5 %collective-permute-start.21 = (bf16[256,384]{1,0:T(8,128)(2,1)S(1)}, bf16[256,384]{1,0:T(8,128)(2,1)S(1)}, u32[]{:S(2)}, u32[]{:S(2)}) collective-permute-start(bf16[256,384]{1,0:T(8,128)(2,1)S(1)} %pad_maximum_fusion.2), channel_id=1, source_target_pairs={{0,1},{1,0},{2,3},{3,2},{4,5},{5,4},{6,7},{7,6},{8,9},{9,8},{10,11... | collective-permute-start | bytes 589832 | tf_op jit(solution)/shard_map/ppermute | solution.py:26
  102.7 5.8 %collective-permute-start.22 = (bf16[128,128]{0,1:T(8,128)(2,1)S(1)}, bf16[128,128]{0,1:T(8,128)(2,1)S(1)}, u32[]{:S(2)}, u32[]{:S(2)}) collective-permute-start(bf16[128,128]{0,1:T(8,128)(2,1)S(1)} %get-tuple-element.83), channel_id=1, source_target_pairs={{64,0},{128,64},{192,128},{65,1},{129,65},{193,129},{66,2},{130,66... | collective-permute-start | bytes 98312 | tf_op jit(solution)/shard_map/ppermute | solution.py:22
  104.0 7.3 %collective-permute-start.23 = (bf16[128,128]{0,1:T(8,128)(2,1)S(1)}, bf16[128,128]{0,1:T(8,128)(2,1)S(1)}, u32[]{:S(2)}, u32[]{:S(2)}) collective-permute-start(bf16[128,128]{0,1:T(8,128)(2,1)S(1)} %get-tuple-element.85), channel_id=1, source_target_pairs={{128,0},{192,64},{129,1},{193,65},{130,2},{194,66},{131,3},{195,67... | collective-permute-start | bytes 98312 | tf_op jit(solution)/shard_map/ppermute | solution.py:22
  105.3 9.1 %collective-permute-start.24 = (bf16[128,128]{0,1:T(8,128)(2,1)S(1)}, bf16[128,128]{0,1:T(8,128)(2,1)S(1)}, u32[]{:S(2)}, u32[]{:S(2)}) collective-permute-start(bf16[128,128]{0,1:T(8,128)(2,1)S(1)} %get-tuple-element.84), channel_id=1, source_target_pairs={{192,0},{193,1},{194,2},{195,3},{196,4},{197,5},{198,6},{199,7},{2... | collective-permute-start | bytes 98312 | tf_op jit(solution)/shard_map/ppermute | solution.py:22
  114.5 1.3 collective-permute-start.25
Sparse Core Ops, SparseCore 0:
  18.7 44.7 all-gather.2

commit v6 on v5

--- a/solution.py
+++ b/solution.py
@@ -192,7 +192,7 @@
     e03 = (f03.astype(F32) + dot(g31, f01_all) + dot(g32, e02_all)).astype(BF16)
     zero = jnp.zeros_like(f01)
     columns = (
-        jnp.where(plane == 1, f01, jnp.where(plane == 2, e02, e03)),
+        jnp.where(plane == 0, zero, jnp.where(plane == 1, f01, jnp.where(plane == 2, e02, e03))),
         jnp.where(plane == 2, f12, jnp.where(plane == 3, e13, zero)),
         jnp.where(plane == 3, f23, zero),
     )
@@ -249,12 +249,10 @@
     spread_e = ordered(spread_e, core)
     upd = (upd.astype(F32) + sum(item.astype(F32) for item in back)).astype(BF16)
     right = jnp.concatenate([dot(upd, p_value_out[0]), direct_out], axis=1)
-    below = dot(upd, spread_e).astype(BF16)
     count = lax.axis_size("y")
-    for k in range(1, count):
-        start = jnp.maximum(plane - k, 0) * 2 * rank
-        item = lax.dynamic_slice_in_dim(below, start, 2 * rank, 1)
-        right = right + send(item, [(i, i - k) for i in range(k, count)]).astype(F32)
+    below = [dot(upd, spread_e[:, 2 * k * rank : 2 * (k + 1) * rank]).astype(BF16) for k in range(count - 1)]
+    below = jnp.stack(below + [jnp.zeros_like(below[0])])
+    right = right + jnp.sum(lax.all_to_all(below, "y", 0, 0).astype(F32), axis=0)
     packed = jnp.concatenate([first_in, second_in, right.astype(BF16)], axis=1)
     packed = jnp.concatenate([packed, swap(packed)], axis=0)
     left, right = packed[:, : 2 * rank], packed[:, 2 * rank :]

time: 147 us -> 146 us (level)
  waiting for transfers between devices: 42.8 us -> 41.1 us
    ppermute x10 -> x7, waiting for transfers between devices: 13.8 us -> 6.18 us  [send(): return lax.ppermute(value, 'y', pairs)]
    all_to_all x0 -> x1, waiting for transfers between devices: none -> 5.81 us  [body(): lax.all_to_all(below, 'y', 0, 0).astype(F32)]
    ppermute x10 -> x7, starting transfers between devices: 16.7 us -> 12.8 us  [send(): return lax.ppermute(value, 'y', pairs)]
    all_to_all x0 -> x1, starting transfers between devices: none -> 3.61 us  [body(): lax.all_to_all(below, 'y', 0, 0).astype(F32)]
    dot_general x14 -> x16, matrix products: 7.27 us -> 7.47 us  [dot(): lax.dot_general(left, right, (((left_dim,), (0,)), ((), ())), preferred_e...]
  transfers between devices with their start and end apart: 29 -> 27, of which waited for: 18 -> 16; matrix products, arithmetic and copies ran while one was open for 6% -> 6% of each run, Pallas kernels for 3% -> 3%
where the time goes in v6:
time: 146 us
  starting transfers between devices  45.2 us (31%)
  waiting for transfers between devices  41.1 us (28%)
  blocking collectives  22.4 us (15%)
  between operations  14.1 us (10%)
  local copies, waits for them, and re-layouts  8.19 us (6%)
  matrix products  7.63 us (5%)
  Pallas kernels  4.25 us (3%)
  other arithmetic  2.98 us (2%)
    all_to_all x1, blocking collectives, body(): parts = lax.all_to_all(doc_sums(left, right, slots, core, rank), XZ, 0, 0)  22.4 us
    ppermute x9, starting transfers between devices, along_x(): lax.ppermute(value, 'x', [(i, (i - steps) % count) for i in range(count)])  13.2 us
    ppermute x7, starting transfers between devices, send(): return lax.ppermute(value, 'y', pairs)  12.8 us
    ppermute x9, waiting for transfers between devices, along_x(): lax.ppermute(value, 'x', [(i, (i - steps) % count) for i in range(count)])  11.6 us
    all_to_all x1, starting transfers between devices, grams(): slices = lax.all_to_all(parts.reshape(shape), XZ, 0, 0)  8.73 us
    all_to_all x1, waiting for transfers between devices, grams(): slices = lax.all_to_all(parts.reshape(shape), XZ, 0, 0)  8.11 us
    dot_general x16, matrix products, dot(): lax.dot_general(left, right, (((left_dim,), (0,)), ((), ())), preferred_e...  7.47 us
    ppermute x7, waiting for transfers between devices, send(): return lax.ppermute(value, 'y', pairs)  6.18 us
  transfers between devices with their start and end apart: 27, of which 16 were waited for; matrix products, arithmetic and copies ran while one was open for 6% of the time, Pallas kernels for 3%

profile of v6, /device:TPU:32, one launch (start us, length us, event | category | flops | bytes accessed | tf_op | source)
XLA Modules:
  0.0 145.7 jit_solution(8106823971397173871)
XLA Ops:
  6.6 3.0 %constant_dynamic-slice_fusion.6 = (bf16[128,2048]{1,0:T(8,128)(2,1)}, bf16[128,2048]{1,0:T(8,128)(2,1)}, bf16[128,2048]{1,0:T(8,128)(2,1)}, bf16[128,2048]{1,0:T(8,128)(2,1)}) fusion(bf16[128,8192]{1,0:T(8,128)(2,1)} %param.11, s32[]{:T(128)S(6)} %select_n.263, s32[]{:T(128)S(6)} %select_n.261, s32[]{:T(128)S(6)} %select_n.259, s32[]{:T(128)S(6)} %select_n.257), kind=kLoop, calls=%fused_computation.108 | loop fusion | bytes 4194320 | tf_op jit(solution)/shard_map/dynamic_slice | solution.py:41
  9.8 1.6 %collective-permute-start = (bf16[64,128]{1,0:T(8,128)(2,1)S(1)}, bf16[64,128]{1,0:T(8,128)(2,1)S(1)}, u32[]{:S(2)}, u32[]{:S(2)}) collective-permute-start(bf16[64,128]{1,0:T(8,128)(2,1)S(1)} %fusion.7), channel_id=1, source_target_pairs={{0,16},{16,32},{32,48},{48,0},{1,17},{17,33},{33,49},{49,1},{2,18}... | collective-permute-start | bytes 49160 | tf_op jit(solution)/shard_map/ppermute | solution.py:46
  11.3 2.7 %collective-permute-start.1 = (bf16[64,128]{1,0:T(8,128)(2,1)S(1)}, bf16[64,128]{1,0:T(8,128)(2,1)S(1)}, u32[]{:S(2)}, u32[]{:S(2)}) collective-permute-start(bf16[64,128]{1,0:T(8,128)(2,1)S(1)} %fusion.7), channel_id=1, source_target_pairs={{0,32},{16,48},{32,0},{48,16},{1,33},{17,49},{33,1},{49,17},{2,34}... | collective-permute-start | bytes 49160 | tf_op jit(solution)/shard_map/ppermute | solution.py:46
  14.1 1.4 collective-permute-start.2
  15.5 1.1 collective-permute-done.1
  16.6 1.2 collective-permute-done.2
  17.8 0.7 maximum_maximum_fusion
  18.6 2.7 %collective-permute-start.10 = (bf16[128,2048]{1,0:T(8,128)(2,1)}, bf16[128,2048]{1,0:T(8,128)(2,1)}, u32[]{:S(2)}, u32[]{:S(2)}) collective-permute-start(bf16[128,2048]{1,0:T(8,128)(2,1)} %get-tuple-element.39), channel_id=1, source_target_pairs={{0,48},{16,0},{32,16},{48,32},{1,49},{17,1},{33,17},{49,33},{2,50}... | collective-permute-start | bytes 1572872 | tf_op jit(solution)/shard_map/ppermute | solution.py:46
  21.4 1.3 collective-permute-start.3
  22.7 0.7 collective-permute-start.4
  23.8 1.3 collective-permute-start.6
  25.1 4.4 %collective-permute-done.3 = bf16[128,512]{1,0:T(8,128)(2,1)S(1)} collective-permute-done((bf16[128,512]{1,0:T(8,128)(2,1)S(1)}, bf16[128,512]{1,0:T(8,128)(2,1)S(1)}, u32[]{:S(2)}, u32[]{:S(2)}) %collective-permute-start.3) | collective-permute-done | bytes 131104 | tf_op jit(solution)/shard_map/ppermute | solution.py:22
  29.5 3.4 %collective-permute-start.7 = (bf16[128,640]{1,0:T(8,128)(2,1)S(1)}, bf16[128,640]{1,0:T(8,128)(2,1)S(1)}, u32[]{:S(2)}, u32[]{:S(2)}) collective-permute-start(bf16[128,640]{1,0:T(8,128)(2,1)S(1)} %pad_maximum_fusion.3), channel_id=1, source_target_pairs={{0,64},{64,128},{128,192},{1,65},{65,129},{129,193},{2,66},{66,130... | collective-permute-start | bytes 491528 | tf_op jit(solution)/shard_map/ppermute | solution.py:22
  33.0 1.6 %collective-permute-start.12 = (bf16[128,2048]{1,0:T(8,128)(2,1)}, bf16[128,2048]{1,0:T(8,128)(2,1)}, u32[]{:S(2)}, u32[]{:S(2)}) collective-permute-start(bf16[128,2048]{1,0:T(8,128)(2,1)} %get-tuple-element.41), channel_id=1, source_target_pairs={{0,32},{16,48},{32,0},{48,16},{1,33},{17,49},{33,1},{49,17},{2,34}... | collective-permute-start | bytes 1572872 | tf_op jit(solution)/shard_map/ppermute | solution.py:46
  34.6 1.1 collective-permute-done.7
  35.8 0.6 collective-permute-start.5
  36.5 0.7 collective-permute-done.8
  38.2 1.0 fusion.3
  39.3 6.5 %collective-permute-done.9.one = bf16[128,2048]{1,0:T(8,128)(2,1)} collective-permute-done((bf16[128,2048]{1,0:T(8,128)(2,1)}, bf16[128,2048]{1,0:T(8,128)(2,1)}, u32[]{:S(2)}, u32[]{:S(2)}) %collective-permute-start.9) | collective-permute-done | bytes 524320 | tf_op jit(solution)/shard_map/ppermute | solution.py:46
  45.7 8.7 %all-to-all-start = ((bf16[32,8,640]{2,1,0:T(8,128)(2,1)}), bf16[32,8,640]{2,1,0:T(8,128)(2,1)S(1)}, u32[]{:S(2)}, u32[]{:S(2)}) async-start(bf16[32,8,640]{2,1,0:T(8,128)(2,1)} %bitcast.75), calls=%async_computation | async-start | bytes 655360 | tf_op jit(solution)/shard_map/all_to_all | solution.py:167
  54.5 2.5 %fusion.9 = f32[128,64]{0,1:T(8,128)S(1)} fusion(bf16[128,8192]{1,0:T(8,128)(2,1)} %param.11, bf16[1,8192,64]{1,2,0:T(8,128)(2,1)S(1)} %copy-done), kind=kOutput, calls=%fused_computation.17 | convolution fusion | flops 134217728 | bytes 3178496 | tf_op jit(solution)/shard_map/dot_general | solution.py:16
  57.0 0.8 convolution_convert_fusion.3
  57.9 0.6 pad_add_fusion
  58.5 8.1 %all-to-all-done = bf16[32,8,640]{2,1,0:T(8,128)(2,1)S(1)} async-done(((bf16[32,8,640]{2,1,0:T(8,128)(2,1)}), bf16[32,8,640]{2,1,0:T(8,128)(2,1)S(1)}, u32[]{:S(2)}, u32[]{:S(2)}) %all-to-all-start) | async-done | bytes 327712 | tf_op jit(solution)/shard_map/all_to_all | solution.py:167
  66.6 0.8 broadcast_in_dim.46
  67.4 5.6 %all-to-all-start.1 = ((bf16[32,8,640]{2,1,0:T(8,128)(2,1)}), bf16[32,8,640]{2,1,0:T(8,128)(2,1)S(1)}, u32[]{:S(2)}, u32[]{:S(2)}) async-start(bf16[32,8,640]{2,1,0:T(8,128)(2,1)} %broadcast_in_dim.46), calls=%async_computation.1 | async-start | bytes 655360 | tf_op jit(solution)/shard_map/all_to_all | solution.py:170
  73.0 1.9 %copy-done.2 = bf16[3072,512]{1,0:T(8,128)(2,1)S(1)} copy-done((bf16[3072,512]{1,0:T(8,128)(2,1)S(1)}, bf16[3072,512]{1,0:T(8,128)(2,1)}, u32[]{:S(2)}) %copy-start.2) | copy-done | bytes 3145752
  74.9 1.0 copy-done.3
  76.0 4.3 %shard_map.100 = (bf16[512,512]{1,0:T(8,128)(2,1)S(1)}, bf16[128,64]{1,0:T(8,128)(2,1)S(1)}) custom-call(bf16[128,2048]{1,0:T(8,128)(2,1)S(1)} %copy-done.3, bf16[128,2048]{1,0:T(8,128)(2,1)} %collective-permute-done.9.one, bf16[128,2048]{1,0:T(8,128)(2,1)} %collective-permute-done.12.two, bf16[128,2048]{1,0:T(8,128)(2,1)} %collective-permute-done.10.three, ...), custom_call_target="tpu_custom_call" | custom-call | flops 1207959552 | bytes 7340032 | tf_op jit(solution)/shard_map/pallas_call | solution.py:111
  80.3 4.7 %all-to-all-done.1 = bf16[32,8,640]{2,1,0:T(8,128)(2,1)S(1)} async-done(((bf16[32,8,640]{2,1,0:T(8,128)(2,1)}), bf16[32,8,640]{2,1,0:T(8,128)(2,1)S(1)}, u32[]{:S(2)}, u32[]{:S(2)}) %all-to-all-start.1) | async-done | bytes 327712 | tf_op jit(solution)/shard_map/all_to_all | solution.py:170
  84.9 0.7 collective-permute-start.14
  85.7 4.8 %collective-permute-start.20 = (bf16[256,640]{1,0:T(8,128)(2,1)S(1)}, bf16[256,640]{1,0:T(8,128)(2,1)S(1)}, u32[]{:S(2)}, u32[]{:S(2)}) collective-permute-start(bf16[256,640]{1,0:T(8,128)(2,1)S(1)} %bitcast.63), channel_id=1, source_target_pairs={{0,192},{1,193},{2,194},{3,195},{4,196},{5,197},{6,198},{7,199},{8... | collective-permute-start | bytes 983048 | tf_op jit(solution)/shard_map/ppermute | solution.py:22
  90.6 0.7 collective-permute-start.13
  91.3 1.3 collective-permute-start.17
  92.5 1.5 %collective-permute-start.18 = (bf16[128,512]{1,0:T(8,128)(2,1)S(1)}, bf16[128,512]{1,0:T(8,128)(2,1)S(1)}, u32[]{:S(2)}, u32[]{:S(2)}) collective-permute-start(bf16[128,512]{1,0:T(8,128)(2,1)S(1)} %get-tuple-element.56), channel_id=1, source_target_pairs={{0,32},{16,48},{32,0},{48,16},{1,33},{17,49},{33,1},{49,17},{2,34}... | collective-permute-start | bytes 393224 | tf_op jit(solution)/shard_map/ppermute | solution.py:46
  94.1 0.3 collective-permute-start.19
  94.7 1.3 collective-permute-done.15
  96.5 0.7 collective-permute-done.20
  97.7 1.2 collective-permute-done.18
  99.0 1.6 %collective-permute-done.19 = bf16[128,512]{1,0:T(8,128)(2,1)S(1)} collective-permute-done((bf16[128,512]{1,0:T(8,128)(2,1)S(1)}, bf16[128,512]{1,0:T(8,128)(2,1)S(1)}, u32[]{:S(2)}, u32[]{:S(2)}) %collective-permute-start.19) | collective-permute-done | bytes 131104 | tf_op jit(solution)/shard_map/ppermute | solution.py:46
  101.0 1.4 collective-permute-done.21
  103.0 0.7 maximum_maximum_fusion.1
  103.7 3.6 %all-to-all-start.2 = ((bf16[4,128,128]{2,1,0:T(8,128)(2,1)}), bf16[4,128,128]{2,1,0:T(8,128)(2,1)S(1)}, u32[]{:S(2)}, u32[]{:S(2)}) async-start(bf16[4,128,128]{2,1,0:T(8,128)(2,1)} %maximum_maximum_fusion.1), calls=%async_computation.2 | async-start | bytes 262144 | tf_op jit(solution)/shard_map/all_to_all | solution.py:255
  107.5 5.8 %all-to-all-done.2 = bf16[4,128,128]{2,1,0:T(8,128)(2,1)S(1)} async-done(((bf16[4,128,128]{2,1,0:T(8,128)(2,1)}), bf16[4,128,128]{2,1,0:T(8,128)(2,1)S(1)}, u32[]{:S(2)}, u32[]{:S(2)}) %all-to-all-start.2) | async-done | bytes 131104 | tf_op jit(solution)/shard_map/all_to_all | solution.py:255
  113.6 1.2 collective-permute-done.22
  114.8 0.7 fusion
  115.6 22.4 %all_to_all.20 = bf16[32,64,128]{2,1,0:T(8,128)(2,1)S(1)} all-to-all(bf16[32,64,128]{2,1,0:T(8,128)(2,1)S(1)} %fusion.8), channel_id=1, replica_groups=mesh['y'=4,'x'=4,'z'=8,'c'=2] {'x','z'}, dimensions={0} | all-to-all | bytes 1048576 | tf_op jit(solution)/shard_map/all_to_all | solution.py:259
  138.2 0.7 reshape.63
  (104 shorter events, 5.3 us)
Async XLA Ops:
  6.5 14.8 %copy-start = (bf16[1,8192,64]{1,2,0:T(8,128)(2,1)S(1)}, bf16[1,8192,64]{1,2,0:T(8,128)(2,1)}, u32[]{:S(2)}) copy-start(bf16[1,8192,64]{1,2,0:T(8,128)(2,1)} %param.17) | copy-start | bytes 3145732
  6.5 66.5 %all-gather.3.cloned.1.call-start = ((), (), s32[]{:S(2)}) async-start(), calls=%async_computation.4 | async-start | bytes 3342336 | tf_op jit(solution)/shard_map/all_gather | solution.py:228
  6.5 3.1 %copy-start.6 = (bf16[1,128,512]{2,1,0:T(8,128)(2,1)S(1)}, bf16[1,128,512]{2,1,0:T(8,128)(2,1)}, u32[]{:S(2)}) copy-start(bf16[1,128,512]{2,1,0:T(8,128)(2,1)} %param.12) | copy-start | bytes 393220
  6.5 3.1 %copy-start.9 = (bf16[1,512,64]{1,2,0:T(8,128)(2,1)S(1)}, bf16[1,512,64]{1,2,0:T(8,128)(2,1)}, u32[]{:S(2)}) copy-start(bf16[1,512,64]{1,2,0:T(8,128)(2,1)} %param.16) | copy-start | bytes 196612
  6.5 11.3 %copy-start.4 = (bf16[1,128,512]{2,1,0:T(8,128)(2,1)S(1)}, bf16[1,128,512]{2,1,0:T(8,128)(2,1)}, u32[]{:S(2)}) copy-start(bf16[1,128,512]{2,1,0:T(8,128)(2,1)} %param.13) | copy-start | bytes 393220
  6.6 16.9 %copy-start.7 = (bf16[1,512,64]{1,2,0:T(8,128)(2,1)S(1)}, bf16[1,512,64]{1,2,0:T(8,128)(2,1)}, u32[]{:S(2)}) copy-start(bf16[1,512,64]{1,2,0:T(8,128)(2,1)} %param.15) | copy-start | bytes 196612
  9.6 26.8 %copy-start.11 = (s32[64]{0:T(128)S(1)}, s32[64]{0:T(128)}, u32[]{:S(2)}) copy-start(s32[64]{0:T(128)} %param.19) | copy-start | bytes 772
  9.6 26.8 %copy-start.12 = (s32[128]{0:T(128)S(1)}, s32[128]{0:T(128)}, u32[]{:S(2)}) copy-start(s32[128]{0:T(128)} %param.18) | copy-start | bytes 1540
  9.8 5.7 %collective-permute-start = (bf16[64,128]{1,0:T(8,128)(2,1)S(1)}, bf16[64,128]{1,0:T(8,128)(2,1)S(1)}, u32[]{:S(2)}, u32[]{:S(2)}) collective-permute-start(bf16[64,128]{1,0:T(8,128)(2,1)S(1)} %fusion.7), channel_id=1, source_target_pairs={{0,16},{16,32},{32,48},{48,0},{1,17},{17,33},{33,49},{49,1},{2,18}... | collective-permute-start | bytes 49160 | tf_op jit(solution)/shard_map/ppermute | solution.py:46
  11.3 5.2 %collective-permute-start.1 = (bf16[64,128]{1,0:T(8,128)(2,1)S(1)}, bf16[64,128]{1,0:T(8,128)(2,1)S(1)}, u32[]{:S(2)}, u32[]{:S(2)}) collective-permute-start(bf16[64,128]{1,0:T(8,128)(2,1)S(1)} %fusion.7), channel_id=1, source_target_pairs={{0,32},{16,48},{32,0},{48,16},{1,33},{17,49},{33,1},{49,17},{2,34}... | collective-permute-start | bytes 49160 | tf_op jit(solution)/shard_map/ppermute | solution.py:46
  14.1 3.7 %collective-permute-start.2 = (bf16[64,128]{1,0:T(8,128)(2,1)S(1)}, bf16[64,128]{1,0:T(8,128)(2,1)S(1)}, u32[]{:S(2)}, u32[]{:S(2)}) collective-permute-start(bf16[64,128]{1,0:T(8,128)(2,1)S(1)} %fusion.7), channel_id=1, source_target_pairs={{0,48},{16,0},{32,16},{48,32},{1,49},{17,1},{33,17},{49,33},{2,50}... | collective-permute-start | bytes 49160 | tf_op jit(solution)/shard_map/ppermute | solution.py:46
  18.6 20.7 %collective-permute-start.10 = (bf16[128,2048]{1,0:T(8,128)(2,1)}, bf16[128,2048]{1,0:T(8,128)(2,1)}, u32[]{:S(2)}, u32[]{:S(2)}) collective-permute-start(bf16[128,2048]{1,0:T(8,128)(2,1)} %get-tuple-element.39), channel_id=1, source_target_pairs={{0,48},{16,0},{32,16},{48,32},{1,49},{17,1},{33,17},{49,33},{2,50}... | collective-permute-start | bytes 1572872 | tf_op jit(solution)/shard_map/ppermute | solution.py:46
  21.3 24.4 %collective-permute-start.9 = (bf16[128,2048]{1,0:T(8,128)(2,1)}, bf16[128,2048]{1,0:T(8,128)(2,1)}, u32[]{:S(2)}, u32[]{:S(2)}) collective-permute-start(bf16[128,2048]{1,0:T(8,128)(2,1)} %get-tuple-element.38), channel_id=1, source_target_pairs={{0,16},{16,32},{32,48},{48,0},{1,17},{17,33},{33,49},{49,1},{2,18}... | collective-permute-start | bytes 1572872 | tf_op jit(solution)/shard_map/ppermute | solution.py:46
  21.4 8.1 %collective-permute-start.3 = (bf16[128,512]{1,0:T(8,128)(2,1)S(1)}, bf16[128,512]{1,0:T(8,128)(2,1)S(1)}, u32[]{:S(2)}, u32[]{:S(2)}) collective-permute-start(bf16[128,512]{1,0:T(8,128)(2,1)S(1)} %bitcast.72), channel_id=1, source_target_pairs={{192,0},{128,64},{193,1},{129,65},{194,2},{130,66},{195,3},{131,67... | collective-permute-start | bytes 393224 | tf_op jit(solution)/shard_map/ppermute | solution.py:22
  22.7 10.2 %collective-permute-start.4 = (bf16[128,512]{1,0:T(8,128)(2,1)S(1)}, bf16[128,512]{1,0:T(8,128)(2,1)S(1)}, u32[]{:S(2)}, u32[]{:S(2)}) collective-permute-start(bf16[128,512]{1,0:T(8,128)(2,1)S(1)} %bitcast.73), channel_id=1, source_target_pairs={{192,64},{193,65},{194,66},{195,67},{196,68},{197,69},{198,70},{19... | collective-permute-start | bytes 393224 | tf_op jit(solution)/shard_map/ppermute | solution.py:22
  23.8 10.8 %collective-permute-start.6 = (bf16[128,640]{1,0:T(8,128)(2,1)S(1)}, bf16[128,640]{1,0:T(8,128)(2,1)S(1)}, u32[]{:S(2)}, u32[]{:S(2)}) collective-permute-start(bf16[128,640]{1,0:T(8,128)(2,1)S(1)} %pad_maximum_fusion.3), channel_id=1, source_target_pairs={{64,0},{65,1},{66,2},{67,3},{68,4},{69,5},{70,6},{71,7},{72,8},{73... | collective-permute-start | bytes 491528 | tf_op jit(solution)/shard_map/ppermute | solution.py:22
  29.5 6.2 %collective-permute-start.7 = (bf16[128,640]{1,0:T(8,128)(2,1)S(1)}, bf16[128,640]{1,0:T(8,128)(2,1)S(1)}, u32[]{:S(2)}, u32[]{:S(2)}) collective-permute-start(bf16[128,640]{1,0:T(8,128)(2,1)S(1)} %pad_maximum_fusion.3), channel_id=1, source_target_pairs={{0,64},{64,128},{128,192},{1,65},{65,129},{129,193},{2,66},{66,130... | collective-permute-start | bytes 491528 | tf_op jit(solution)/shard_map/ppermute | solution.py:22
  33.0 33.7 %collective-permute-start.12 = (bf16[128,2048]{1,0:T(8,128)(2,1)}, bf16[128,2048]{1,0:T(8,128)(2,1)}, u32[]{:S(2)}, u32[]{:S(2)}) collective-permute-start(bf16[128,2048]{1,0:T(8,128)(2,1)} %get-tuple-element.41), channel_id=1, source_target_pairs={{0,32},{16,48},{32,0},{48,16},{1,33},{17,49},{33,1},{49,17},{2,34}... | collective-permute-start | bytes 1572872 | tf_op jit(solution)/shard_map/ppermute | solution.py:46
  35.7 1.5 %collective-permute-start.8 = (bf16[128,640]{1,0:T(8,128)(2,1)S(1)}, bf16[128,640]{1,0:T(8,128)(2,1)S(1)}, u32[]{:S(2)}, u32[]{:S(2)}) collective-permute-start(bf16[128,640]{1,0:T(8,128)(2,1)S(1)} %broadcast_select_fusion.3), channel_id=1, source_target_pairs={{0,1},{1,0},{2,3},{3,2},{4,5},{5,4},{6,7},{7,6},{8,9},{9,8},{10,11... | collective-permute-start | bytes 491528 | tf_op jit(solution)/shard_map/ppermute | solution.py:26
  35.8 1.7 %collective-permute-start.5 = (bf16[128,768]{1,0:T(8,128)(2,1)S(1)}, bf16[128,768]{1,0:T(8,128)(2,1)S(1)}, u32[]{:S(2)}, u32[]{:S(2)}) collective-permute-start(bf16[128,768]{1,0:T(8,128)(2,1)S(1)} %pad_maximum_fusion.1), channel_id=1, source_target_pairs={{0,1},{1,0},{2,3},{3,2},{4,5},{5,4},{6,7},{7,6},{8,9},{9,8},{10,11... | collective-permute-start | bytes 589832 | tf_op jit(solution)/shard_map/ppermute | solution.py:26
  37.2 20.7 %collective-permute-start.11 = (s32[128]{0:T(128)S(1)}, s32[128]{0:T(128)S(1)}, u32[]{:S(2)}, u32[]{:S(2)}) collective-permute-start(s32[128]{0:T(128)S(1)} %select_reduce_fusion), channel_id=1, source_target_pairs={{0,1},{1,0},{2,3},{3,2},{4,5},{5,4},{6,7},{7,6},{8,9},{9,8},{10,11... | collective-permute-start | bytes 1544 | tf_op jit(solution)/shard_map/ppermute | solution.py:26
  39.2 17.8 %copy-start.1 = (bf16[1,128,8192]{2,1,0:T(8,128)(2,1)S(1)}, bf16[1,128,8192]{2,1,0:T(8,128)(2,1)}, u32[]{:S(2)}) copy-start(bf16[1,128,8192]{2,1,0:T(8,128)(2,1)} %param.10) | copy-start | bytes 6291460
  45.7 20.9 %all-to-all-start = ((bf16[32,8,640]{2,1,0:T(8,128)(2,1)}), bf16[32,8,640]{2,1,0:T(8,128)(2,1)S(1)}, u32[]{:S(2)}, u32[]{:S(2)}) async-start(bf16[32,8,640]{2,1,0:T(8,128)(2,1)} %bitcast.75), calls=%async_computation | async-start | bytes 655360 | tf_op jit(solution)/shard_map/all_to_all | solution.py:167
  54.5 2.6 %copy-start.5 = (bf16[1,8192,64]{1,2,0:T(8,128)(2,1)S(1)}, bf16[1,8192,64]{1,2,0:T(8,128)(2,1)}, u32[]{:S(2)}) copy-start(bf16[1,8192,64]{1,2,0:T(8,128)(2,1)} %param.14) | copy-start | bytes 3145732
  67.4 17.5 %all-to-all-start.1 = ((bf16[32,8,640]{2,1,0:T(8,128)(2,1)}), bf16[32,8,640]{2,1,0:T(8,128)(2,1)S(1)}, u32[]{:S(2)}, u32[]{:S(2)}) async-start(bf16[32,8,640]{2,1,0:T(8,128)(2,1)} %broadcast_in_dim.46), calls=%async_computation.1 | async-start | bytes 655360 | tf_op jit(solution)/shard_map/all_to_all | solution.py:170
  73.0 1.9 %copy-start.2 = (bf16[3072,512]{1,0:T(8,128)(2,1)S(1)}, bf16[3072,512]{1,0:T(8,128)(2,1)}, u32[]{:S(2)}) copy-start(bf16[3072,512]{1,0:T(8,128)(2,1)} %all-gather.3.cloned.1.call-done) | copy-start | bytes 9437188
  74.9 1.0 copy-start.3
  84.9 9.2 %collective-permute-start.14 = (bf16[256,640]{1,0:T(8,128)(2,1)S(1)}, bf16[256,640]{1,0:T(8,128)(2,1)S(1)}, u32[]{:S(2)}, u32[]{:S(2)}) collective-permute-start(bf16[256,640]{1,0:T(8,128)(2,1)S(1)} %bitcast.61), channel_id=1, source_target_pairs={{64,128},{128,192},{65,129},{129,193},{66,130},{130,194},{67,131},... | collective-permute-start | bytes 983048 | tf_op jit(solution)/shard_map/ppermute | solution.py:22
  85.7 11.5 %collective-permute-start.20 = (bf16[256,640]{1,0:T(8,128)(2,1)S(1)}, bf16[256,640]{1,0:T(8,128)(2,1)S(1)}, u32[]{:S(2)}, u32[]{:S(2)}) collective-permute-start(bf16[256,640]{1,0:T(8,128)(2,1)S(1)} %bitcast.63), channel_id=1, source_target_pairs={{0,192},{1,193},{2,194},{3,195},{4,196},{5,197},{6,198},{7,199},{8... | collective-permute-start | bytes 983048 | tf_op jit(solution)/shard_map/ppermute | solution.py:22
  90.6 3.9 %collective-permute-start.13 = (bf16[256,384]{1,0:T(8,128)(2,1)S(1)}, bf16[256,384]{1,0:T(8,128)(2,1)S(1)}, u32[]{:S(2)}, u32[]{:S(2)}) collective-permute-start(bf16[256,384]{1,0:T(8,128)(2,1)S(1)} %slice.119), channel_id=1, source_target_pairs={{64,192},{65,193},{66,194},{67,195},{68,196},{69,197},{70,198},{71... | collective-permute-start | bytes 589832 | tf_op jit(solution)/shard_map/ppermute | solution.py:22
  91.3 6.5 %collective-permute-start.17 = (bf16[128,512]{1,0:T(8,128)(2,1)S(1)}, bf16[128,512]{1,0:T(8,128)(2,1)S(1)}, u32[]{:S(2)}, u32[]{:S(2)}) collective-permute-start(bf16[128,512]{1,0:T(8,128)(2,1)S(1)} %get-tuple-element.55), channel_id=1, source_target_pairs={{0,48},{16,0},{32,16},{48,32},{1,49},{17,1},{33,17},{49,33},{2,50}... | collective-permute-start | bytes 393224 | tf_op jit(solution)/shard_map/ppermute | solution.py:46
  92.5 6.5 %collective-permute-start.18 = (bf16[128,512]{1,0:T(8,128)(2,1)S(1)}, bf16[128,512]{1,0:T(8,128)(2,1)S(1)}, u32[]{:S(2)}, u32[]{:S(2)}) collective-permute-start(bf16[128,512]{1,0:T(8,128)(2,1)S(1)} %get-tuple-element.56), channel_id=1, source_target_pairs={{0,32},{16,48},{32,0},{48,16},{1,33},{17,49},{33,1},{49,17},{2,34}... | collective-permute-start | bytes 393224 | tf_op jit(solution)/shard_map/ppermute | solution.py:46
  94.1 6.4 %collective-permute-start.19 = (bf16[128,512]{1,0:T(8,128)(2,1)S(1)}, bf16[128,512]{1,0:T(8,128)(2,1)S(1)}, u32[]{:S(2)}, u32[]{:S(2)}) collective-permute-start(bf16[128,512]{1,0:T(8,128)(2,1)S(1)} %get-tuple-element.57), channel_id=1, source_target_pairs={{0,16},{16,32},{32,48},{48,0},{1,17},{17,33},{33,49},{49,1},{2,18}... | collective-permute-start | bytes 393224 | tf_op jit(solution)/shard_map/ppermute | solution.py:46
  94.6 1.4 collective-permute-start.15
  96.3 1.4 collective-permute-start.16
  100.8 6.6 %copy-start.8 = (bf16[1,512,64]{1,2,0:T(8,128)(2,1)S(1)}, bf16[1,512,64]{1,2,0:T(8,128)(2,1)}, u32[]{:S(2)}) copy-start(bf16[1,512,64]{1,2,0:T(8,128)(2,1)} %param.15) | copy-start | bytes 196612
  100.8 12.7 %copy-start.10 = (s32[256]{0:T(256)S(1)}, s32[256]{0:T(256)}, u32[]{:S(2)}) copy-start(s32[256]{0:T(256)} %pad_add_fusion) | copy-start | bytes 3076
  100.8 1.5 %collective-permute-start.21 = (bf16[256,384]{1,0:T(8,128)(2,1)S(1)}, bf16[256,384]{1,0:T(8,128)(2,1)S(1)}, u32[]{:S(2)}, u32[]{:S(2)}) collective-permute-start(bf16[256,384]{1,0:T(8,128)(2,1)S(1)} %pad_maximum_fusion.2), channel_id=1, source_target_pairs={{0,1},{1,0},{2,3},{3,2},{4,5},{5,4},{6,7},{7,6},{8,9},{9,8},{10,11... | collective-permute-start | bytes 589832 | tf_op jit(solution)/shard_map/ppermute | solution.py:26
  103.7 9.6 %all-to-all-start.2 = ((bf16[4,128,128]{2,1,0:T(8,128)(2,1)}), bf16[4,128,128]{2,1,0:T(8,128)(2,1)S(1)}, u32[]{:S(2)}, u32[]{:S(2)}) async-start(bf16[4,128,128]{2,1,0:T(8,128)(2,1)} %maximum_maximum_fusion.1), calls=%async_computation.2 | async-start | bytes 262144 | tf_op jit(solution)/shard_map/all_to_all | solution.py:255
  113.4 1.3 collective-permute-start.22
Sparse Core Ops, SparseCore 0:
  18.7 44.7 all-gather.2

commit v7 on v6

--- a/solution.py
+++ b/solution.py
@@ -138,7 +138,7 @@
 
 
 def exchanged(items):
-    return [items[0]] + [along_x(items[k], -k) for k in range(1, len(items))]
+    return [along_x(item, -k - 1) for k, item in enumerate(items)]
 
 
 def together(value, others):
@@ -220,7 +220,7 @@
     documents = owner_slot.shape[0]
 
     places, place = lax.axis_size("x"), lax.axis_index("x")
-    items = [quarter_of(cotangent, place + k, places) for k in range(places)]
+    items = [quarter_of(cotangent, place + k, places) for k in range(1, places)]
     wv, items = together(wv, items)
     moved = exchanged(items)
     mixed = packed_rows(wo, wv, p_value_in[0])
@@ -233,15 +233,15 @@
     direct_out = dot(cotangent, p_out[0])
     out_rows = lax.dynamic_slice_in_dim(p_out[0], device * rows, rows, 0)
     right_rows = jnp.concatenate([wo, dot(wo, p_value_out[0]).astype(BF16), out_rows], axis=1)
-    early = [first_in, direct_out, jnp.concatenate([slots, swap(slots)]), moved[2]]
+    early = [first_in, direct_out, jnp.concatenate([slots, swap(slots)]), moved[1]]
 
     def work(near, early):
         tokens = acts.shape[0]
-        parts, value = products([near[0], near[1], early[3], near[2]], acts, full)
+        parts, value = products([quarter_of(near[0], place, places), near[1], early[3], near[2]], acts, full)
         return [value] + [parts[k * tokens : (k + 1) * tokens] for k in range(places)]
 
     half, early, done = grams(
-        wv, right_rows, plane, core, [moved[0], moved[1], moved[3]], early, work
+        wv, right_rows, plane, core, [cotangent, moved[0], moved[2]], early, work
     )
     first_in, direct_out, slots, far = early
     second_in, upd = done[0], done[1]

time: 146 us -> 148 us (1.014)
  waiting for transfers between devices: 41.1 us -> 39.1 us
  blocking collectives: 22.4 us -> 24.3 us
  local copies, waits for them, and re-layouts: 8.19 us -> 9.83 us
    all_to_all x1, waiting for transfers between devices: 4.66 us -> 2.75 us  [grams(): every = lax.all_to_all(jnp.broadcast_to(total[None], shape), XZ, 0, 0)]
    all_to_all x1, blocking collectives: 22.4 us -> 24.3 us  [body(): parts = lax.all_to_all(doc_sums(left, right, slots, core, rank), XZ, 0, 0)]
    dynamic_slice x1 -> x2, local copies, waits for them, and re-layouts: 3.02 us -> 4.66 us  [quarter_of(): return lax.dynamic_slice_in_dim(value, place % count * width, width, 1)]
  transfers between devices with their start and end apart: 27 -> 27, of which waited for: 16 -> 16; matrix products, arithmetic and copies ran while one was open for 6% -> 7% of each run, Pallas kernels for 3% -> 3%
where the time goes in v7:
time: 148 us; the launch traced here: 147 us
  starting transfers between devices  45.2 us (31%)
  waiting for transfers between devices  39.1 us (26%)
  blocking collectives  24.3 us (16%)
  between operations  14.1 us (10%)
  local copies, waits for them, and re-layouts  9.83 us (7%)
  matrix products  7.64 us (5%)
  Pallas kernels  4.25 us (3%)
  other arithmetic  2.99 us (2%)
    all_to_all x1, blocking collectives, body(): parts = lax.all_to_all(doc_sums(left, right, slots, core, rank), XZ, 0, 0)  24.3 us
    ppermute x9, starting transfers between devices, along_x(): lax.ppermute(value, 'x', [(i, (i - steps) % count) for i in range(count)])  13.2 us
    ppermute x7, starting transfers between devices, send(): return lax.ppermute(value, 'y', pairs)  12.8 us
    ppermute x9, waiting for transfers between devices, along_x(): lax.ppermute(value, 'x', [(i, (i - steps) % count) for i in range(count)])  11.6 us
    all_to_all x1, starting transfers between devices, grams(): slices = lax.all_to_all(parts.reshape(shape), XZ, 0, 0)  8.73 us
    all_to_all x1, waiting for transfers between devices, grams(): slices = lax.all_to_all(parts.reshape(shape), XZ, 0, 0)  8.14 us
    dot_general x16, matrix products, dot(): lax.dot_general(left, right, (((left_dim,), (0,)), ((), ())), preferred_e...  7.48 us
    ppermute x7, waiting for transfers between devices, send(): return lax.ppermute(value, 'y', pairs)  6.18 us
  transfers between devices with their start and end apart: 27, of which 16 were waited for; matrix products, arithmetic and copies ran while one was open for 7% of the time, Pallas kernels for 3%

profile of v7, /device:TPU:32, one launch (start us, length us, event | category | flops | bytes accessed | tf_op | source)
XLA Modules:
  0.0 147.4 jit_solution(11000687128688539239)
XLA Ops:
  6.6 2.7 %constant_dynamic-slice_fusion.7 = (bf16[128,2048]{1,0:T(8,128)(2,1)}, bf16[128,2048]{1,0:T(8,128)(2,1)}, bf16[128,2048]{1,0:T(8,128)(2,1)}) fusion(bf16[128,8192]{1,0:T(8,128)(2,1)} %param.11, s32[]{:T(128)S(6)} %select_n.261, s32[]{:T(128)S(6)} %select_n.259, s32[]{:T(128)S(6)} %select_n.257), kind=kLoop, calls=%fused_computation.109 | loop fusion | bytes 3145740 | tf_op jit(solution)/shard_map/dynamic_slice | solution.py:41
  9.6 1.6 %collective-permute-start = (bf16[64,128]{1,0:T(8,128)(2,1)S(1)}, bf16[64,128]{1,0:T(8,128)(2,1)S(1)}, u32[]{:S(2)}, u32[]{:S(2)}) collective-permute-start(bf16[64,128]{1,0:T(8,128)(2,1)S(1)} %fusion.7), channel_id=1, source_target_pairs={{0,16},{16,32},{32,48},{48,0},{1,17},{17,33},{33,49},{49,1},{2,18}... | collective-permute-start | bytes 49160 | tf_op jit(solution)/shard_map/ppermute | solution.py:46
  11.1 2.7 %collective-permute-start.1 = (bf16[64,128]{1,0:T(8,128)(2,1)S(1)}, bf16[64,128]{1,0:T(8,128)(2,1)S(1)}, u32[]{:S(2)}, u32[]{:S(2)}) collective-permute-start(bf16[64,128]{1,0:T(8,128)(2,1)S(1)} %fusion.7), channel_id=1, source_target_pairs={{0,32},{16,48},{32,0},{48,16},{1,33},{17,49},{33,1},{49,17},{2,34}... | collective-permute-start | bytes 49160 | tf_op jit(solution)/shard_map/ppermute | solution.py:46
  13.9 1.4 collective-permute-start.2
  15.3 1.1 collective-permute-done.1
  16.4 1.2 collective-permute-done.2
  17.6 0.7 maximum_maximum_fusion
  18.4 2.7 %collective-permute-start.10 = (bf16[128,2048]{1,0:T(8,128)(2,1)}, bf16[128,2048]{1,0:T(8,128)(2,1)}, u32[]{:S(2)}, u32[]{:S(2)}) collective-permute-start(bf16[128,2048]{1,0:T(8,128)(2,1)} %get-tuple-element.37), channel_id=1, source_target_pairs={{0,48},{16,0},{32,16},{48,32},{1,49},{17,1},{33,17},{49,33},{2,50}... | collective-permute-start | bytes 1572872 | tf_op jit(solution)/shard_map/ppermute | solution.py:46
  21.2 1.3 collective-permute-start.3
  22.5 0.7 collective-permute-start.4
  23.6 1.3 collective-permute-start.6
  24.9 4.4 %collective-permute-done.3 = bf16[128,512]{1,0:T(8,128)(2,1)S(1)} collective-permute-done((bf16[128,512]{1,0:T(8,128)(2,1)S(1)}, bf16[128,512]{1,0:T(8,128)(2,1)S(1)}, u32[]{:S(2)}, u32[]{:S(2)}) %collective-permute-start.3) | collective-permute-done | bytes 131104 | tf_op jit(solution)/shard_map/ppermute | solution.py:22
  29.3 3.4 %collective-permute-start.7 = (bf16[128,640]{1,0:T(8,128)(2,1)S(1)}, bf16[128,640]{1,0:T(8,128)(2,1)S(1)}, u32[]{:S(2)}, u32[]{:S(2)}) collective-permute-start(bf16[128,640]{1,0:T(8,128)(2,1)S(1)} %pad_maximum_fusion.3), channel_id=1, source_target_pairs={{0,64},{64,128},{128,192},{1,65},{65,129},{129,193},{2,66},{66,130... | collective-permute-start | bytes 491528 | tf_op jit(solution)/shard_map/ppermute | solution.py:22
  32.8 1.6 %collective-permute-start.12 = (bf16[128,2048]{1,0:T(8,128)(2,1)}, bf16[128,2048]{1,0:T(8,128)(2,1)}, u32[]{:S(2)}, u32[]{:S(2)}) collective-permute-start(bf16[128,2048]{1,0:T(8,128)(2,1)} %get-tuple-element.39), channel_id=1, source_target_pairs={{0,32},{16,48},{32,0},{48,16},{1,33},{17,49},{33,1},{49,17},{2,34}... | collective-permute-start | bytes 1572872 | tf_op jit(solution)/shard_map/ppermute | solution.py:46
  34.4 1.1 collective-permute-done.7
  35.6 0.6 collective-permute-start.5
  36.3 0.7 collective-permute-done.8
  38.0 1.0 fusion.3
  39.1 6.4 %collective-permute-done.9.one = bf16[128,2048]{1,0:T(8,128)(2,1)} collective-permute-done((bf16[128,2048]{1,0:T(8,128)(2,1)}, bf16[128,2048]{1,0:T(8,128)(2,1)}, u32[]{:S(2)}, u32[]{:S(2)}) %collective-permute-start.9) | collective-permute-done | bytes 524320 | tf_op jit(solution)/shard_map/ppermute | solution.py:46
  45.5 8.7 %all-to-all-start = ((bf16[32,8,640]{2,1,0:T(8,128)(2,1)}), bf16[32,8,640]{2,1,0:T(8,128)(2,1)S(1)}, u32[]{:S(2)}, u32[]{:S(2)}) async-start(bf16[32,8,640]{2,1,0:T(8,128)(2,1)} %bitcast.75), calls=%async_computation | async-start | bytes 655360 | tf_op jit(solution)/shard_map/all_to_all | solution.py:167
  54.3 2.5 %fusion.9 = f32[128,64]{0,1:T(8,128)S(1)} fusion(bf16[128,8192]{1,0:T(8,128)(2,1)} %param.11, bf16[1,8192,64]{1,2,0:T(8,128)(2,1)S(1)} %copy-done), kind=kOutput, calls=%fused_computation.17 | convolution fusion | flops 134217728 | bytes 3178496 | tf_op jit(solution)/shard_map/dot_general | solution.py:16
  56.8 0.8 convolution_convert_fusion.3
  57.7 0.6 pad_add_fusion
  58.3 8.1 %all-to-all-done = bf16[32,8,640]{2,1,0:T(8,128)(2,1)S(1)} async-done(((bf16[32,8,640]{2,1,0:T(8,128)(2,1)}), bf16[32,8,640]{2,1,0:T(8,128)(2,1)S(1)}, u32[]{:S(2)}, u32[]{:S(2)}) %all-to-all-start) | async-done | bytes 327712 | tf_op jit(solution)/shard_map/all_to_all | solution.py:167
  66.5 0.8 broadcast_in_dim.46
  67.2 5.6 %all-to-all-start.1 = ((bf16[32,8,640]{2,1,0:T(8,128)(2,1)}), bf16[32,8,640]{2,1,0:T(8,128)(2,1)S(1)}, u32[]{:S(2)}, u32[]{:S(2)}) async-start(bf16[32,8,640]{2,1,0:T(8,128)(2,1)} %broadcast_in_dim.46), calls=%async_computation.1 | async-start | bytes 655360 | tf_op jit(solution)/shard_map/all_to_all | solution.py:170
  72.8 1.9 %constant_dynamic-slice_fusion.near = bf16[128,2048]{1,0:T(8,128)(2,1)} fusion(bf16[128,8192]{1,0:T(8,128)(2,1)} %param.11, s32[]{:T(128)S(6)} %select_n.299), kind=kLoop, calls=%fused_computation.102 | loop fusion | bytes 1048580 | tf_op jit(solution)/shard_map/dynamic_slice | solution.py:41
  74.8 1.9 %copy-done.2 = bf16[3072,512]{1,0:T(8,128)(2,1)S(1)} copy-done((bf16[3072,512]{1,0:T(8,128)(2,1)S(1)}, bf16[3072,512]{1,0:T(8,128)(2,1)}, u32[]{:S(2)}) %copy-start.2) | copy-done | bytes 3145752
  76.6 1.0 copy-done.3
  77.7 4.2 %shard_map.100 = (bf16[512,512]{1,0:T(8,128)(2,1)S(1)}, bf16[128,64]{1,0:T(8,128)(2,1)S(1)}) custom-call(bf16[128,2048]{1,0:T(8,128)(2,1)S(1)} %copy-done.3, bf16[128,2048]{1,0:T(8,128)(2,1)} %collective-permute-done.9.one, bf16[128,2048]{1,0:T(8,128)(2,1)} %collective-permute-done.12.two, bf16[128,2048]{1,0:T(8,128)(2,1)} %collective-permute-done.10.three, ...), custom_call_target="tpu_custom_call" | custom-call | flops 1207959552 | bytes 7340032 | tf_op jit(solution)/shard_map/pallas_call | solution.py:111
  82.0 2.8 %all-to-all-done.1 = bf16[32,8,640]{2,1,0:T(8,128)(2,1)S(1)} async-done(((bf16[32,8,640]{2,1,0:T(8,128)(2,1)}), bf16[32,8,640]{2,1,0:T(8,128)(2,1)S(1)}, u32[]{:S(2)}, u32[]{:S(2)}) %all-to-all-start.1) | async-done | bytes 327712 | tf_op jit(solution)/shard_map/all_to_all | solution.py:170
  84.7 0.7 collective-permute-start.14
  85.5 4.8 %collective-permute-start.20 = (bf16[256,640]{1,0:T(8,128)(2,1)S(1)}, bf16[256,640]{1,0:T(8,128)(2,1)S(1)}, u32[]{:S(2)}, u32[]{:S(2)}) collective-permute-start(bf16[256,640]{1,0:T(8,128)(2,1)S(1)} %bitcast.63), channel_id=1, source_target_pairs={{0,192},{1,193},{2,194},{3,195},{4,196},{5,197},{6,198},{7,199},{8... | collective-permute-start | bytes 983048 | tf_op jit(solution)/shard_map/ppermute | solution.py:22
  90.4 0.7 collective-permute-start.13
  91.0 1.3 collective-permute-start.17
  92.3 1.5 %collective-permute-start.18 = (bf16[128,512]{1,0:T(8,128)(2,1)S(1)}, bf16[128,512]{1,0:T(8,128)(2,1)S(1)}, u32[]{:S(2)}, u32[]{:S(2)}) collective-permute-start(bf16[128,512]{1,0:T(8,128)(2,1)S(1)} %get-tuple-element.54), channel_id=1, source_target_pairs={{0,32},{16,48},{32,0},{48,16},{1,33},{17,49},{33,1},{49,17},{2,34}... | collective-permute-start | bytes 393224 | tf_op jit(solution)/shard_map/ppermute | solution.py:46
  94.5 1.3 collective-permute-done.15
  96.3 0.7 collective-permute-done.20
  97.5 1.2 collective-permute-done.18
  98.8 1.6 %collective-permute-done.19 = bf16[128,512]{1,0:T(8,128)(2,1)S(1)} collective-permute-done((bf16[128,512]{1,0:T(8,128)(2,1)S(1)}, bf16[128,512]{1,0:T(8,128)(2,1)S(1)}, u32[]{:S(2)}, u32[]{:S(2)}) %collective-permute-start.19) | collective-permute-done | bytes 131104 | tf_op jit(solution)/shard_map/ppermute | solution.py:46
  100.8 1.4 collective-permute-done.21
  102.8 0.7 maximum_maximum_fusion.1
  103.5 3.6 %all-to-all-start.2 = ((bf16[4,128,128]{2,1,0:T(8,128)(2,1)}), bf16[4,128,128]{2,1,0:T(8,128)(2,1)S(1)}, u32[]{:S(2)}, u32[]{:S(2)}) async-start(bf16[4,128,128]{2,1,0:T(8,128)(2,1)} %maximum_maximum_fusion.1), calls=%async_computation.2 | async-start | bytes 262144 | tf_op jit(solution)/shard_map/all_to_all | solution.py:255
  107.3 5.8 %all-to-all-done.2 = bf16[4,128,128]{2,1,0:T(8,128)(2,1)S(1)} async-done(((bf16[4,128,128]{2,1,0:T(8,128)(2,1)}), bf16[4,128,128]{2,1,0:T(8,128)(2,1)S(1)}, u32[]{:S(2)}, u32[]{:S(2)}) %all-to-all-start.2) | async-done | bytes 131104 | tf_op jit(solution)/shard_map/all_to_all | solution.py:255
  113.4 1.2 collective-permute-done.22
  114.6 0.7 fusion
  115.4 24.3 %all_to_all.20 = bf16[32,64,128]{2,1,0:T(8,128)(2,1)S(1)} all-to-all(bf16[32,64,128]{2,1,0:T(8,128)(2,1)S(1)} %fusion.8), channel_id=1, replica_groups=mesh['y'=4,'x'=4,'z'=8,'c'=2] {'x','z'}, dimensions={0} | all-to-all | bytes 1048576 | tf_op jit(solution)/shard_map/all_to_all | solution.py:259
  139.9 0.7 reshape.63
  (105 shorter events, 5.6 us)
Async XLA Ops:
  6.5 14.5 %copy-start = (bf16[1,8192,64]{1,2,0:T(8,128)(2,1)S(1)}, bf16[1,8192,64]{1,2,0:T(8,128)(2,1)}, u32[]{:S(2)}) copy-start(bf16[1,8192,64]{1,2,0:T(8,128)(2,1)} %param.17) | copy-start | bytes 3145732
  6.5 2.8 %copy-start.6 = (bf16[1,128,512]{2,1,0:T(8,128)(2,1)S(1)}, bf16[1,128,512]{2,1,0:T(8,128)(2,1)}, u32[]{:S(2)}) copy-start(bf16[1,128,512]{2,1,0:T(8,128)(2,1)} %param.12) | copy-start | bytes 393220
  6.5 2.8 %copy-start.9 = (bf16[1,512,64]{1,2,0:T(8,128)(2,1)S(1)}, bf16[1,512,64]{1,2,0:T(8,128)(2,1)}, u32[]{:S(2)}) copy-start(bf16[1,512,64]{1,2,0:T(8,128)(2,1)} %param.16) | copy-start | bytes 196612
  6.5 11.1 %copy-start.4 = (bf16[1,128,512]{2,1,0:T(8,128)(2,1)S(1)}, bf16[1,128,512]{2,1,0:T(8,128)(2,1)}, u32[]{:S(2)}) copy-start(bf16[1,128,512]{2,1,0:T(8,128)(2,1)} %param.13) | copy-start | bytes 393220
  6.5 68.2 %all-gather.3.cloned.1.call-start = ((), (), s32[]{:S(2)}) async-start(), calls=%async_computation.4 | async-start | bytes 3342336 | tf_op jit(solution)/shard_map/all_gather | solution.py:228
  6.6 16.6 %copy-start.7 = (bf16[1,512,64]{1,2,0:T(8,128)(2,1)S(1)}, bf16[1,512,64]{1,2,0:T(8,128)(2,1)}, u32[]{:S(2)}) copy-start(bf16[1,512,64]{1,2,0:T(8,128)(2,1)} %param.15) | copy-start | bytes 196612
  9.4 26.8 %copy-start.11 = (s32[64]{0:T(128)S(1)}, s32[64]{0:T(128)}, u32[]{:S(2)}) copy-start(s32[64]{0:T(128)} %param.19) | copy-start | bytes 772
  9.4 26.8 %copy-start.12 = (s32[128]{0:T(128)S(1)}, s32[128]{0:T(128)}, u32[]{:S(2)}) copy-start(s32[128]{0:T(128)} %param.18) | copy-start | bytes 1540
  9.6 5.7 %collective-permute-start = (bf16[64,128]{1,0:T(8,128)(2,1)S(1)}, bf16[64,128]{1,0:T(8,128)(2,1)S(1)}, u32[]{:S(2)}, u32[]{:S(2)}) collective-permute-start(bf16[64,128]{1,0:T(8,128)(2,1)S(1)} %fusion.7), channel_id=1, source_target_pairs={{0,16},{16,32},{32,48},{48,0},{1,17},{17,33},{33,49},{49,1},{2,18}... | collective-permute-start | bytes 49160 | tf_op jit(solution)/shard_map/ppermute | solution.py:46
  11.1 5.2 %collective-permute-start.1 = (bf16[64,128]{1,0:T(8,128)(2,1)S(1)}, bf16[64,128]{1,0:T(8,128)(2,1)S(1)}, u32[]{:S(2)}, u32[]{:S(2)}) collective-permute-start(bf16[64,128]{1,0:T(8,128)(2,1)S(1)} %fusion.7), channel_id=1, source_target_pairs={{0,32},{16,48},{32,0},{48,16},{1,33},{17,49},{33,1},{49,17},{2,34}... | collective-permute-start | bytes 49160 | tf_op jit(solution)/shard_map/ppermute | solution.py:46
  13.9 3.7 %collective-permute-start.2 = (bf16[64,128]{1,0:T(8,128)(2,1)S(1)}, bf16[64,128]{1,0:T(8,128)(2,1)S(1)}, u32[]{:S(2)}, u32[]{:S(2)}) collective-permute-start(bf16[64,128]{1,0:T(8,128)(2,1)S(1)} %fusion.7), channel_id=1, source_target_pairs={{0,48},{16,0},{32,16},{48,32},{1,49},{17,1},{33,17},{49,33},{2,50}... | collective-permute-start | bytes 49160 | tf_op jit(solution)/shard_map/ppermute | solution.py:46
  18.4 20.7 %collective-permute-start.10 = (bf16[128,2048]{1,0:T(8,128)(2,1)}, bf16[128,2048]{1,0:T(8,128)(2,1)}, u32[]{:S(2)}, u32[]{:S(2)}) collective-permute-start(bf16[128,2048]{1,0:T(8,128)(2,1)} %get-tuple-element.37), channel_id=1, source_target_pairs={{0,48},{16,0},{32,16},{48,32},{1,49},{17,1},{33,17},{49,33},{2,50}... | collective-permute-start | bytes 1572872 | tf_op jit(solution)/shard_map/ppermute | solution.py:46
  21.1 24.4 %collective-permute-start.9 = (bf16[128,2048]{1,0:T(8,128)(2,1)}, bf16[128,2048]{1,0:T(8,128)(2,1)}, u32[]{:S(2)}, u32[]{:S(2)}) collective-permute-start(bf16[128,2048]{1,0:T(8,128)(2,1)} %get-tuple-element.36), channel_id=1, source_target_pairs={{0,16},{16,32},{32,48},{48,0},{1,17},{17,33},{33,49},{49,1},{2,18}... | collective-permute-start | bytes 1572872 | tf_op jit(solution)/shard_map/ppermute | solution.py:46
  21.2 8.1 %collective-permute-start.3 = (bf16[128,512]{1,0:T(8,128)(2,1)S(1)}, bf16[128,512]{1,0:T(8,128)(2,1)S(1)}, u32[]{:S(2)}, u32[]{:S(2)}) collective-permute-start(bf16[128,512]{1,0:T(8,128)(2,1)S(1)} %bitcast.72), channel_id=1, source_target_pairs={{192,0},{128,64},{193,1},{129,65},{194,2},{130,66},{195,3},{131,67... | collective-permute-start | bytes 393224 | tf_op jit(solution)/shard_map/ppermute | solution.py:22
  22.5 10.2 %collective-permute-start.4 = (bf16[128,512]{1,0:T(8,128)(2,1)S(1)}, bf16[128,512]{1,0:T(8,128)(2,1)S(1)}, u32[]{:S(2)}, u32[]{:S(2)}) collective-permute-start(bf16[128,512]{1,0:T(8,128)(2,1)S(1)} %bitcast.73), channel_id=1, source_target_pairs={{192,64},{193,65},{194,66},{195,67},{196,68},{197,69},{198,70},{19... | collective-permute-start | bytes 393224 | tf_op jit(solution)/shard_map/ppermute | solution.py:22
  23.6 10.8 %collective-permute-start.6 = (bf16[128,640]{1,0:T(8,128)(2,1)S(1)}, bf16[128,640]{1,0:T(8,128)(2,1)S(1)}, u32[]{:S(2)}, u32[]{:S(2)}) collective-permute-start(bf16[128,640]{1,0:T(8,128)(2,1)S(1)} %pad_maximum_fusion.3), channel_id=1, source_target_pairs={{64,0},{65,1},{66,2},{67,3},{68,4},{69,5},{70,6},{71,7},{72,8},{73... | collective-permute-start | bytes 491528 | tf_op jit(solution)/shard_map/ppermute | solution.py:22
  29.3 6.2 %collective-permute-start.7 = (bf16[128,640]{1,0:T(8,128)(2,1)S(1)}, bf16[128,640]{1,0:T(8,128)(2,1)S(1)}, u32[]{:S(2)}, u32[]{:S(2)}) collective-permute-start(bf16[128,640]{1,0:T(8,128)(2,1)S(1)} %pad_maximum_fusion.3), channel_id=1, source_target_pairs={{0,64},{64,128},{128,192},{1,65},{65,129},{129,193},{2,66},{66,130... | collective-permute-start | bytes 491528 | tf_op jit(solution)/shard_map/ppermute | solution.py:22
  32.8 33.7 %collective-permute-start.12 = (bf16[128,2048]{1,0:T(8,128)(2,1)}, bf16[128,2048]{1,0:T(8,128)(2,1)}, u32[]{:S(2)}, u32[]{:S(2)}) collective-permute-start(bf16[128,2048]{1,0:T(8,128)(2,1)} %get-tuple-element.39), channel_id=1, source_target_pairs={{0,32},{16,48},{32,0},{48,16},{1,33},{17,49},{33,1},{49,17},{2,34}... | collective-permute-start | bytes 1572872 | tf_op jit(solution)/shard_map/ppermute | solution.py:46
  35.5 1.5 %collective-permute-start.8 = (bf16[128,640]{1,0:T(8,128)(2,1)S(1)}, bf16[128,640]{1,0:T(8,128)(2,1)S(1)}, u32[]{:S(2)}, u32[]{:S(2)}) collective-permute-start(bf16[128,640]{1,0:T(8,128)(2,1)S(1)} %broadcast_select_fusion.3), channel_id=1, source_target_pairs={{0,1},{1,0},{2,3},{3,2},{4,5},{5,4},{6,7},{7,6},{8,9},{9,8},{10,11... | collective-permute-start | bytes 491528 | tf_op jit(solution)/shard_map/ppermute | solution.py:26
  35.6 1.7 %collective-permute-start.5 = (bf16[128,768]{1,0:T(8,128)(2,1)S(1)}, bf16[128,768]{1,0:T(8,128)(2,1)S(1)}, u32[]{:S(2)}, u32[]{:S(2)}) collective-permute-start(bf16[128,768]{1,0:T(8,128)(2,1)S(1)} %pad_maximum_fusion.1), channel_id=1, source_target_pairs={{0,1},{1,0},{2,3},{3,2},{4,5},{5,4},{6,7},{7,6},{8,9},{9,8},{10,11... | collective-permute-start | bytes 589832 | tf_op jit(solution)/shard_map/ppermute | solution.py:26
  37.0 20.7 %collective-permute-start.11 = (s32[128]{0:T(128)S(1)}, s32[128]{0:T(128)S(1)}, u32[]{:S(2)}, u32[]{:S(2)}) collective-permute-start(s32[128]{0:T(128)S(1)} %select_reduce_fusion), channel_id=1, source_target_pairs={{0,1},{1,0},{2,3},{3,2},{4,5},{5,4},{6,7},{7,6},{8,9},{9,8},{10,11... | collective-permute-start | bytes 1544 | tf_op jit(solution)/shard_map/ppermute | solution.py:26
  39.1 17.7 %copy-start.1 = (bf16[1,128,8192]{2,1,0:T(8,128)(2,1)S(1)}, bf16[1,128,8192]{2,1,0:T(8,128)(2,1)}, u32[]{:S(2)}) copy-start(bf16[1,128,8192]{2,1,0:T(8,128)(2,1)} %param.10) | copy-start | bytes 6291460
  45.5 20.9 %all-to-all-start = ((bf16[32,8,640]{2,1,0:T(8,128)(2,1)}), bf16[32,8,640]{2,1,0:T(8,128)(2,1)S(1)}, u32[]{:S(2)}, u32[]{:S(2)}) async-start(bf16[32,8,640]{2,1,0:T(8,128)(2,1)} %bitcast.75), calls=%async_computation | async-start | bytes 655360 | tf_op jit(solution)/shard_map/all_to_all | solution.py:167
  54.2 2.6 %copy-start.5 = (bf16[1,8192,64]{1,2,0:T(8,128)(2,1)S(1)}, bf16[1,8192,64]{1,2,0:T(8,128)(2,1)}, u32[]{:S(2)}) copy-start(bf16[1,8192,64]{1,2,0:T(8,128)(2,1)} %param.14) | copy-start | bytes 3145732
  67.2 17.5 %all-to-all-start.1 = ((bf16[32,8,640]{2,1,0:T(8,128)(2,1)}), bf16[32,8,640]{2,1,0:T(8,128)(2,1)S(1)}, u32[]{:S(2)}, u32[]{:S(2)}) async-start(bf16[32,8,640]{2,1,0:T(8,128)(2,1)} %broadcast_in_dim.46), calls=%async_computation.1 | async-start | bytes 655360 | tf_op jit(solution)/shard_map/all_to_all | solution.py:170
  74.8 1.9 %copy-start.2 = (bf16[3072,512]{1,0:T(8,128)(2,1)S(1)}, bf16[3072,512]{1,0:T(8,128)(2,1)}, u32[]{:S(2)}) copy-start(bf16[3072,512]{1,0:T(8,128)(2,1)} %all-gather.3.cloned.1.call-done) | copy-start | bytes 9437188
  76.6 1.0 copy-start.3
  84.7 9.1 %collective-permute-start.14 = (bf16[256,640]{1,0:T(8,128)(2,1)S(1)}, bf16[256,640]{1,0:T(8,128)(2,1)S(1)}, u32[]{:S(2)}, u32[]{:S(2)}) collective-permute-start(bf16[256,640]{1,0:T(8,128)(2,1)S(1)} %bitcast.61), channel_id=1, source_target_pairs={{64,128},{128,192},{65,129},{129,193},{66,130},{130,194},{67,131},... | collective-permute-start | bytes 983048 | tf_op jit(solution)/shard_map/ppermute | solution.py:22
  85.5 11.5 %collective-permute-start.20 = (bf16[256,640]{1,0:T(8,128)(2,1)S(1)}, bf16[256,640]{1,0:T(8,128)(2,1)S(1)}, u32[]{:S(2)}, u32[]{:S(2)}) collective-permute-start(bf16[256,640]{1,0:T(8,128)(2,1)S(1)} %bitcast.63), channel_id=1, source_target_pairs={{0,192},{1,193},{2,194},{3,195},{4,196},{5,197},{6,198},{7,199},{8... | collective-permute-start | bytes 983048 | tf_op jit(solution)/shard_map/ppermute | solution.py:22
  90.4 3.9 %collective-permute-start.13 = (bf16[256,384]{1,0:T(8,128)(2,1)S(1)}, bf16[256,384]{1,0:T(8,128)(2,1)S(1)}, u32[]{:S(2)}, u32[]{:S(2)}) collective-permute-start(bf16[256,384]{1,0:T(8,128)(2,1)S(1)} %slice.119), channel_id=1, source_target_pairs={{64,192},{65,193},{66,194},{67,195},{68,196},{69,197},{70,198},{71... | collective-permute-start | bytes 589832 | tf_op jit(solution)/shard_map/ppermute | solution.py:22
  91.0 6.5 %collective-permute-start.17 = (bf16[128,512]{1,0:T(8,128)(2,1)S(1)}, bf16[128,512]{1,0:T(8,128)(2,1)S(1)}, u32[]{:S(2)}, u32[]{:S(2)}) collective-permute-start(bf16[128,512]{1,0:T(8,128)(2,1)S(1)} %get-tuple-element.53), channel_id=1, source_target_pairs={{0,48},{16,0},{32,16},{48,32},{1,49},{17,1},{33,17},{49,33},{2,50}... | collective-permute-start | bytes 393224 | tf_op jit(solution)/shard_map/ppermute | solution.py:46
  92.3 6.5 %collective-permute-start.18 = (bf16[128,512]{1,0:T(8,128)(2,1)S(1)}, bf16[128,512]{1,0:T(8,128)(2,1)S(1)}, u32[]{:S(2)}, u32[]{:S(2)}) collective-permute-start(bf16[128,512]{1,0:T(8,128)(2,1)S(1)} %get-tuple-element.54), channel_id=1, source_target_pairs={{0,32},{16,48},{32,0},{48,16},{1,33},{17,49},{33,1},{49,17},{2,34}... | collective-permute-start | bytes 393224 | tf_op jit(solution)/shard_map/ppermute | solution.py:46
  93.9 6.4 %collective-permute-start.19 = (bf16[128,512]{1,0:T(8,128)(2,1)S(1)}, bf16[128,512]{1,0:T(8,128)(2,1)S(1)}, u32[]{:S(2)}, u32[]{:S(2)}) collective-permute-start(bf16[128,512]{1,0:T(8,128)(2,1)S(1)} %get-tuple-element.55), channel_id=1, source_target_pairs={{0,16},{16,32},{32,48},{48,0},{1,17},{17,33},{33,49},{49,1},{2,18}... | collective-permute-start | bytes 393224 | tf_op jit(solution)/shard_map/ppermute | solution.py:46
  94.4 1.4 collective-permute-start.15
  96.1 1.4 collective-permute-start.16
  100.5 6.6 %copy-start.8 = (bf16[1,512,64]{1,2,0:T(8,128)(2,1)S(1)}, bf16[1,512,64]{1,2,0:T(8,128)(2,1)}, u32[]{:S(2)}) copy-start(bf16[1,512,64]{1,2,0:T(8,128)(2,1)} %param.15) | copy-start | bytes 196612
  100.6 12.8 %copy-start.10 = (s32[256]{0:T(256)S(1)}, s32[256]{0:T(256)}, u32[]{:S(2)}) copy-start(s32[256]{0:T(256)} %pad_add_fusion) | copy-start | bytes 3076
  100.6 1.5 %collective-permute-start.21 = (bf16[256,384]{1,0:T(8,128)(2,1)S(1)}, bf16[256,384]{1,0:T(8,128)(2,1)S(1)}, u32[]{:S(2)}, u32[]{:S(2)}) collective-permute-start(bf16[256,384]{1,0:T(8,128)(2,1)S(1)} %pad_maximum_fusion.2), channel_id=1, source_target_pairs={{0,1},{1,0},{2,3},{3,2},{4,5},{5,4},{6,7},{7,6},{8,9},{9,8},{10,11... | collective-permute-start | bytes 589832 | tf_op jit(solution)/shard_map/ppermute | solution.py:26
  103.5 9.6 %all-to-all-start.2 = ((bf16[4,128,128]{2,1,0:T(8,128)(2,1)}), bf16[4,128,128]{2,1,0:T(8,128)(2,1)S(1)}, u32[]{:S(2)}, u32[]{:S(2)}) async-start(bf16[4,128,128]{2,1,0:T(8,128)(2,1)} %maximum_maximum_fusion.1), calls=%async_computation.2 | async-start | bytes 262144 | tf_op jit(solution)/shard_map/all_to_all | solution.py:255
  113.3 1.3 collective-permute-start.22
Sparse Core Ops, SparseCore 0:
  18.5 44.7 all-gather.2
